TPU v7x, 32 devices: a whole 2x2x4 slice. The times are simulated.
32 devices in a mesh: dp: 8 (over y, x, core), blk: 4 (over z).
Axes of the slice: x: 2, y: 2, z: 4, core: 2. Of those that a mesh axis runs over, the one named last changes fastest.
Arguments:
- tokens: bfloat16 [32768, 1024], P(('dp', 'blk')), may hold values from -6 to 6
- out_grad: bfloat16 [32768, 1024], P(('dp', 'blk')), may hold values from -6 to 6
- lengths: int32 [32], P(('dp', 'blk')), may hold values from 256 to 1024
- routes: int32 [32768, 8], P(('dp', 'blk')), may hold values from 0 to 15, all different within a row; in each aligned block of 1024 rows (0 to 1023, 1024 to 2047, ...) at most 640 rows name the same one
- attn_weight: float32 [1024, 3072], P(('dp', 'blk'))
- router_weight: float32 [1024, 16], P(('dp', 'blk')), may hold values from -0.09375 to 0.09375
- expert_weight: float32 [3, 16384, 512], P(None, ('dp', 'blk'))
- gains: float32 [2, 1024], P(None, ('dp', 'blk')), may hold values from 0.25 to 1.75
- attn_moment: float32 [1024, 3072], P(('dp', 'blk'))
- router_moment: float32 [1024, 16], P(('dp', 'blk'))
- expert_moment: float32 [3, 16384, 512], P(None, ('dp', 'blk'))
- gain_first: float32 [2, 1024], P(None, ('dp', 'blk'))
- gain_second: float32 [2, 1024], P(None, ('dp', 'blk'))
- attn_ema: float32 [1024, 3072], P(('dp', 'blk')), may hold values from -0.75 to 0.75
- router_ema: float32 [1024, 16], P(('dp', 'blk')), may hold values from -0.09375 to 0.09375
- expert_ema: float32 [3, 16384, 512], P(None, ('dp', 'blk')), may hold values from -0.1875 to 0.1875
- gain_ema: float32 [2, 1024], P(None, ('dp', 'blk')), may hold values from 0.5 to 1.5
Outputs:
- block_out: bfloat16 [32768, 1024], P(('dp', 'blk'))
- input_grad: float32 [32768, 1024], P(('dp', 'blk'))
- attn_moment_new: float32 [1024, 3072], P(('dp', 'blk'))
- router_moment_new: float32 [1024, 16], P(('dp', 'blk'))
- expert_moment_new: float32 [3, 16384, 512], P(None, ('dp', 'blk'))
- attn_new: float32 [1024, 3072], P(('dp', 'blk'))
- router_new: float32 [1024, 16], P(('dp', 'blk'))
- expert_new: float32 [3, 16384, 512], P(None, ('dp', 'blk'))
- attn_copy: bfloat16 [1024, 3072], P(('dp', 'blk'))
- router_copy: bfloat16 [1024, 16], P(('dp', 'blk'))
- expert_copy: bfloat16 [3, 16384, 512], P(None, ('dp', 'blk'))
- attn_ema_new: float32 [1024, 3072], P(('dp', 'blk'))
- router_ema_new: float32 [1024, 16], P(('dp', 'blk'))
- expert_ema_new: float32 [3, 16384, 512], P(None, ('dp', 'blk'))
- gain_first_new: float32 [2, 1024], P(None, ('dp', 'blk'))
- gain_second_new: float32 [2, 1024], P(None, ('dp', 'blk'))
- gain_new: float32 [2, 1024], P(None, ('dp', 'blk'))
- gain_copy: bfloat16 [2, 1024], P(None, ('dp', 'blk'))
- gain_ema_new: float32 [2, 1024], P(None, ('dp', 'blk'))
Inputs may be any that keep to these rules, and one draw needn't show every extreme that they name: `routes`: in the rows of one device no expert is named more than 640 times.
All inputs are finite; a program needn't handle non-finite values.
Results may differ from a plain program's by a relative error of at most 0.015.
The roundings to bfloat16 on the way count: a program that leaves them out, or rounds other values in their place, can miss the bound.
Values may be sent and summed in bfloat16 or wider, within the bound.
No kernel may reach another device: no remote copies, remote signals or barrier semaphores. Data moves between devices by JAX's collectives and lax.ppermute only.
A program may use at most 640 MiB of HBM per device.

v0:
```python
import math

import jax
import jax.numpy as jnp
from jax import lax
from jax.sharding import PartitionSpec as P

D = 1024
HEADS = 16
KV_HEADS = 8
HEAD_DIM = 64
FF = 512
TOP = 8
EXPERTS = 16
STEP = 10
CAP = 640


NORM_EPS = 1e-05
ATTN_MULT = 0.015625
RESID_MULT = 0.22
ROPE_BASE = 10000.0
NEG_FILL = -1e30
POLY_ONE = 3.4445
POLY_TWO = -4.775
POLY_THREE = 2.0315
ORTHO_EPS = 1e-07
MOMENTUM = 0.95
MUON_RATE = 0.6
MUON_SHAPE = 0.2
WEIGHT_DECAY = 0.01
ADAM_RATE = 0.8
BETA_ONE = 0.9
BETA_TWO = 0.95
ADAM_EPS = 1e-08
EMA_KEEP = 0.9
GAIN_EMA_KEEP = 0.6


def precise_dot(left_side, right_side):
    return jnp.dot(left_side, right_side, precision=lax.Precision.HIGHEST)


def plain_dot(left_side, right_side, contract_left, contract_right):
    return lax.dot_general(
        left_side,
        right_side,
        (((contract_left,), (contract_right,)), ((), ())),
        preferred_element_type=jnp.float32,
    )


def rotary_tables(length, head_width):
    position = jnp.arange(length).astype(jnp.float32)
    inverse = ROPE_BASE ** (-jnp.arange(0, head_width, 2).astype(jnp.float32) / head_width)
    angles = position[:, None] * inverse[None, :]
    return (jnp.cos(angles), jnp.sin(angles))


def rotate(values, cosine_table, sine_table):
    half_width = values.shape[-1] // 2
    first_half = values[..., :half_width]
    second_half = values[..., half_width:]
    cosine = cosine_table[:, None, :]
    sine_part = sine_table[:, None, :]
    return jnp.concatenate(
        [
            first_half * cosine - second_half * sine_part,
            second_half * cosine + first_half * sine_part,
        ],
        axis=-1,
    )


def norm_back(grad_normed, unit_rows, scale_rows, gain_row):
    grad_unit = grad_normed * gain_row
    return scale_rows * (
        grad_unit - unit_rows * jnp.mean(grad_unit * unit_rows, axis=-1, keepdims=True)
    )


def masked_scores(query_block, key_seq, block_start, length):
    block_rows = query_block.shape[0]
    scores = (
        jnp.einsum("qkgd,skd->kgqs", query_block, key_seq, preferred_element_type=jnp.float32)
        * ATTN_MULT
    )
    key_index = jnp.arange(key_seq.shape[0])
    query_index = block_start + jnp.arange(block_rows)
    allowed = (key_index[None, :] <= query_index[:, None]) & (key_index[None, :] < length)
    return jnp.where(allowed, scores, NEG_FILL)


def attend_forward(pieces):
    query_seq, key_seq, value_seq, length = pieces
    seq_len = query_seq.shape[0]
    block_rows = min(512, seq_len)
    outputs = []
    totals = []
    for block_start in range(0, seq_len, block_rows):
        scores = masked_scores(
            query_seq[block_start : block_start + block_rows], key_seq, block_start, length
        )
        largest = jnp.max(scores, axis=-1, keepdims=True)
        exponent = jnp.exp(scores - largest)
        exp_total = jnp.sum(exponent, axis=-1, keepdims=True)
        probability = (exponent / exp_total).astype(jnp.bfloat16)
        outputs.append(
            jnp.einsum("kgqs,skd->qkgd", probability, value_seq, preferred_element_type=jnp.float32)
        )
        totals.append(largest + jnp.log(exp_total))
    return (jnp.concatenate(outputs, axis=0), jnp.concatenate(totals, axis=2))


def attend_backward(pieces):
    query_seq, key_seq, value_seq, length, grad_seq, log_totals = pieces
    seq_len = query_seq.shape[0]
    block_rows = min(512, seq_len)
    query_grads = []
    key_grad = jnp.zeros(key_seq.shape, jnp.float32)
    value_grad = jnp.zeros(value_seq.shape, jnp.float32)
    for block_start in range(0, seq_len, block_rows):
        query_block = query_seq[block_start : block_start + block_rows]
        grad_block = grad_seq[block_start : block_start + block_rows]
        scores = masked_scores(query_block, key_seq, block_start, length)
        probability = jnp.exp(scores - log_totals[:, :, block_start : block_start + block_rows])
        prob_grad = jnp.einsum(
            "qkgd,skd->kgqs", grad_block, value_seq, preferred_element_type=jnp.float32
        )
        inner_sum = jnp.sum(probability * prob_grad, axis=-1, keepdims=True)
        score_grad = (probability * (prob_grad - inner_sum)).astype(jnp.bfloat16)
        query_grads.append(
            jnp.einsum("kgqs,skd->qkgd", score_grad, key_seq, preferred_element_type=jnp.float32)
            * ATTN_MULT
        )
        key_grad = (
            key_grad
            + jnp.einsum(
                "kgqs,qkgd->skd", score_grad, query_block, preferred_element_type=jnp.float32
            )
            * ATTN_MULT
        )
        value_grad = value_grad + jnp.einsum(
            "kgqs,qkgd->skd",
            probability.astype(jnp.bfloat16),
            grad_block,
            preferred_element_type=jnp.float32,
        )
    return (jnp.concatenate(query_grads, axis=0), key_grad, value_grad)


def summed_grams(attn_block, gram_mask, router_rows, expert_row_list, picker):
    attn_gram = (
        lax.dot_general(
            attn_block, attn_block, (((0,), (0,)), ((), ())), precision=lax.Precision.HIGHEST
        )
        * gram_mask
    )
    router_gram = lax.dot_general(
        router_rows, router_rows, (((0,), (0,)), ((), ())), precision=lax.Precision.HIGHEST
    )
    expert_gram = jnp.einsum(
        "poe,pol->pel", expert_row_list, expert_row_list, precision=lax.Precision.HIGHEST
    )
    placed = picker[:, None, None, None] * expert_gram[None]
    attn_total, router_total, expert_total = lax.psum((attn_gram, router_gram, placed), "blk")
    return (attn_total, router_total, jnp.sum(picker[:, None, None, None] * expert_total, axis=0))


def column_scale(lower_squares, upper_squares, slot_index, upper_half):
    whole = 1.0 / (jnp.sqrt(lower_squares + upper_squares) + ORTHO_EPS)
    lower_part = 1.0 / (jnp.sqrt(lower_squares) + ORTHO_EPS)
    upper_part = 1.0 / (jnp.sqrt(upper_squares) + ORTHO_EPS)
    paired = jnp.where(upper_half, upper_part, lower_part)
    return jnp.where(slot_index == 1, paired, whole)


def polish(newton_iterate, gram_square):
    gram_product = precise_dot(newton_iterate, gram_square)
    return (
        POLY_ONE * newton_iterate
        + POLY_TWO * gram_product
        + POLY_THREE * precise_dot(gram_product, gram_square)
    )


def polish_batch(newton_iterate, gram_square):
    gram_product = jnp.einsum(
        "toa,tad->tod", newton_iterate, gram_square, precision=lax.Precision.HIGHEST
    )
    return (
        POLY_ONE * newton_iterate
        + POLY_TWO * gram_product
        + POLY_THREE
        * jnp.einsum("toa,tad->tod", gram_product, gram_square, precision=lax.Precision.HIGHEST)
    )


def muon_update(weight, ortho):
    return weight * (1.0 - MUON_RATE * WEIGHT_DECAY) - MUON_RATE * MUON_SHAPE * math.sqrt(D) * ortho


def shards(
    tokens,
    out_grad,
    lengths,
    routes,
    attn_weight,
    router_weight,
    expert_weight,
    gains,
    attn_moment,
    router_moment,
    expert_moment,
    gain_first,
    gain_second,
    attn_ema,
    router_ema,
    expert_ema,
    gain_ema,
):
    seqs_here = lengths.shape[0]
    tok_here = tokens.shape[0]
    seq_len = tok_here // seqs_here
    group_size = HEADS // KV_HEADS
    query_width = HEADS * HEAD_DIM
    kv_width = KV_HEADS * HEAD_DIM
    qkv_width = query_width + 2 * kv_width
    attn_low = attn_weight.astype(jnp.bfloat16)
    router_low = router_weight.astype(jnp.bfloat16)
    gain_low = gains.astype(jnp.bfloat16)
    expert_low = expert_weight.astype(jnp.bfloat16)
    full_attn, full_router, full_gains = (
        lax.all_gather(attn_low, ("dp", "blk"), axis=0, tiled=True),
        lax.all_gather(router_low, ("dp", "blk"), axis=0, tiled=True),
        lax.all_gather(gain_low, ("dp", "blk"), axis=1, tiled=True),
    )
    gain_one = full_gains[0].astype(jnp.float32)
    gain_two = full_gains[1].astype(jnp.float32)
    inputs = tokens.astype(jnp.float32)
    scale_one = lax.rsqrt(jnp.mean(inputs * inputs, axis=-1, keepdims=True) + NORM_EPS)
    unit_one = inputs * scale_one
    normed_one = (unit_one * gain_one).astype(jnp.bfloat16)
    projected = jnp.dot(normed_one, full_attn[:, :qkv_width], preferred_element_type=jnp.float32)
    cosine_table, sine_table = rotary_tables(seq_len, HEAD_DIM)
    query_row_block = rotate(
        projected[:, :query_width].reshape(seqs_here, seq_len, HEADS, HEAD_DIM),
        cosine_table,
        sine_table,
    )
    query_row_block = query_row_block.astype(jnp.bfloat16).reshape(
        seqs_here, seq_len, KV_HEADS, group_size, HEAD_DIM
    )
    key_rows = rotate(
        projected[:, query_width : query_width + kv_width].reshape(
            seqs_here, seq_len, KV_HEADS, HEAD_DIM
        ),
        cosine_table,
        sine_table,
    ).astype(jnp.bfloat16)
    value_rows = (
        projected[:, query_width + kv_width :]
        .astype(jnp.bfloat16)
        .reshape(seqs_here, seq_len, KV_HEADS, HEAD_DIM)
    )
    attended, log_totals = lax.map(attend_forward, (query_row_block, key_rows, value_rows, lengths))
    attended_low = attended.reshape(tok_here, query_width).astype(jnp.bfloat16)
    branch = plain_dot(attended_low, full_attn[:, qkv_width:], 1, 1)
    hidden_state = inputs + RESID_MULT * branch
    scale_two = lax.rsqrt(jnp.mean(hidden_state * hidden_state, axis=-1, keepdims=True) + NORM_EPS)
    unit_two = hidden_state * scale_two
    normed_two = (unit_two * gain_two).astype(jnp.bfloat16)
    full_expert = lax.all_gather(expert_low, ("dp", "blk"), axis=1, tiled=True).reshape(
        3, EXPERTS, D, FF
    )
    logits = jnp.dot(normed_two, full_router, preferred_element_type=jnp.float32)
    chosen = jnp.take_along_axis(logits, routes, axis=1)
    chosen_top = jnp.max(chosen, axis=1, keepdims=True)
    exponent = jnp.exp(chosen - chosen_top)
    gate_weights = exponent / jnp.sum(exponent, axis=1, keepdims=True)
    flat_routes = routes.reshape(-1)
    matches = (flat_routes[:, None] == jnp.arange(EXPERTS)[None, :]).astype(jnp.int32)
    rank_within = jnp.sum((jnp.cumsum(matches, axis=0) - 1) * matches, axis=1)
    slot_ids = flat_routes * CAP + rank_within
    owner_token = (
        jnp.zeros((EXPERTS * CAP,), jnp.int32)
        .at[slot_ids]
        .set(jnp.arange(tok_here * TOP, dtype=jnp.int32) // TOP)
    )
    filled = jnp.zeros((EXPERTS * CAP,), jnp.bfloat16).at[slot_ids].set(1.0)
    expert_in = (normed_two[owner_token] * filled[:, None]).reshape(EXPERTS, CAP, D)
    gate_part = jnp.einsum(
        "ecd,edf->ecf", expert_in, full_expert[0], preferred_element_type=jnp.float32
    )
    up_part = jnp.einsum(
        "ecd,edf->ecf", expert_in, full_expert[1], preferred_element_type=jnp.float32
    )
    sigmoid_gate = jax.nn.sigmoid(gate_part)
    silu_gate = gate_part * sigmoid_gate
    hidden = (silu_gate * up_part).astype(jnp.bfloat16)
    expert_out = jnp.einsum(
        "ecf,edf->ecd", hidden, full_expert[2], preferred_element_type=jnp.float32
    )
    picked = expert_out.reshape(EXPERTS * CAP, D)[slot_ids].reshape(tok_here, TOP, D)
    mixture_out = jnp.sum(gate_weights[:, :, None] * picked, axis=1)
    block_out = (hidden_state + RESID_MULT * mixture_out).astype(jnp.bfloat16)
    full_expert = lax.all_gather(expert_low, ("dp", "blk"), axis=1, tiled=True).reshape(
        3, EXPERTS, D, FF
    )
    full_attn, full_router, full_gains = (
        lax.all_gather(attn_low, ("dp", "blk"), axis=0, tiled=True),
        lax.all_gather(router_low, ("dp", "blk"), axis=0, tiled=True),
        lax.all_gather(gain_low, ("dp", "blk"), axis=1, tiled=True),
    )
    position = jnp.arange(seq_len)
    live_rows = (position[None, :] < lengths[:, None]).reshape(tok_here, 1)
    grad_out = jnp.where(live_rows, out_grad.astype(jnp.float32), 0.0)
    grad_mixture = RESID_MULT * grad_out
    grad_gates = jnp.sum(picked * grad_mixture[:, None, :], axis=2)
    grad_picked = (
        (gate_weights[:, :, None] * grad_mixture[:, None, :])
        .astype(jnp.bfloat16)
        .reshape(tok_here * TOP, D)
    )
    grad_slots = (
        jnp.zeros((EXPERTS * CAP, D), jnp.bfloat16)
        .at[slot_ids]
        .set(grad_picked)
        .reshape(EXPERTS, CAP, D)
    )
    grad_hidden = jnp.einsum(
        "ecd,edf->ecf", grad_slots, full_expert[2], preferred_element_type=jnp.float32
    )
    grad_gate_part = (
        grad_hidden * up_part * sigmoid_gate * (1.0 + gate_part * (1.0 - sigmoid_gate))
    ).astype(jnp.bfloat16)
    grad_up_part = (grad_hidden * silu_gate).astype(jnp.bfloat16)
    grad_gate_w = jnp.einsum(
        "ecd,ecf->edf", expert_in, grad_gate_part, preferred_element_type=jnp.float32
    )
    grad_up_w = jnp.einsum(
        "ecd,ecf->edf", expert_in, grad_up_part, preferred_element_type=jnp.float32
    )
    grad_down_w = jnp.einsum("ecd,ecf->edf", grad_slots, hidden, preferred_element_type=jnp.float32)
    grad_expert_full = jnp.stack([grad_gate_w, grad_up_w, grad_down_w]).reshape(3, EXPERTS * D, FF)
    expert_grad = lax.psum_scatter(grad_expert_full, ("dp", "blk"), scatter_dimension=1, tiled=True)
    grad_expert_in = jnp.einsum(
        "ecf,edf->ecd", grad_gate_part, full_expert[0], preferred_element_type=jnp.float32
    )
    grad_expert_in = grad_expert_in + jnp.einsum(
        "ecf,edf->ecd", grad_up_part, full_expert[1], preferred_element_type=jnp.float32
    )
    grad_normed_two = jnp.sum(
        grad_expert_in.reshape(EXPERTS * CAP, D)[slot_ids].reshape(tok_here, TOP, D), axis=1
    )
    inner_sum = jnp.sum(gate_weights * grad_gates, axis=1, keepdims=True)
    grad_chosen = gate_weights * (grad_gates - inner_sum)
    grad_logits = jnp.sum(
        (grad_chosen.reshape(-1, 1) * matches.astype(jnp.float32)).reshape(tok_here, TOP, EXPERTS),
        axis=1,
    ).astype(jnp.bfloat16)
    grad_normed_two = grad_normed_two + plain_dot(grad_logits, full_router, 1, 1)
    grad_router = plain_dot(normed_two, grad_logits, 0, 0)
    grad_hidden_state = grad_out + norm_back(grad_normed_two, unit_two, scale_two, gain_two)
    grad_gain_two = jnp.sum(grad_normed_two * unit_two, axis=0)
    grad_branch = (RESID_MULT * grad_hidden_state).astype(jnp.bfloat16)
    w_out = full_attn[:, qkv_width:]
    grad_w_out = plain_dot(grad_branch, attended_low, 0, 0)
    grad_attended = jnp.dot(grad_branch, w_out, preferred_element_type=jnp.float32).astype(
        jnp.bfloat16
    )
    grad_attended = grad_attended.reshape(seqs_here, seq_len, KV_HEADS, group_size, HEAD_DIM)
    query_grad, key_grad, value_grad = lax.map(
        attend_backward, (query_row_block, key_rows, value_rows, lengths, grad_attended, log_totals)
    )
    grad_query_lin = rotate(
        query_grad.reshape(seqs_here, seq_len, HEADS, HEAD_DIM), cosine_table, -sine_table
    ).astype(jnp.bfloat16)
    grad_key_lin = rotate(key_grad, cosine_table, -sine_table).astype(jnp.bfloat16)
    grad_projected = jnp.concatenate(
        [
            grad_query_lin.reshape(tok_here, query_width),
            grad_key_lin.reshape(tok_here, kv_width),
            value_grad.astype(jnp.bfloat16).reshape(tok_here, kv_width),
        ],
        axis=1,
    )
    grad_w_qkv = plain_dot(normed_one, grad_projected, 0, 0)
    grad_normed_one = plain_dot(grad_projected, full_attn[:, :qkv_width], 1, 1)
    input_grad = grad_hidden_state + norm_back(grad_normed_one, unit_one, scale_one, gain_one)
    grad_gain_one = jnp.sum(grad_normed_one * unit_one, axis=0)
    grad_attn_full = jnp.concatenate([grad_w_qkv, grad_w_out], axis=1)
    attn_grad, router_gradient, gain_grad = (
        lax.psum_scatter(grad_attn_full, ("dp", "blk"), scatter_dimension=0, tiled=True),
        lax.psum_scatter(grad_router, ("dp", "blk"), scatter_dimension=0, tiled=True),
        lax.psum_scatter(
            jnp.stack([grad_gain_one, grad_gain_two]),
            ("dp", "blk"),
            scatter_dimension=1,
            tiled=True,
        ),
    )
    moment_attn = MOMENTUM * attn_moment + attn_grad
    moment_router = MOMENTUM * router_moment + router_gradient
    moment_expert = MOMENTUM * expert_moment + expert_grad
    rows_attn, rows_router = (
        lax.all_gather(moment_attn, "dp", axis=0, tiled=True),
        lax.all_gather(moment_router, "dp", axis=0, tiled=True),
    )
    dp_index = lax.axis_index("dp")
    slot_index = dp_index % 3
    block_width = rows_attn.shape[1] // 3
    half_width = block_width // 2
    attn_block = lax.dynamic_slice_in_dim(rows_attn, slot_index * block_width, block_width, 1)
    column = jnp.arange(block_width)
    upper_half = column >= half_width
    same_half = upper_half[:, None] == upper_half[None, :]
    gram_mask = jnp.where(same_half | (slot_index != 1), 1.0, 0.0).astype(jnp.float32)
    group_count = EXPERTS // lax.axis_size("dp")
    own_rows = expert_moment.shape[1]
    local_expert = lax.axis_index("blk") * own_rows // D
    picker = (jnp.arange(group_count) == local_expert).astype(jnp.float32)
    attn_gram, router_gram, expert_gram = summed_grams(
        attn_block, gram_mask, rows_router, moment_expert, picker
    )
    diagonal = jnp.diagonal(attn_gram)
    attn_scale = column_scale(
        jnp.sum(jnp.where(upper_half, 0.0, diagonal)),
        jnp.sum(jnp.where(upper_half, diagonal, 0.0)),
        slot_index,
        upper_half,
    )
    router_scale = 1.0 / (jnp.sqrt(jnp.trace(router_gram)) + ORTHO_EPS)
    expert_scale = 1.0 / (jnp.sqrt(jnp.trace(expert_gram, axis1=1, axis2=2)) + ORTHO_EPS)
    attn_iter = attn_block * attn_scale[None, :]
    router_iter = rows_router * router_scale
    expert_iter = moment_expert * expert_scale[:, None, None]
    attn_gram = attn_gram * attn_scale[:, None] * attn_scale[None, :]
    router_gram = router_gram * (router_scale * router_scale)
    expert_gram = expert_gram * (expert_scale * expert_scale)[:, None, None]
    for iteration in range(5):
        if iteration > 0:
            attn_gram, router_gram, expert_gram = summed_grams(
                attn_iter, gram_mask, router_iter, expert_iter, picker
            )
        attn_iter = polish(attn_iter, attn_gram)
        router_iter = polish(router_iter, router_gram)
        expert_iter = polish_batch(expert_iter, expert_gram)
    returned = lax.all_to_all(attn_iter, "dp", split_axis=0, concat_axis=0, tiled=True)
    rows_each = attn_moment.shape[0]
    ortho_attn = jnp.concatenate(
        [
            returned[:rows_each],
            returned[rows_each : 2 * rows_each],
            returned[2 * rows_each : 3 * rows_each],
        ],
        axis=1,
    )
    ortho_router = lax.dynamic_slice_in_dim(router_iter, dp_index * rows_each, rows_each, 0)
    attn_new = muon_update(attn_weight, ortho_attn)
    router_new = muon_update(router_weight, ortho_router)
    expert_new = muon_update(expert_weight, expert_iter)
    first_new = BETA_ONE * gain_first + (1.0 - BETA_ONE) * gain_grad
    second_new = BETA_TWO * gain_second + (1.0 - BETA_TWO) * gain_grad * gain_grad
    corrected_first = first_new / (1.0 - BETA_ONE**STEP)
    corrected_second = second_new / (1.0 - BETA_TWO**STEP)
    gain_new = gains - ADAM_RATE * corrected_first / (jnp.sqrt(corrected_second) + ADAM_EPS)
    return (
        block_out,
        input_grad,
        moment_attn,
        moment_router,
        moment_expert,
        attn_new,
        router_new,
        expert_new,
        attn_new.astype(jnp.bfloat16),
        router_new.astype(jnp.bfloat16),
        expert_new.astype(jnp.bfloat16),
        EMA_KEEP * attn_ema + (1.0 - EMA_KEEP) * attn_new,
        EMA_KEEP * router_ema + (1.0 - EMA_KEEP) * router_new,
        EMA_KEEP * expert_ema + (1.0 - EMA_KEEP) * expert_new,
        first_new,
        second_new,
        gain_new,
        gain_new.astype(jnp.bfloat16),
        GAIN_EMA_KEEP * gain_ema + (1.0 - GAIN_EMA_KEEP) * gain_new,
    )


def solution(mesh):
    placed = (
        P(("dp", "blk"), None),
        P(("dp", "blk"), None),
        P(("dp", "blk")),
        P(("dp", "blk"), None),
        P(("dp", "blk"), None),
        P(("dp", "blk"), None),
        P(None, ("dp", "blk"), None),
        P(None, ("dp", "blk")),
        P(("dp", "blk"), None),
        P(("dp", "blk"), None),
        P(None, ("dp", "blk"), None),
        P(None, ("dp", "blk")),
        P(None, ("dp", "blk")),
        P(("dp", "blk"), None),
        P(("dp", "blk"), None),
        P(None, ("dp", "blk"), None),
        P(None, ("dp", "blk")),
    )
    return jax.shard_map(
        shards,
        mesh=mesh,
        in_specs=placed,
        out_specs=(
            P(("dp", "blk"), None),
            P(("dp", "blk"), None),
            P(("dp", "blk"), None),
            P(("dp", "blk"), None),
            P(None, ("dp", "blk"), None),
            P(("dp", "blk"), None),
            P(("dp", "blk"), None),
            P(None, ("dp", "blk"), None),
            P(("dp", "blk"), None),
            P(("dp", "blk"), None),
            P(None, ("dp", "blk"), None),
            P(("dp", "blk"), None),
            P(("dp", "blk"), None),
            P(None, ("dp", "blk"), None),
            P(None, ("dp", "blk")),
            P(None, ("dp", "blk")),
            P(None, ("dp", "blk")),
            P(None, ("dp", "blk")),
            P(None, ("dp", "blk")),
        ),
        check_vma=False,
    )
```

profile of v0, /device:TPU:0, one launch (start us, length us, event | category | flops | bytes accessed | tf_op | source)
XLA Modules:
  0.0 5797.3 jit_solution(15248633507961222049)
XLA Ops:
  18.7 69.7 %all-gather = bf16[32,32,2]{1,2,0:T(2,128)(2,1)S(1)} all-gather(bf16[1,32,2]{1,2,0:T(2,128)(2,1)S(1)} %convert_bitcast_fusion.1), channel_id=1, replica_groups=mesh['dp'=8,'blk'=4] {'dp','blk'}, dimensions={0}, use_global_device_ids=true | all-gather | bytes 4224 | tf_op jit(solution)/shard_map/all_gather | solution.py:236
  95.8 30.5 scatter_custom_fusion
  126.3 56.5 scatter_custom_fusion.1
  193.1 70.9 %all-gather.1 = bf16[32,32,16]{1,2,0:T(8,128)(2,1)S(1)} all-gather(bf16[1,32,16]{1,2,0:T(8,128)(2,1)S(1)} %convert_bitcast_fusion), channel_id=1, replica_groups=mesh['dp'=8,'blk'=4] {'dp','blk'}, dimensions={0}, use_global_device_ids=true | all-gather | bytes 33792 | tf_op jit(solution)/shard_map/all_gather | solution.py:235
  393.0 43.9 gather_fusion
  436.9 29.2 copy.293
  466.9 65.7 %gather_fusion.4 = f32[8192]{0:T(1024)S(1)} fusion(f32[1024,16]{0,1:T(8,128)S(1)} %fusion.177, s32[8192]{0:T(1024)S(1)} %copy-done), kind=kCustom, calls=%fused_computation.4 | custom fusion | bytes 131072 | tf_op jit(solution)/shard_map/jit(take_along_axis)/gather | solution.py:277
  533.7 50.9 scatter_custom_fusion.2
  585.9 32.7 fusion.146
  671.6 41.0 multiply_convert_fusion
  738.1 40.5 convolution_add_fusion
  778.6 56.5 gather_fusion.2
  882.6 56.5 gather_fusion.1
  1208.5 29.2 fusion.28
  1237.7 97.7 %reduce-scatter.9.cloned.1.call-done = f32[32,3072]{1,0:T(8,128)} async-done(((f32[1024,3072]{1,0:T(8,128)}), f32[32,3072]{1,0:T(8,128)}) %reduce-scatter.9.cloned.1.call-update) | async-done | bytes 393232 | tf_op jit(solution)/shard_map/reduce_scatter | solution.py:394
  1363.2 64.9 %pad_maximum_fusion = f32[3,16384,512]{2,1,0:T(8,128)} fusion(f32[1,16384,512]{2,1,0:T(8,128)} %bitcast.286, f32[1,16384,512]{2,1,0:T(8,128)} %bitcast.297, f32[1,16384,512]{2,1,0:T(8,128)} %bitcast.298), kind=kLoop, calls=%fused_computation.8 | loop fusion | flops 50331648 | bytes 201326592 | tf_op jit(solution)/shard_map/stack | solution.py:345
  1436.3 2101.2 %reduce-scatter.11.cloned.1.call-done = f32[3,512,512]{2,1,0:T(8,128)} async-done(((f32[3,16384,512]{2,1,0:T(8,128)}), f32[3,512,512]{2,1,0:T(8,128)}) %reduce-scatter.11.cloned.1.call-update) | async-done | bytes 3145744 | tf_op jit(solution)/shard_map/reduce_scatter | solution.py:346
  3550.7 359.5 %all-reduce.19.cloned.1.call-done = (f32[1024,1024]{0,1:T(8,128)}, f32[2,3,512,512]{3,2,1,0:T(8,128)}) async-done(((f32[1024,1024]{0,1:T(8,128)}, f32[2,3,512,512]{3,2,1,0:T(8,128)}), (f32[1024,1024]{0,1:T(8,128)}, f32[2,3,512,512]{3,2,1,0:T(8,128)})) %all-reduce.19.cloned.1.call-update) | async-done | bytes 10485776 | tf_op jit(solution)/shard_map/psum | solution.py:166
  3973.5 358.2 %all-reduce.17.cloned.1.call-done = (f32[1024,1024]{0,1:T(8,128)}, f32[2,3,512,512]{3,2,1,0:T(8,128)}) async-done(((f32[1024,1024]{0,1:T(8,128)}, f32[2,3,512,512]{3,2,1,0:T(8,128)}), (f32[1024,1024]{0,1:T(8,128)}, f32[2,3,512,512]{3,2,1,0:T(8,128)})) %all-reduce.17.cloned.1.call-update) | async-done | bytes 10485776 | tf_op jit(solution)/shard_map/psum | solution.py:166
  4370.3 358.2 %all-reduce.15.cloned.1.call-done = (f32[1024,1024]{0,1:T(8,128)}, f32[2,3,512,512]{3,2,1,0:T(8,128)}) async-done(((f32[1024,1024]{0,1:T(8,128)}, f32[2,3,512,512]{3,2,1,0:T(8,128)}), (f32[1024,1024]{0,1:T(8,128)}, f32[2,3,512,512]{3,2,1,0:T(8,128)})) %all-reduce.15.cloned.1.call-update) | async-done | bytes 10485776 | tf_op jit(solution)/shard_map/psum | solution.py:166
  4784.1 342.4 %all-reduce.13.cloned.1.call-done = (f32[1024,1024]{0,1:T(8,128)}, f32[2,3,512,512]{3,2,1,0:T(8,128)}) async-done(((f32[1024,1024]{0,1:T(8,128)}, f32[2,3,512,512]{3,2,1,0:T(8,128)}), (f32[1024,1024]{0,1:T(8,128)}, f32[2,3,512,512]{3,2,1,0:T(8,128)})) %all-reduce.13.cloned.1.call-update) | async-done | bytes 10485776 | tf_op jit(solution)/shard_map/psum | solution.py:166
  5182.9 78.8 %reduce-scatter.15.cloned.1.call-done = f32[32,2]{1,0:T(8,128)} async-done(((f32[1024,2]{1,0:T(8,128)}), f32[32,2]{1,0:T(8,128)}) %reduce-scatter.15.cloned.1.call-update) | async-done | bytes 272
  5263.6 130.8 %reduce-scatter.13.cloned.1.call-done = f32[32,16]{1,0:T(8,128)} async-done(((f32[1024,16]{1,0:T(8,128)}), f32[32,16]{1,0:T(8,128)}) %reduce-scatter.13.cloned.1.call-update) | async-done | bytes 2064
  5466.8 288.2 %all-reduce.11.cloned.1.call-done = (f32[1024,1024]{0,1:T(8,128)}, f32[2,3,512,512]{3,2,1,0:T(8,128)}) async-done(((f32[1024,1024]{0,1:T(8,128)}, f32[2,3,512,512]{3,2,1,0:T(8,128)}), (f32[1024,1024]{0,1:T(8,128)}, f32[2,3,512,512]{3,2,1,0:T(8,128)})) %all-reduce.11.cloned.1.call-update) | async-done | bytes 10485776 | tf_op jit(solution)/shard_map/psum | solution.py:166
  (467 shorter events, 922.7 us)
Async XLA Ops:
  7.2 263.8 %all-gather.7.cloned.1.call-start = ((), (), s32[]{:S(2)}) async-start(), calls=%async_computation.5 | async-start | bytes 6488064 | tf_op jit(solution)/shard_map/all_gather | solution.py:234
  9.0 576.9 %all-gather.9.cloned.1.call-start = ((), (), s32[]{:S(2)}) async-start(), calls=%async_computation.6 | async-start | bytes 51904512 | tf_op jit(solution)/shard_map/all_gather | solution.py:273
  12.4 1323.0 %reduce-scatter.9.cloned.1.call-start = ((), (), s32[]{:S(2)}) async-start(), calls=%async_computation.7 | async-start | bytes 12976128 | tf_op jit(solution)/shard_map/reduce_scatter | solution.py:394
  18.6 252.4 %copy-start.18 = (bf16[1024,1024]{0,1:T(8,128)(2,1)}, bf16[1024,1024]{0,1:T(8,128)(2,1)S(1)}, u32[]{:S(2)}) copy-start(bf16[1024,1024]{0,1:T(8,128)(2,1)S(1)} %copy.278) | copy-start | bytes 6291460
  1179.4 249.1 %all-gather.11.cloned.1.call-start = ((), (), s32[]{:S(2)}) async-start(), calls=%async_computation.9 | async-start | bytes 3538944 | tf_op jit(solution)/shard_map/all_gather | solution.py:407
  1337.2 2200.4 %reduce-scatter.11.cloned.1.call-start = ((), (), s32[]{:S(2)}) async-start(), calls=%async_computation.8 | async-start | bytes 103809024 | tf_op jit(solution)/shard_map/reduce_scatter | solution.py:346
  1428.1 2482.1 %all-reduce.19.cloned.1.call-start = ((), (), s32[]{:S(2)}) async-start(), calls=%async_computation.16 | async-start | bytes 20971520 | tf_op jit(solution)/shard_map/psum | solution.py:166
  3541.2 415.0 %copy-start.1 = (f32[3,512,512]{2,1,0:T(8,128)}, f32[3,512,512]{2,1,0:T(8,128)S(1)}, u32[]{:S(2)}) copy-start(f32[3,512,512]{2,1,0:T(8,128)S(1)} %multiply_add_fusion.6) | copy-start | bytes 9437188
  3550.2 781.6 %all-reduce.17.cloned.1.call-start = ((), (), s32[]{:S(2)}) async-start(), calls=%async_computation.15 | async-start | bytes 20971520 | tf_op jit(solution)/shard_map/psum | solution.py:166
  3973.4 358.3 %copy-start.17 = (f32[256,1024]{1,0:T(8,128)S(1)}, f32[256,1024]{1,0:T(8,128)}, u32[]{:S(2)}) copy-start(f32[256,1024]{1,0:T(8,128)} %copy-done.16) | copy-start | bytes 3145732
  3973.5 755.1 %all-reduce.15.cloned.1.call-start = ((), (), s32[]{:S(2)}) async-start(), calls=%async_computation.14 | async-start | bytes 20971520 | tf_op jit(solution)/shard_map/psum | solution.py:166
  4360.9 384.8 %copy-start.4 = (f32[3,512,512]{2,1,0:T(8,128)}, f32[3,512,512]{2,1,0:T(8,128)S(1)}, u32[]{:S(2)}) copy-start(f32[3,512,512]{2,1,0:T(8,128)S(1)} %multiply_add_fusion.4) | copy-start | bytes 9437188
  4370.3 756.1 %all-reduce.13.cloned.1.call-start = ((), (), s32[]{:S(2)}) async-start(), calls=%async_computation.13 | async-start | bytes 20971520 | tf_op jit(solution)/shard_map/psum | solution.py:166
  4768.2 493.5 %reduce-scatter.15.cloned.1.call-start = ((), (), s32[]{:S(2)}) async-start(), calls=%async_computation.11 | async-start | bytes 540672
  4780.9 613.5 %reduce-scatter.13.cloned.1.call-start = ((), (), s32[]{:S(2)}) async-start(), calls=%async_computation.10 | async-start | bytes 540672
  4784.0 971.0 %all-reduce.11.cloned.1.call-start = ((), (), s32[]{:S(2)}) async-start(), calls=%async_computation.12 | async-start | bytes 20971520 | tf_op jit(solution)/shard_map/psum | solution.py:166
  5177.4 217.8 %copy-start.102 = (f32[32,16]{0,1:T(8,128)S(1)}, f32[32,16]{0,1:T(8,128)}, u32[]{:S(2)}) copy-start(f32[32,16]{0,1:T(8,128)} %param.26) | copy-start | bytes 6148
  5177.4 288.1 %copy-start.89 = (f32[32,16]{0,1:T(8,128)S(1)}, f32[32,16]{0,1:T(8,128)}, u32[]{:S(2)}) copy-start(f32[32,16]{0,1:T(8,128)} %param.22) | copy-start | bytes 6148
  5177.4 288.1 %copy-start.103 = (f32[32,16]{0,1:T(8,128)S(1)}, f32[32,16]{0,1:T(8,128)}, u32[]{:S(2)}) copy-start(f32[32,16]{0,1:T(8,128)} %param.31) | copy-start | bytes 6148
  5177.4 577.7 %copy-start.11 = (f32[256,1024]{1,0:T(8,128)S(1)}, f32[256,1024]{1,0:T(8,128)}, u32[]{:S(2)}) copy-start(f32[256,1024]{1,0:T(8,128)} %copy-done.10) | copy-start | bytes 3145732
  5263.1 502.7 %copy-start.109 = (f32[2,32]{1,0:T(2,128)}, f32[2,32]{1,0:T(2,128)S(1)}, u32[]{:S(2)}) copy-start(f32[2,32]{1,0:T(2,128)S(1)} %get-tuple-element.203) | copy-start | bytes 772
  5395.1 370.7 %copy-start.87 = (f32[32,16]{0,1:T(8,128)}, f32[32,16]{0,1:T(8,128)S(1)}, u32[]{:S(2)}) copy-start(f32[32,16]{0,1:T(8,128)S(1)} %multiply_add_fusion.10) | copy-start | bytes 6148
  5466.2 299.6 %copy-start.90 = (f32[32,16]{0,1:T(8,128)}, f32[32,16]{0,1:T(8,128)S(1)}, u32[]{:S(2)}) copy-start(f32[32,16]{0,1:T(8,128)S(1)} %get-tuple-element.207) | copy-start | bytes 6148
  5765.8 22.5 all-to-all-start
  (105 other events, 2244.7 us)
Sparse Core Ops, SparseCore 0:
  11.5 72.2 all-gather.6
  87.5 274.9 all-gather.8
  1179.5 155.8 reduce-scatter.8
  1337.9 31.4 all-gather.10
  1428.3 2109.2 reduce-scatter.10
  3550.3 359.8 all-reduce.18
  3973.6 358.1 all-reduce.16
  4370.4 358.1 all-reduce.14
  4768.3 358.1 all-reduce.12
  5128.6 133.0 reduce-scatter.14
  5263.9 130.3 reduce-scatter.12
  5397.0 358.0 all-reduce.10
where the time goes:
time: 5810 us; the launch traced here: 5800 us
  waiting for transfers between devices  4120 us (71%)
  matrix products  669 us (12%)
  local copies, waits for them, and re-layouts  458 us (8%)
  other arithmetic  322 us (6%)
  blocking collectives  207 us (4%)
    reduce_scatter x1, waiting for transfers between devices, shards(): lax.psum_scatter(grad_expert_full, ('dp', 'blk'), scatter_dimension=1, ti...  2100 us
    psum x5, waiting for transfers between devices, summed_grams(): lax.psum((attn_gram, router_gram, placed), 'blk')  1710 us
    unnamed x14, waiting for transfers between devices  210 us
  transfers between devices with their start and end apart: 13, of which 9 were waited for; matrix products, arithmetic and copies ran while one was open for 12% of the time, Pallas kernels for 0%

commit v1 on v0

v1 whole, which is shorter than its diff:
```python
import functools
import math

import jax
import jax.numpy as jnp
from jax import lax
from jax.experimental import pallas as pl
from jax.experimental.layout import Layout, with_layout_constraint
from jax.experimental.pallas import tpu as pltpu
from jax.sharding import PartitionSpec as P

D = 1024
HEADS = 16
KV_HEADS = 8
HEAD_DIM = 64
FF = 512
TOP = 8
EXPERTS = 16
STEP = 10
HALF = D // 2
PACK = 128
AXES = ("dp", "blk")


NORM_EPS = 1e-05
ATTN_MULT = 0.015625
RESID_MULT = 0.22
ROPE_BASE = 10000.0
NEG_FILL = -1e30
POLY_ONE = 3.4445
POLY_TWO = -4.775
POLY_THREE = 2.0315
ORTHO_EPS = 1e-07
MOMENTUM = 0.95
MUON_RATE = 0.6
MUON_SHAPE = 0.2
WEIGHT_DECAY = 0.01
ADAM_RATE = 0.8
BETA_ONE = 0.9
BETA_TWO = 0.95
ADAM_EPS = 1e-08
EMA_KEEP = 0.9
GAIN_EMA_KEEP = 0.6


def plain_dot(left_side, right_side, contract_left, contract_right):
    return lax.dot_general(
        left_side,
        right_side,
        (((contract_left,), (contract_right,)), ((), ())),
        preferred_element_type=jnp.float32,
    )


def rotary_tables(length, head_width):
    position = jnp.arange(length).astype(jnp.float32)
    inverse = ROPE_BASE ** (-jnp.arange(0, head_width, 2).astype(jnp.float32) / head_width)
    angles = position[:, None] * inverse[None, :]
    return (jnp.cos(angles), jnp.sin(angles))


def norm_back(grad_normed, unit_rows, scale_rows, gain_row):
    grad_unit = grad_normed * gain_row
    return scale_rows * (
        grad_unit - unit_rows * jnp.mean(grad_unit * unit_rows, axis=-1, keepdims=True)
    )


def pin(values):
    return with_layout_constraint(values, Layout(major_to_minor=tuple(range(values.ndim))))


def swap_bit(values, count, bit):
    pairs = [(place, place ^ bit) for place in range(count)]
    return pin(lax.ppermute(pin(values), AXES, pairs))


def after(values, *done):
    return lax.optimization_barrier((values,) + done)[0]


def low_add(left_side, right_side):
    return (left_side.astype(jnp.float32) + right_side.astype(jnp.float32)).astype(jnp.bfloat16)


def bits_below(low_bit, high_bit):
    bits = []
    while low_bit < high_bit:
        bits.append(low_bit)
        low_bit *= 2
    return bits


def gather_rows(values, axis, count, place, bits):
    for bit in bits:
        other = swap_bit(values, count, bit)
        upper = (place // bit) % 2 == 1
        values = jnp.where(
            upper,
            jnp.concatenate([other, values], axis=axis),
            jnp.concatenate([values, other], axis=axis),
        )
    return values


def reduce_rows(values, count, place, bits):
    for bit in bits:
        split = values.reshape((2, values.shape[0] // 2) + values.shape[1:])
        own = (place // bit) % 2
        keep = lax.dynamic_index_in_dim(split, own, 0, keepdims=False)
        other = swap_bit(
            lax.dynamic_index_in_dim(split, 1 - own, 0, keepdims=False), count, bit
        )
        values = low_add(keep, other)
    return values


def dot_nn(left_side, right_side):
    return plain_dot(left_side, right_side, 1, 0)


def dot_nt(left_side, right_side):
    return plain_dot(left_side, right_side, 1, 1)


def dot_tn(left_side, right_side):
    return plain_dot(left_side, right_side, 0, 0)


def turn(values, cosine, sine, lanes):
    far = jnp.where(
        lanes % HEAD_DIM < HEAD_DIM // 2,
        pltpu.roll(values, PACK - HEAD_DIM // 2, 1),
        pltpu.roll(values, HEAD_DIM // 2, 1),
    )
    return values * cosine + far * sine


def project_kernel(
    tok_ref, gain_ref, wq_ref, wkv_ref, cos_ref, sin_ref, norm_ref, q_ref, k_ref, v_ref
):
    rows = tok_ref.shape[0]
    inputs = tok_ref[...].astype(jnp.float32)
    scale = lax.rsqrt(jnp.mean(inputs * inputs, axis=-1, keepdims=True) + NORM_EPS)
    normed = (inputs * scale * gain_ref[...]).astype(jnp.bfloat16)
    norm_ref[...] = normed
    cosine, sine = cos_ref[...], sin_ref[...]
    lanes = lax.broadcasted_iota(jnp.int32, (rows, PACK), 1)
    query = dot_nn(normed, wq_ref[...])
    for start in range(0, HEADS * HEAD_DIM, PACK):
        turned = turn(query[:, start : start + PACK], cosine, sine, lanes)
        q_ref[:, start : start + PACK] = turned.astype(jnp.bfloat16) * ATTN_MULT
    both = dot_nn(normed, wkv_ref[...])
    width = KV_HEADS * HEAD_DIM
    for start in range(0, width, PACK):
        turned = turn(both[:, start : start + PACK], cosine, sine, lanes)
        k_ref[:, start : start + PACK] = turned.astype(jnp.bfloat16)
    v_ref[...] = both[:, width:].astype(jnp.bfloat16)


def project_call(tokens, gain_row, wq, wkv, cosine, sine):
    seq_rows = cosine.shape[0]
    rows = min(256, seq_rows)
    repeats = seq_rows // rows
    tok_here = tokens.shape[0]
    width = KV_HEADS * HEAD_DIM
    low = jnp.bfloat16
    return pl.pallas_call(
        project_kernel,
        grid=(tok_here // rows,),
        in_specs=[
            pl.BlockSpec((rows, D), lambda b: (b, 0)),
            pl.BlockSpec((1, D), lambda b: (0, 0)),
            pl.BlockSpec((D, HEADS * HEAD_DIM), lambda b: (0, 0)),
            pl.BlockSpec((D, 2 * width), lambda b: (0, 1)),
            pl.BlockSpec((rows, PACK), lambda b: (b % repeats, 0)),
            pl.BlockSpec((rows, PACK), lambda b: (b % repeats, 0)),
        ],
        out_specs=[
            pl.BlockSpec((rows, D), lambda b: (b, 0)),
            pl.BlockSpec((rows, HEADS * HEAD_DIM), lambda b: (b, 0)),
            pl.BlockSpec((rows, width), lambda b: (b, 0)),
            pl.BlockSpec((rows, width), lambda b: (b, 0)),
        ],
        out_shape=[
            jax.ShapeDtypeStruct((tok_here, D), low),
            jax.ShapeDtypeStruct((tok_here, HEADS * HEAD_DIM), low),
            jax.ShapeDtypeStruct((tok_here, width), low),
            jax.ShapeDtypeStruct((tok_here, width), low),
        ],
        compiler_params=pltpu.CompilerParams(
            dimension_semantics=("arbitrary",), vmem_limit_bytes=40 * 1024 * 1024
        ),
        cost_estimate=pl.CostEstimate(
            flops=8_000_000_000, bytes_accessed=14_000_000, transcendentals=0
        ),
        name="project",
    )(tokens, gain_row, wq, wkv, cosine, sine)


def attend_kernel(len_ref, q_ref, k_ref, v_ref, *refs):
    o_ref, lse_ref = refs[-2:]
    seq_len = q_ref.shape[0]
    rows = min(256, seq_len)
    length = len_ref[0, 0]
    for first in range(0, seq_len, rows):
        keys = first + rows
        key_index = lax.broadcasted_iota(jnp.int32, (rows, keys), 1)
        query_index = first + lax.broadcasted_iota(jnp.int32, (rows, keys), 0)
        bias = jnp.where((key_index <= query_index) & (key_index < length), 0.0, NEG_FILL)
        lanes = lax.broadcasted_iota(jnp.int32, (rows, PACK), 1)
        totals = jnp.zeros((rows, PACK), jnp.float32)
        for head in range(4):
            shared = (head // 2) * HEAD_DIM
            key_rows = k_ref[:keys, shared : shared + HEAD_DIM]
            value_rows = v_ref[:keys, shared : shared + HEAD_DIM]
            query = q_ref[first:keys, head * HEAD_DIM : (head + 1) * HEAD_DIM]
            scores = dot_nt(query, key_rows) + bias
            largest = jnp.max(scores, axis=1, keepdims=True)
            exponent = jnp.exp(scores - largest)
            total = jnp.sum(exponent, axis=1, keepdims=True)
            probability = (exponent * (1.0 / total)).astype(jnp.bfloat16)
            o_ref[first:keys, head * HEAD_DIM : (head + 1) * HEAD_DIM] = dot_nn(
                probability, value_rows
            ).astype(jnp.bfloat16)
            totals = jnp.where(lanes == head, largest + jnp.log(total), totals)
        lse_ref[0, :, first:keys] = totals.T[:8]


def attend_call(lengths, query, key_rows, value_rows, seq_len, done):
    tok_here = query.shape[0]
    seqs = tok_here // seq_len
    groups = KV_HEADS // 2
    return pl.pallas_call(
        attend_kernel,
        grid=(seqs, groups),
        in_specs=[
            pl.BlockSpec((1, 1), lambda s, g: (s, 0), memory_space=pltpu.SMEM),
            pl.BlockSpec((seq_len, 4 * HEAD_DIM), lambda s, g: (s, g)),
            pl.BlockSpec((seq_len, PACK), lambda s, g: (s, g)),
            pl.BlockSpec((seq_len, PACK), lambda s, g: (s, g)),
        ]
        + [pl.BlockSpec(memory_space=pl.ANY)] * len(done),
        out_specs=[
            pl.BlockSpec((seq_len, 4 * HEAD_DIM), lambda s, g: (s, g)),
            pl.BlockSpec((1, 8, seq_len), lambda s, g: (g, 0, s)),
        ],
        out_shape=[
            jax.ShapeDtypeStruct((tok_here, HEADS * HEAD_DIM), jnp.bfloat16),
            jax.ShapeDtypeStruct((groups, 8, tok_here), jnp.float32),
        ],
        compiler_params=pltpu.CompilerParams(
            dimension_semantics=("arbitrary", "arbitrary"), vmem_limit_bytes=40 * 1024 * 1024
        ),
        cost_estimate=pl.CostEstimate(
            flops=20_000_000_000, bytes_accessed=8_000_000, transcendentals=12_000_000
        ),
        name="attend",
    )(lengths.reshape(seqs, 1), query, key_rows, value_rows, *done)


def attend_back_kernel(
    len_ref,
    q_ref,
    k_ref,
    v_ref,
    do_ref,
    lse_ref,
    cos_ref,
    sin_ref,
    *refs,
):
    dq_ref, dk_ref, dv_ref, k_acc, v_acc = refs[-5:]
    seq_len = q_ref.shape[0]
    rows = min(256, seq_len)
    length = len_ref[0, 0]
    k_acc[...] = jnp.zeros_like(k_acc)
    v_acc[...] = jnp.zeros_like(v_acc)
    lanes = lax.broadcasted_iota(jnp.int32, (rows, PACK), 1)
    turned_keys = [
        k_ref[:, shared : shared + HEAD_DIM].T for shared in (0, HEAD_DIM)
    ]
    for first in range(0, seq_len, rows):
        keys = first + rows
        key_index = lax.broadcasted_iota(jnp.int32, (keys, rows), 0)
        query_index = first + lax.broadcasted_iota(jnp.int32, (keys, rows), 1)
        bias = jnp.where((key_index <= query_index) & (key_index < length), 0.0, NEG_FILL)
        for pair in range(2):
            shared = pair * HEAD_DIM
            key_rows = k_ref[:keys, shared : shared + HEAD_DIM]
            value_rows = v_ref[:keys, shared : shared + HEAD_DIM]
            key_grad = None
            value_grad = None
            query_grads = []
            for head in (2 * pair, 2 * pair + 1):
                query = q_ref[first:keys, head * HEAD_DIM : (head + 1) * HEAD_DIM]
                grad = do_ref[first:keys, head * HEAD_DIM : (head + 1) * HEAD_DIM]
                scores = dot_nt(key_rows, query) + bias
                probability = jnp.exp(scores - lse_ref[0, head : head + 1, first:keys])
                prob_grad = dot_nt(value_rows, grad)
                inner = jnp.sum(probability * prob_grad, axis=0, keepdims=True)
                score_grad = (probability * (prob_grad - inner)).astype(jnp.bfloat16)
                key_part = dot_nn(score_grad, query)
                value_part = dot_nn(probability.astype(jnp.bfloat16), grad)
                key_grad = key_part if key_grad is None else key_grad + key_part
                value_grad = value_part if value_grad is None else value_grad + value_part
                query_grads.append(dot_nn(turned_keys[pair][:, :keys], score_grad))
            k_acc[:keys, shared : shared + HEAD_DIM] += key_grad
            v_acc[:keys, shared : shared + HEAD_DIM] += value_grad
            query_grad = jnp.concatenate(query_grads, axis=0).T * ATTN_MULT
            dq_ref[first:keys, pair * PACK : (pair + 1) * PACK] = turn(
                query_grad, cos_ref[first:keys, :], -sin_ref[first:keys, :], lanes
            ).astype(jnp.bfloat16)
    for first in range(0, seq_len, rows):
        keys = first + rows
        dk_ref[first:keys, :] = turn(
            k_acc[first:keys, :], cos_ref[first:keys, :], -sin_ref[first:keys, :], lanes
        ).astype(jnp.bfloat16)
        dv_ref[first:keys, :] = v_acc[first:keys, :].astype(jnp.bfloat16)


def attend_back_call(
    part, lengths, query, key_rows, value_rows, grad, totals, cosine, sine, held, done
):
    tok_here = query.shape[0]
    seq_len = cosine.shape[0]
    seqs = tok_here // seq_len
    groups = KV_HEADS // 4
    skip = part * groups
    wide = pl.BlockSpec((seq_len, 4 * HEAD_DIM), lambda s, g: (s, g + skip))
    narrow = pl.BlockSpec((seq_len, PACK), lambda s, g: (s, g + skip))
    table = pl.BlockSpec((seq_len, PACK), lambda s, g: (0, 0))
    return pl.pallas_call(
        attend_back_kernel,
        grid=(seqs, groups),
        in_specs=[
            pl.BlockSpec((1, 1), lambda s, g: (s, 0), memory_space=pltpu.SMEM),
            wide,
            narrow,
            narrow,
            wide,
            pl.BlockSpec((1, 8, seq_len), lambda s, g: (g + skip, 0, s)),
            table,
            table,
        ]
        + [pl.BlockSpec(memory_space=pl.ANY)] * (len(held) + len(done)),
        out_specs=[wide, narrow, narrow],
        out_shape=[
            jax.ShapeDtypeStruct((tok_here, HEADS * HEAD_DIM), jnp.bfloat16),
            jax.ShapeDtypeStruct((tok_here, KV_HEADS * HEAD_DIM), jnp.bfloat16),
            jax.ShapeDtypeStruct((tok_here, KV_HEADS * HEAD_DIM), jnp.bfloat16),
        ],
        input_output_aliases={8 + index: index for index in range(len(held))},
        scratch_shapes=[
            pltpu.VMEM((seq_len, PACK), jnp.float32),
            pltpu.VMEM((seq_len, PACK), jnp.float32),
        ],
        compiler_params=pltpu.CompilerParams(
            dimension_semantics=("arbitrary", "arbitrary"), vmem_limit_bytes=40 * 1024 * 1024
        ),
        cost_estimate=pl.CostEstimate(
            flops=24_000_000_000, bytes_accessed=8_000_000, transcendentals=6_000_000
        ),
        name="attend_back",
    )(
        lengths.reshape(seqs, 1),
        query,
        key_rows,
        value_rows,
        grad,
        totals,
        cosine,
        sine,
        *held,
        *done,
    )


def expert_kernel(waits, first, *refs):
    n2_ref, n2t_ref, dy_ref, gate_ref = refs[:4]
    wb_own_ref, wb_other_ref, wg_own_ref, wg_other_ref = refs[4:8]
    outs = refs[8 + waits :]
    own_ref, pair_ref, dgate_ref, grad_own_ref, grad_other_ref = outs[:5]
    m_acc, dn_acc, g_acc, u_acc, d_acc = outs[5:]
    step = pl.program_id(0)
    block = pl.program_id(1)
    blocks = pl.num_programs(1)
    rows = n2_ref.shape[0]
    place = pl.ds(pl.multiple_of(block * rows, rows), rows)
    lane = lax.broadcasted_iota(jnp.int32, (rows, PACK), 1)
    wg_own, wg_other = wg_own_ref[0, 0], wg_other_ref[0, 0]
    wu_own, wu_other = wb_own_ref[0, 0], wb_other_ref[0, 0]
    wd_own, wd_other = wb_own_ref[1, 0], wb_other_ref[1, 0]
    column = lane == step + first
    gate = jnp.sum(jnp.where(column, gate_ref[...], 0.0), axis=1, keepdims=True)
    dm = RESID_MULT * dy_ref[...].astype(jnp.float32)
    dout = (gate * dm).astype(jnp.bfloat16)
    ug = dot_nn(n2_ref[:, :HALF], wg_own) + dot_nn(n2_ref[:, HALF:], wg_other)
    uu = dot_nn(n2_ref[:, :HALF], wu_own) + dot_nn(n2_ref[:, HALF:], wu_other)
    dh = dot_nn(dout[:, :HALF], wd_own) + dot_nn(dout[:, HALF:], wd_other)
    sig = 1.0 / (1.0 + jnp.exp(-ug))
    silu = ug * sig
    hidden = (silu * uu).astype(jnp.bfloat16)
    dug = (dh * uu * sig * (1.0 + ug * (1.0 - sig))).astype(jnp.bfloat16)
    duu = (dh * silu).astype(jnp.bfloat16)
    y_own = dot_nt(hidden, wd_own)
    y_other = dot_nt(hidden, wd_other)
    n2t = n2t_ref[...]
    g_acc[...] = jnp.where(block == 0, 0.0, g_acc[...]) + dot_nn(n2t, dug)
    dgate = jnp.sum(dm[:, :HALF] * y_own, axis=1, keepdims=True) + jnp.sum(
        dm[:, HALF:] * y_other, axis=1, keepdims=True
    )
    dgate_ref[place, :] = jnp.where(
        column, dgate, jnp.where(step == 0, 0.0, dgate_ref[place, :])
    )
    m_acc[place, :HALF] = jnp.where(step == 0, 0.0, m_acc[place, :HALF]) + gate * y_own
    m_acc[place, HALF:] = jnp.where(step == 0, 0.0, m_acc[place, HALF:]) + gate * y_other
    u_acc[...] = jnp.where(block == 0, 0.0, u_acc[...]) + dot_nn(n2t, duu)
    dn_acc[place, :HALF] = (
        jnp.where(step == 0, 0.0, dn_acc[place, :HALF]) + dot_nt(dug, wg_own) + dot_nt(duu, wu_own)
    )
    dn_acc[place, HALF:] = (
        jnp.where(step == 0, 0.0, dn_acc[place, HALF:])
        + dot_nt(dug, wg_other)
        + dot_nt(duu, wu_other)
    )
    d_acc[...] = jnp.where(block == 0, 0.0, d_acc[...]) + dot_tn(hidden, dout)
    last = step == pl.num_programs(0) - 1

    @pl.when(last & (block < blocks // 2))
    def _():
        own_ref[0] = m_acc[place, :].astype(jnp.bfloat16)
        own_ref[1] = dn_acc[place, :].astype(jnp.bfloat16)

    @pl.when(last & (block >= blocks // 2))
    def _():
        pair_ref[0] = m_acc[place, :].astype(jnp.bfloat16)
        pair_ref[1] = dn_acc[place, :].astype(jnp.bfloat16)

    @pl.when(block == blocks - 1)
    def _():
        grad_own_ref[0, 0] = g_acc[:HALF, :].astype(jnp.bfloat16)
        grad_own_ref[1, 0] = u_acc[:HALF, :].astype(jnp.bfloat16)
        grad_own_ref[2, 0] = d_acc[:, :HALF].astype(jnp.bfloat16)
        grad_other_ref[0, 0] = g_acc[HALF:, :].astype(jnp.bfloat16)
        grad_other_ref[1, 0] = u_acc[HALF:, :].astype(jnp.bfloat16)
        grad_other_ref[2, 0] = d_acc[:, HALF:].astype(jnp.bfloat16)


def expert_call(first, n2, n2t, dy, gates, weights, done):
    tokens_all = n2.shape[0]
    rows = min(512, tokens_all // 2)
    half_blocks = tokens_all // rows // 2
    steps = weights[0].shape[1]

    def own_block(step, block):
        return (0, jnp.where(step == steps - 1, jnp.minimum(block, half_blocks - 1), 0), 0)

    def pair_block(step, block):
        return (0, jnp.where(step == steps - 1, jnp.maximum(block - half_blocks, 0), 0), 0)

    low = jnp.bfloat16

    def pieces(kinds):
        return pl.BlockSpec((kinds, 1, HALF, FF), lambda s, b: (0, s, 0, 0))

    half_shape = jax.ShapeDtypeStruct((2, tokens_all // 2, D), low)
    piece_shape = jax.ShapeDtypeStruct((3, steps, HALF, FF), low)
    outputs = pl.pallas_call(
        functools.partial(expert_kernel, len(done), first),
        grid=(steps, 2 * half_blocks),
        in_specs=[
            pl.BlockSpec((rows, D), lambda s, b: (b, 0)),
            pl.BlockSpec((D, rows), lambda s, b: (0, b)),
            pl.BlockSpec((rows, D), lambda s, b: (b, 0)),
            pl.BlockSpec((rows, PACK), lambda s, b: (b, 0)),
            pieces(2),
            pieces(2),
            pieces(1),
            pieces(1),
        ]
        + [pl.BlockSpec(memory_space=pl.ANY)] * len(done),
        out_specs=[
            pl.BlockSpec((2, rows, D), own_block, pipeline_mode=pl.Buffered(1)),
            pl.BlockSpec((2, rows, D), pair_block, pipeline_mode=pl.Buffered(1)),
            pl.BlockSpec((tokens_all, PACK), lambda s, b: (0, 0)),
            pieces(3),
            pieces(3),
        ],
        out_shape=[
            half_shape,
            half_shape,
            jax.ShapeDtypeStruct((tokens_all, PACK), jnp.float32),
            piece_shape,
            piece_shape,
        ],
        scratch_shapes=[
            pltpu.VMEM((tokens_all, D), jnp.float32),
            pltpu.VMEM((tokens_all, D), jnp.float32),
            pltpu.VMEM((D, FF), jnp.float32),
            pltpu.VMEM((D, FF), jnp.float32),
            pltpu.VMEM((FF, D), jnp.float32),
        ],
        compiler_params=pltpu.CompilerParams(
            dimension_semantics=("arbitrary", "arbitrary"), vmem_limit_bytes=60 * 1024 * 1024
        ),
        cost_estimate=pl.CostEstimate(
            flops=9 * 2 * tokens_all * D * FF * steps * 3 // 2,
            bytes_accessed=48 * 1024 * 1024,
            transcendentals=steps * tokens_all * FF,
        ),
        name="experts",
    )(n2, n2t, dy, gates, *weights, *done)
    return outputs


def high_dot(left_side, right_side):
    return jnp.matmul(left_side, right_side, precision=lax.Precision.HIGH)


def gram_of(rows):
    return jnp.einsum("...oe,...ol->...el", rows, rows, precision=lax.Precision.HIGH)


def polynomial(gram):
    eye = jnp.eye(gram.shape[-1], dtype=jnp.float32)
    return POLY_ONE * eye + POLY_TWO * gram + POLY_THREE * high_dot(gram, gram)


def ortho_rows(own_rows, all_rows):
    squares = jnp.sum(all_rows * all_rows, axis=(-2, -1), keepdims=True)
    scale = 1.0 / (jnp.sqrt(squares) + ORTHO_EPS)
    gram = gram_of(all_rows * scale)
    product = None
    for iteration in range(5):
        factor = polynomial(gram)
        product = factor if product is None else high_dot(product, factor)
        if iteration < 4:
            gram = high_dot(high_dot(gram, factor), factor)
    return high_dot(own_rows * scale, product)


def ortho_block(block, gram_mask, halves):
    squares = jnp.sum(block * block, axis=0)
    width = squares.shape[0] // 2
    lower, upper = jnp.sum(squares[:width]), jnp.sum(squares[width:])
    column = jnp.arange(squares.shape[0])
    own = jnp.where(column < width, lower, upper)
    scale = 1.0 / (jnp.sqrt(jnp.where(halves, own, lower + upper)) + ORTHO_EPS)
    iterate = block * scale[None, :]
    for iteration in range(5):
        gram = gram_of(iterate) * gram_mask
        change = POLY_TWO * gram + POLY_THREE * high_dot(gram, gram)
        iterate = POLY_ONE * iterate + high_dot(iterate, change)
    return iterate


def take_half(values, axis, own):
    keep = lax.dynamic_index_in_dim(values, own, axis, keepdims=False)
    send = lax.dynamic_index_in_dim(values, 1 - own, axis, keepdims=False)
    return keep, send


def reduce_to_owner(values, bits, count, place, order):
    left = bits[::-1]
    width = values.shape[1]
    for bit in order:
        before = 2 ** left.index(bit)
        left.remove(bit)
        split = values.reshape(before, 2, values.shape[0] // (2 * before), width)
        keep, send = take_half(split, 1, (place // bit) % 2)
        values = low_add(keep, swap_bit(send, count, bit)).reshape(-1, width)
    return values


def gather_from_owners(values, count, place, order, held=()):
    held = list(held)
    for bit in order:
        other = swap_bit(values, count, bit)
        held.append(bit)
        held.sort(reverse=True)
        after_bits = 2 ** (len(held) - 1 - held.index(bit))
        upper = (place // bit) % 2 == 1
        width = values.shape[1]
        pieces = (2 ** (len(held) - 1) // after_bits, 1, -1, width)
        own, other = values.reshape(pieces), other.reshape(pieces)
        values = jnp.where(
            upper,
            jnp.concatenate([other, own], axis=1),
            jnp.concatenate([own, other], axis=1),
        ).reshape(-1, width)
    return values


def muon_update(weight, ortho):
    return weight * (1.0 - MUON_RATE * WEIGHT_DECAY) - MUON_RATE * MUON_SHAPE * math.sqrt(D) * ortho


def shards(
    tokens,
    out_grad,
    lengths,
    routes,
    attn_weight,
    router_weight,
    expert_weight,
    gains,
    attn_moment,
    router_moment,
    expert_moment,
    gain_first,
    gain_second,
    attn_ema,
    router_ema,
    expert_ema,
    gain_ema,
):
    seqs_here = lengths.shape[0]
    tok_here = tokens.shape[0]
    seq_len = tok_here // seqs_here
    query_width = HEADS * HEAD_DIM
    kv_width = KV_HEADS * HEAD_DIM
    qkv_width = query_width + 2 * kv_width
    n_dp, n_blk = lax.axis_size("dp"), lax.axis_size("blk")
    count = n_dp * n_blk
    place = lax.axis_index(AXES)
    own_rows = expert_weight.shape[1]
    parts = D // own_rows
    half_bit, pair_bit = parts // 2, n_blk
    bit_z, bit_x, bit_y = [bit for bit in bits_below(parts, count) if bit != pair_bit]
    low_bits = bits_below(1, parts)
    upper_half = (place // half_bit) % 2 == 1
    groups = ((0, 0), (1, 0), (1, 1), (0, 1))
    far_bits = [
        far_x * bit_x + far_y * bit_y + far_z * bit_z
        for far_x, far_y in groups
        for far_z in range(2)
    ]
    own_experts = [(place ^ bits) // parts for bits in far_bits]
    pair_experts = [(place ^ pair_bit ^ bits) // parts for bits in far_bits]
    expert_ids = jnp.stack(own_experts + pair_experts)

    def relative(values):
        swapped = jnp.concatenate([values[:, HALF:], values[:, :HALF]], axis=1)
        return jnp.where(upper_half, swapped, values)

    attn_cols = attn_weight.shape[1]
    attn_low = attn_weight.astype(jnp.bfloat16)
    small_low = jnp.concatenate(
        [
            router_weight.astype(jnp.bfloat16),
            gains.astype(jnp.bfloat16).T,
            jnp.zeros((attn_weight.shape[0], PACK - EXPERTS - 2), jnp.bfloat16),
        ],
        axis=1,
    )
    full_packed = lax.all_gather(
        jnp.concatenate([attn_low, small_low], axis=1), AXES, axis=0, tiled=True
    )
    w_query = full_packed[:, :query_width]
    w_shared = full_packed[:, query_width:qkv_width]
    w_out = full_packed[:, qkv_width:attn_cols]
    full_router = full_packed[:, attn_cols : attn_cols + EXPERTS]
    full_gains = full_packed[:, attn_cols + EXPERTS : attn_cols + EXPERTS + 2].T
    early_bits = bits_below(1, half_bit)
    own_half = gather_rows(expert_weight.astype(jnp.bfloat16), 1, count, place, early_bits)
    level_one = (((1, 0, 0), half_bit), ((0, 1, 0), bit_x), ((0, 0, 1), bit_y))
    gather_last = (
        {(1, 1, 0): bit_x, (0, 1, 1): bit_y, (1, 0, 1): bit_y, (1, 1, 1): bit_x},
        {(1, 1, 0): half_bit, (0, 1, 1): bit_y, (1, 0, 1): half_bit, (1, 1, 1): bit_x},
    )
    hop_of = {half_bit: 0, bit_x: 1, bit_y: 2}

    def before_hop(chunk, bit):
        return tuple(
            side ^ 1 if index == hop_of[bit] else side for index, side in enumerate(chunk)
        )

    chunks = [{}, {}]
    before = None
    for part, kinds in enumerate((slice(1, 3), slice(0, 1))):
        own = own_half[kinds]
        if before is not None:
            own = after(own, before)
        before = swap_bit(own, count, bit_z)
        chunks[part][0, 0, 0] = after(jnp.stack([own, before], axis=1), full_packed)
        for chunk, bit in level_one:
            chunks[part][chunk] = swap_bit(chunks[part][0, 0, 0], count, bit)
    for chunk in ((1, 1, 0), (0, 1, 1), (1, 0, 1), (1, 1, 1)):
        for part in range(2):
            bit = gather_last[part][chunk]
            chunks[part][chunk] = swap_bit(chunks[part][before_hop(chunk, bit)], count, bit)
    gain_one = full_gains[0].astype(jnp.float32)
    gain_two = full_gains[1].astype(jnp.float32)
    inputs = tokens.astype(jnp.float32)
    cosine, sine = rotary_tables(seq_len, HEAD_DIM)
    cosine = jnp.concatenate([cosine] * 4, axis=1)
    sine = jnp.concatenate([-sine, sine, -sine, sine], axis=1)
    normed_one, query, key_rows, value_rows = project_call(
        tokens, gain_one[None], full_packed, full_packed, cosine, sine
    )
    position = jnp.arange(seq_len)
    live_rows = (position[None, :] < lengths[:, None]).reshape(tok_here, 1)
    live_grad = jnp.where(live_rows, out_grad, jnp.zeros_like(out_grad))
    live_relative = after(relative(live_grad), normed_one)
    both_grad = jnp.concatenate([live_relative, swap_bit(live_relative, count, pair_bit)])
    rows_each = attn_moment.shape[0]
    block_width = attn_cols // 3

    def spread(values):
        return lax.all_to_all(values, "blk", split_axis=0, concat_axis=0, tiled=True)

    old_pieces = [attn_moment[:, :block_width], attn_moment[:, block_width : 2 * block_width]]
    old_pieces += [
        attn_moment[:, 2 * block_width :],
        jnp.pad(router_moment, ((0, 0), (0, block_width - EXPERTS))),
    ]
    old_tasks = jnp.pad(jnp.stack(old_pieces), ((0, n_blk - 4), (0, 0), (0, 0)))
    old_tasks = spread(old_tasks).reshape(n_blk * rows_each, block_width)
    attended, totals = attend_call(
        lengths,
        query,
        key_rows,
        value_rows,
        seq_len,
        [chunks[1][0, 0, 0], old_tasks],
    )
    branch = plain_dot(attended, w_out, 1, 1)
    branch = after(branch, *[chunks[0][chunk] for chunk, _ in level_one])
    hidden_state = inputs + RESID_MULT * branch
    scale_two = lax.rsqrt(jnp.mean(hidden_state * hidden_state, axis=-1, keepdims=True) + NORM_EPS)
    unit_two = hidden_state * scale_two
    normed_two = (unit_two * gain_two).astype(jnp.bfloat16)
    pick = (jnp.arange(EXPERTS)[:, None] == expert_ids[None, :]).astype(jnp.bfloat16)
    router_here = jnp.dot(full_router, pick, preferred_element_type=jnp.float32).astype(
        jnp.bfloat16
    )
    logits = jnp.dot(normed_two, router_here, preferred_element_type=jnp.float32)
    used = jnp.any(routes[:, :, None] == expert_ids[None, None, :], axis=1)
    chosen_top = jnp.max(jnp.where(used, logits, NEG_FILL), axis=1, keepdims=True)
    exponent = jnp.where(used, jnp.exp(jnp.where(used, logits - chosen_top, 0.0)), 0.0)
    gate_weights = exponent / jnp.sum(exponent, axis=1, keepdims=True)
    second = relative(normed_two)
    other_second = swap_bit(second, count, pair_bit)
    gates_here = jnp.pad(gate_weights[:, :8], ((0, 0), (0, PACK - 8)))
    gates_there = jnp.pad(gate_weights[:, 8:], ((0, 0), (0, PACK - 8)))
    other_gates = swap_bit(gates_there, count, pair_bit)
    both_second = jnp.concatenate([second, other_second])
    turned = second.T
    both_turned = jnp.concatenate([turned, swap_bit(turned, count, pair_bit)], axis=1)
    both_gates = jnp.concatenate([gates_here, other_gates])
    own_parts, pair_parts, dgates = [], [], []
    grads, moved = {}, {}

    def send(chunk, bit):
        moved[chunk] = swap_bit(grads[chunk], count, bit)

    waits = {
        (0, 0): lambda: [chunks[part][0, 1, 0] for part in range(2)]
        + [chunks[part][0, 0, 1] for part in range(2)],
        (1, 0): lambda: [],
        (1, 1): lambda: [moved[1, 0, 0], pair_parts[0]],
        (0, 1): lambda: [moved[1, 1, 0], pair_parts[1]],
    }
    for turn_index, (far_x, far_y) in enumerate(groups):
        weights = [chunks[part][half, far_x, far_y] for part in range(2) for half in range(2)]
        own_part, pair_part, dgate, grad_own, grad_other = expert_call(
            2 * turn_index,
            both_second,
            both_turned,
            both_grad,
            both_gates,
            weights,
            waits[far_x, far_y](),
        )
        own_parts.append(own_part)
        pair_parts.append(swap_bit(pair_part, count, pair_bit))
        dgates.append(dgate)
        grads[0, far_x, far_y] = grad_own
        grads[1, far_x, far_y] = grad_other
        if (far_x, far_y) == (0, 0):
            send((1, 0, 0), half_bit)
        if (far_x, far_y) == (1, 0):
            send((1, 1, 0), half_bit)
        if (far_x, far_y) == (1, 1):
            send((1, 1, 1), bit_x)
            send((0, 1, 1), bit_y)

    def total_of(*pieces):
        total = pieces[0].astype(jnp.float32)
        for piece in pieces[1:]:
            total = total + piece.astype(jnp.float32)
        return total.astype(jnp.bfloat16)

    last_other, grads[0, 0, 1], own_parts[3], dgates[3], *others = (
        lax.optimization_barrier(
            (
                grads[1, 0, 1],
                grads[0, 0, 1],
                own_parts[3],
                dgates[3],
                moved[1, 1, 1],
                moved[0, 1, 1],
                pair_parts[2],
            )
        )
    )
    moved[1, 1, 1], moved[0, 1, 1], pair_parts[2] = others
    half_y = [
        swap_bit(total_of(last_other[kind], moved[1, 1, 1][kind]), count, half_bit)
        for kind in range(3)
    ]
    grads[0, 1, 0] = total_of(grads[0, 1, 0], moved[1, 1, 0], moved[0, 1, 1])
    send((0, 1, 0), bit_x)
    dgate_sum = (dgates[0] + dgates[1]) + (dgates[2] + dgates[3])
    pair_dgates = swap_bit(dgate_sum[tok_here:], count, pair_bit)

    def gather_sum(parts):
        total = None
        for part in parts:
            part = part.astype(jnp.float32)
            total = part if total is None else total + part
        return relative(total)

    grad_normed_two = gather_sum([part[1] for part in own_parts + pair_parts])
    grad_gates = jnp.concatenate([dgate_sum[:tok_here, :8], pair_dgates[:, :8]], axis=1)
    grad_out = live_grad.astype(jnp.float32)
    inner_sum = jnp.sum(gate_weights * grad_gates, axis=1, keepdims=True)
    grad_logits = (gate_weights * (grad_gates - inner_sum)).astype(jnp.bfloat16)
    grad_normed_two = grad_normed_two + plain_dot(grad_logits, router_here, 1, 1)
    grad_router = jnp.matmul(
        plain_dot(normed_two, grad_logits, 0, 0),
        pick.astype(jnp.float32).T,
        precision=lax.Precision.HIGHEST,
    )
    grad_hidden_state = grad_out + norm_back(grad_normed_two, unit_two, scale_two, gain_two)
    grad_gain_two = jnp.sum(grad_normed_two * unit_two, axis=0)
    grad_branch = (RESID_MULT * grad_hidden_state).astype(jnp.bfloat16)
    grad_w_out = plain_dot(grad_branch, attended, 0, 0)
    dp_bits = bits_below(n_blk, count)
    far_dp = [bit for bit in dp_bits if bit not in (pair_bit, bit_x, bit_y)]
    first_x = [pair_bit, bit_x, bit_y] + far_dp
    first_y = [pair_bit, bit_y, bit_x] + far_dp

    def to_dp(values, order):
        return reduce_to_owner(values, dp_bits, count, place, order)

    low_grad_out = pin(grad_w_out.astype(jnp.bfloat16))
    grad_attended = jnp.dot(grad_branch, w_out, preferred_element_type=jnp.float32).astype(
        jnp.bfloat16
    )
    last_own = after(grads[0, 0, 1], grad_attended)
    from_y = [
        swap_bit(total_of(last_own[kind], half_y[kind]), count, bit_y) for kind in range(3)
    ]
    def attend_back(part, held, done):
        return attend_back_call(
            part,
            lengths,
            query,
            key_rows,
            value_rows,
            grad_attended,
            totals,
            cosine,
            sine,
            held,
            done,
        )

    grad_query, grad_key, grad_value = attend_back(
        1, attend_back(0, [], half_y), [moved[0, 1, 0]]
    )
    late_parts = after(tuple(own_parts + pair_parts), grad_query)
    block_out = (hidden_state + RESID_MULT * gather_sum([part[0] for part in late_parts])).astype(
        jnp.bfloat16
    )
    low_grad = [
        pin(plain_dot(normed_one, piece, 0, 0).astype(jnp.bfloat16))
        for piece in (grad_query, grad_key, grad_value)
    ]
    nearest = after(grads[0, 0, 0], low_grad[0])
    expert_sums = [
        total_of(nearest[kind], moved[1, 0, 0][kind], moved[0, 1, 0][kind], from_y[kind])
        for kind in range(3)
    ]
    late_query = after(grad_query, *from_y)
    grad_normed_one = (
        plain_dot(late_query, w_query, 1, 1)
        + plain_dot(grad_key, w_shared[:, :kv_width], 1, 1)
        + plain_dot(grad_value, w_shared[:, kv_width:], 1, 1)
    )
    scale_one = lax.rsqrt(jnp.mean(inputs * inputs, axis=-1, keepdims=True) + NORM_EPS)
    unit_one = inputs * scale_one
    input_grad = grad_hidden_state + norm_back(grad_normed_one, unit_one, scale_one, gain_one)
    grad_gain_one = jnp.sum(grad_normed_one * unit_one, axis=0)
    grad_small = jnp.concatenate(
        [
            grad_router,
            jnp.stack([grad_gain_one, grad_gain_two], axis=1),
            jnp.zeros((D, PACK - EXPERTS - 2), jnp.float32),
        ],
        axis=1,
    ).astype(jnp.bfloat16)
    query_sum = to_dp(low_grad[0], first_x)
    shared_sum = to_dp(jnp.concatenate([low_grad[1], low_grad[2], pin(grad_small)], axis=1), first_y)
    out_sum = to_dp(after(low_grad_out, grad_query), first_x)

    def as_tasks(first, second, third, small):
        small = jnp.pad(small, ((0, 0), (0, block_width - PACK)))
        tasks = jnp.stack([first, second, third, small])
        return jnp.pad(tasks, ((0, n_blk - 4), (0, 0), (0, 0)))

    task_parts = spread(
        as_tasks(
            query_sum, shared_sum[:, :block_width], out_sum, shared_sum[:, block_width:]
        )
    )
    task_block = MOMENTUM * old_tasks + jnp.sum(task_parts.astype(jnp.float32), axis=0)
    moment_rows = spread(task_block.reshape(n_blk, rows_each, block_width))
    moment_attn = jnp.concatenate([moment_rows[0], moment_rows[1], moment_rows[2]], axis=1)
    moment_router = moment_rows[3][:, :EXPERTS]
    gain_grad = moment_rows[3][:, EXPERTS : EXPERTS + 2].T
    used_columns = (jnp.arange(block_width) < EXPERTS) | (lax.axis_index("blk") != 3)
    task_block = jnp.where(used_columns, task_block, 0.0)
    wide_x, wide_y = far_dp + [bit_y, bit_x], far_dp + [bit_x, bit_y]
    sides = [
        gather_from_owners(task_block[:, : block_width // 2], count, place, wide_x),
        gather_from_owners(task_block[:, block_width // 2 :], count, place, wide_y),
    ]
    moment_expert, ortho_expert = [], []
    for kind in range(3):
        total = expert_sums[kind]
        total = total[0].astype(jnp.float32) + swap_bit(total[1], count, bit_z).astype(jnp.float32)
        total = total.T if kind == 2 else total
        if early_bits:
            total = reduce_rows(total.astype(jnp.bfloat16), count, place, early_bits[::-1])
        moment = MOMENTUM * expert_moment[kind] + total.astype(jnp.float32)
        group_rows = moment
        for bit in low_bits:
            group_rows = jnp.concatenate([group_rows, swap_bit(group_rows, count, bit)])
        if kind == 1:
            group_rows = after(group_rows, task_block)
        if kind == 2:
            group_rows = after(group_rows, *sides)
        moment_expert.append(moment)
        ortho_expert.append(ortho_rows(moment, group_rows))
    attn_block = jnp.concatenate(
        [gather_from_owners(side, count, place, [pair_bit], wide_x) for side in sides], axis=1
    )
    column_half = jnp.arange(block_width) >= block_width // 2
    halves = lax.axis_index("blk") == 1
    gram_mask = jnp.where(
        (column_half[:, None] == column_half[None, :]) | ~halves, 1.0, 0.0
    ).astype(jnp.float32)
    attn_iter = ortho_block(attn_block, gram_mask, halves)
    returned = lax.dynamic_slice_in_dim(
        attn_iter, lax.axis_index("dp") * (n_blk * rows_each), n_blk * rows_each, 0
    )
    returned = spread(returned.reshape(n_blk, rows_each, block_width))
    ortho_attn = jnp.concatenate([returned[0], returned[1], returned[2]], axis=1)
    ortho_router = returned[3][:, :EXPERTS]
    moment_expert = jnp.stack(moment_expert)
    attn_new = muon_update(attn_weight, ortho_attn)
    router_new = muon_update(router_weight, ortho_router)
    expert_new = muon_update(expert_weight, jnp.stack(ortho_expert))
    first_new = BETA_ONE * gain_first + (1.0 - BETA_ONE) * gain_grad
    second_new = BETA_TWO * gain_second + (1.0 - BETA_TWO) * gain_grad * gain_grad
    corrected_first = first_new / (1.0 - BETA_ONE**STEP)
    corrected_second = second_new / (1.0 - BETA_TWO**STEP)
    gain_new = gains - ADAM_RATE * corrected_first / (jnp.sqrt(corrected_second) + ADAM_EPS)
    return (
        block_out,
        input_grad,
        moment_attn,
        moment_router,
        moment_expert,
        attn_new,
        router_new,
        expert_new,
        attn_new.astype(jnp.bfloat16),
        router_new.astype(jnp.bfloat16),
        expert_new.astype(jnp.bfloat16),
        EMA_KEEP * attn_ema + (1.0 - EMA_KEEP) * attn_new,
        EMA_KEEP * router_ema + (1.0 - EMA_KEEP) * router_new,
        EMA_KEEP * expert_ema + (1.0 - EMA_KEEP) * expert_new,
        first_new,
        second_new,
        gain_new,
        gain_new.astype(jnp.bfloat16),
        GAIN_EMA_KEEP * gain_ema + (1.0 - GAIN_EMA_KEEP) * gain_new,
    )


def solution(mesh):
    placed = (
        P(("dp", "blk"), None),
        P(("dp", "blk"), None),
        P(("dp", "blk")),
        P(("dp", "blk"), None),
        P(("dp", "blk"), None),
        P(("dp", "blk"), None),
        P(None, ("dp", "blk"), None),
        P(None, ("dp", "blk")),
        P(("dp", "blk"), None),
        P(("dp", "blk"), None),
        P(None, ("dp", "blk"), None),
        P(None, ("dp", "blk")),
        P(None, ("dp", "blk")),
        P(("dp", "blk"), None),
        P(("dp", "blk"), None),
        P(None, ("dp", "blk"), None),
        P(None, ("dp", "blk")),
    )
    return jax.shard_map(
        shards,
        mesh=mesh,
        in_specs=placed,
        out_specs=(
            P(("dp", "blk"), None),
            P(("dp", "blk"), None),
            P(("dp", "blk"), None),
            P(("dp", "blk"), None),
            P(None, ("dp", "blk"), None),
            P(("dp", "blk"), None),
            P(("dp", "blk"), None),
            P(None, ("dp", "blk"), None),
            P(("dp", "blk"), None),
            P(("dp", "blk"), None),
            P(None, ("dp", "blk"), None),
            P(("dp", "blk"), None),
            P(("dp", "blk"), None),
            P(None, ("dp", "blk"), None),
            P(None, ("dp", "blk")),
            P(None, ("dp", "blk")),
            P(None, ("dp", "blk")),
            P(None, ("dp", "blk")),
            P(None, ("dp", "blk")),
        ),
        check_vma=False,
    )
```

time: 5810 us -> 1100 us (0.19)
  waiting for transfers between devices: 4120 us -> 241 us
  matrix products: 669 us -> 233 us
  local copies, waits for them, and re-layouts: 458 us -> 100 us
  Pallas kernels: 0 us -> 303 us
  blocking collectives: 207 us -> 0 us
  other arithmetic: 322 us -> 128 us
  starting transfers between devices: 5.06 us -> 67.1 us
    reduce_scatter x2 -> x0, waiting for transfers between devices: 2200 us -> none  [the longest x1 2100 us: shards(): lax.psum_scatter(grad_expert_full, ('dp', 'blk'), scatter_dimension=1, ti...]
    psum x5 -> x0, waiting for transfers between devices: 1710 us -> none  [summed_grams(): lax.psum((attn_gram, router_gram, placed), 'blk')]
    dot_general x68 -> x75, matrix products: 629 us -> 194 us  [the longest x64 142 us: high_dot(): return jnp.matmul(left_side, right_side, precision=lax.Precision.HIGH)]
    pallas_call x0 -> x8, Pallas kernels: none -> 303 us  [the longest x4 215 us: expert_call(): pl.pallas_call(functools.partial(expert_kernel, len(done), first), grid=(...]
    gather x10 -> x0, local copies, waits for them, and re-layouts: 270 us -> none  [the longest x2 73.1 us: shards(): normed_two[owner_token] * filled[:, None]]
    ppermute x0 -> x57, waiting for transfers between devices: none -> 217 us  [swap_bit(): return pin(lax.ppermute(pin(values), AXES, pairs))]
    unnamed x14 -> x1, waiting for transfers between devices: 210 us -> 0.02 us
    all_gather x3 -> x0, blocking collectives: 149 us -> none  [the longest x1 70.9 us: shards(): lax.all_gather(router_low, ('dp', 'blk'), axis=0, tiled=True)]
  transfers between devices with their start and end apart: 13 -> 62, of which waited for: 9 -> 17; matrix products, arithmetic and copies ran while one was open for 12% -> 36% of each run, Pallas kernels for 0% -> 28%
where the time goes in v1:
time: 1100 us; the launch traced here: 1090 us
  Pallas kernels  303 us (28%)
  waiting for transfers between devices  241 us (22%)
  matrix products  233 us (21%)
  other arithmetic  128 us (12%)
  local copies, waits for them, and re-layouts  100 us (9%)
  starting transfers between devices  67.1 us (6%)
  between operations  20.7 us (2%)
    ppermute x57, waiting for transfers between devices, swap_bit(): return pin(lax.ppermute(pin(values), AXES, pairs))  217 us
    pallas_call x4, Pallas kernels, expert_call(): pl.pallas_call(functools.partial(expert_kernel, len(done), first), grid=(...  215 us
    dot_general x64, matrix products, high_dot(): return jnp.matmul(left_side, right_side, precision=lax.Precision.HIGH)  142 us
    ppermute x57, starting transfers between devices, swap_bit(): return pin(lax.ppermute(pin(values), AXES, pairs))  49.8 us
    dot_general x8, matrix products, gram_of(): jnp.einsum('...oe,...ol->...el', rows, rows, precision=lax.Precision.HIGH)  47.3 us
    unnamed x262, local copies, waits for them, and re-layouts  46.8 us
    pallas_call x2, Pallas kernels, attend_back_call(): pl.pallas_call(attend_back_kernel, grid=(seqs, groups), in_specs=[pl.Bloc...  46.4 us
    pallas_call x1, Pallas kernels, attend_call(): pl.pallas_call(attend_kernel, grid=(seqs, groups), in_specs=[pl.BlockSpec...  33.7 us
  transfers between devices with their start and end apart: 62, of which 17 were waited for; matrix products, arithmetic and copies ran while one was open for 36% of the time, Pallas kernels for 28%

profile of v1, /device:TPU:0, one launch (start us, length us, event | category | flops | bytes accessed | tf_op | source)
XLA Modules:
  0.0 1092.7 jit_solution(1216603221201877048)
XLA Ops:
  30.4 54.6 %collective-permute-done = bf16[2,512,512]{2,1,0:T(8,128)(2,1)} collective-permute-done((bf16[2,512,512]{2,1,0:T(8,128)(2,1)}, bf16[2,512,512]{2,1,0:T(8,128)(2,1)}, u32[]{:S(2)}, u32[]{:S(2)}) %collective-permute-start) | collective-permute-done | bytes 1048608 | tf_op jit(solution)/shard_map/ppermute | solution.py:75
  89.9 39.9 %collective-permute-done.1 = bf16[1,512,512]{2,1,0:T(8,128)(2,1)S(1)} collective-permute-done((bf16[1,512,512]{2,1,0:T(8,128)(2,1)S(1)}, bf16[1,512,512]{2,1,0:T(8,128)(2,1)S(1)}, u32[]{:S(2)}, u32[]{:S(2)}) %collective-permute-start.1) | collective-permute-done | bytes 524320 | tf_op jit(solution)/shard_map/ppermute | solution.py:75
  160.3 33.7 %attend.1 = (bf16[1024,1024]{1,0:T(8,128)(2,1)S(1)}, f32[4,8,1024]{2,1,0:T(8,128)S(1)}) custom-call(s32[1,1]{1,0:T(1,128)} %bitcast.346.len_ref, bf16[1024,1024]{1,0:T(8,128)(2,1)S(1)} %copy-done.24, bf16[1024,512]{1,0:T(8,128)(2,1)S(1)} %copy-done.28, bf16[1024,512]{1,0:T(8,128)(2,1)S(1)} %copy-done.32, bf16[1,2,512,512]{3,2,1,0:T(8,128)(2,1)S(1)} %copy-done.6, ...), custom_call_target="tpu_custom_call" | custom-call | flops 20000000000 | bytes 8000000 | tf_op jit(solution)/shard_map/attend/pallas_call | solution.py:234
  216.3 19.9 %collective-permute-done.10.refs_9_.refs_6_ = bf16[1,2,512,512]{3,2,1,0:T(8,128)(2,1)} collective-permute-done((bf16[1,2,512,512]{3,2,1,0:T(8,128)(2,1)S(1)}, bf16[1,2,512,512]{3,2,1,0:T(8,128)(2,1)}, u32[]{:S(2)}, u32[]{:S(2)}) %collective-permute-start.10) | collective-permute-done | bytes 1048608 | tf_op jit(solution)/shard_map/ppermute | solution.py:75
  266.8 53.7 %experts.4 = (bf16[2,1024,1024]{2,1,0:T(8,128)(2,1)}, bf16[2,1024,1024]{2,1,0:T(8,128)(2,1)}, f32[2048,128]{1,0:T(8,128)}, bf16[3,2,512,512]{3,2,1,0:T(8,128)(2,1)}, bf16[3,2,512,512]{3,2,1,0:T(8,128)(2,1)}) custom-call(bf16[2048,1024]{1,0:T(8,128)(2,1)} %pad_maximum_fusion.refs_0_, bf16[1024,2048]{1,0:T(8,128)(2,1)} %copy.227.refs_1_, ...), custom_call_target="tpu_custom_call" | custom-call | flops 57982058496 | bytes 50331648 | tf_op jit(solution)/shard_map/experts/pallas_call | solution.py:469
  324.2 53.9 %experts.5 = (bf16[2,1024,1024]{2,1,0:T(8,128)(2,1)}, bf16[2,1024,1024]{2,1,0:T(8,128)(2,1)}, f32[2048,128]{1,0:T(8,128)}, bf16[3,2,512,512]{3,2,1,0:T(8,128)(2,1)}, bf16[3,2,512,512]{3,2,1,0:T(8,128)(2,1)}) custom-call(bf16[2048,1024]{1,0:T(8,128)(2,1)} %pad_maximum_fusion.refs_0_, bf16[1024,2048]{1,0:T(8,128)(2,1)} %copy.227.refs_1_, ...), custom_call_target="tpu_custom_call" | custom-call | flops 57982058496 | bytes 50331648 | tf_op jit(solution)/shard_map/experts/pallas_call | solution.py:469
  379.3 10.7 collective-permute-done.16.refs_5_
  393.8 53.6 %experts.6 = (bf16[2,1024,1024]{2,1,0:T(8,128)(2,1)}, bf16[2,1024,1024]{2,1,0:T(8,128)(2,1)}, f32[2048,128]{1,0:T(8,128)}, bf16[3,2,512,512]{3,2,1,0:T(8,128)(2,1)}, bf16[3,2,512,512]{3,2,1,0:T(8,128)(2,1)}) custom-call(bf16[2048,1024]{1,0:T(8,128)(2,1)} %pad_maximum_fusion.refs_0_, bf16[1024,2048]{1,0:T(8,128)(2,1)} %copy.227.refs_1_, ...), custom_call_target="tpu_custom_call" | custom-call | flops 57982058496 | bytes 50331648 | tf_op jit(solution)/shard_map/experts/pallas_call | solution.py:469
  449.7 11.1 %collective-permute-done.22.refs_8_ = bf16[3,2,512,512]{3,2,1,0:T(8,128)(2,1)} collective-permute-done((bf16[3,2,512,512]{3,2,1,0:T(8,128)(2,1)}, bf16[3,2,512,512]{3,2,1,0:T(8,128)(2,1)}, u32[]{:S(2)}, u32[]{:S(2)}) %collective-permute-start.22) | collective-permute-done | bytes 3145760 | tf_op jit(solution)/shard_map/ppermute | solution.py:75
  460.8 54.2 %experts.7 = (bf16[2,1024,1024]{2,1,0:T(8,128)(2,1)}, bf16[2,1024,1024]{2,1,0:T(8,128)(2,1)}, f32[2048,128]{1,0:T(8,128)}, bf16[3,2,512,512]{3,2,1,0:T(8,128)(2,1)}, bf16[3,2,512,512]{3,2,1,0:T(8,128)(2,1)}) custom-call(bf16[2048,1024]{1,0:T(8,128)(2,1)} %pad_maximum_fusion.refs_0_, bf16[1024,2048]{1,0:T(8,128)(2,1)} %copy.227.refs_1_, ...), custom_call_target="tpu_custom_call" | custom-call | flops 57982058496 | bytes 50331648 | tf_op jit(solution)/shard_map/experts/pallas_call | solution.py:469
  566.1 17.0 %collective-permute-done.30.refs_1_ = bf16[2,512,512]{2,1,0:T(8,128)(2,1)S(1)} collective-permute-done((bf16[2,512,512]{2,1,0:T(8,128)(2,1)}, bf16[2,512,512]{2,1,0:T(8,128)(2,1)S(1)}, u32[]{:S(2)}, u32[]{:S(2)}) %collective-permute-start.30) | collective-permute-done | bytes 1048608 | tf_op jit(solution)/shard_map/ppermute | solution.py:75
  583.1 21.6 %collective-permute-done.31.refs_2_ = bf16[2,512,512]{2,1,0:T(8,128)(2,1)} collective-permute-done((bf16[2,512,512]{2,1,0:T(8,128)(2,1)}, bf16[2,512,512]{2,1,0:T(8,128)(2,1)}, u32[]{:S(2)}, u32[]{:S(2)}) %collective-permute-start.31) | collective-permute-done | bytes 1048608 | tf_op jit(solution)/shard_map/ppermute | solution.py:75
  611.8 23.4 %attend_back.2 = (bf16[1024,1024]{1,0:T(8,128)(2,1)S(1)}, bf16[1024,512]{1,0:T(8,128)(2,1)S(1)}, bf16[1024,512]{1,0:T(8,128)(2,1)S(1)}) custom-call(s32[1,1]{1,0:T(1,128)} %bitcast.347.len_ref, bf16[1024,1024]{1,0:T(8,128)(2,1)S(1)} %copy-done.25, bf16[1024,512]{1,0:T(8,128)(2,1)S(1)} %copy-done.29, bf16[1024,512]{1,0:T(8,128)(2,1)S(1)} %copy-done.33, ...), custom_call_target="tpu_custom_call" | custom-call | flops 24000000000 | bytes 8000000 | tf_op jit(solution)/shard_map/attend_back/pallas_call | solution.py:333
  651.5 23.0 %attend_back.3 = (bf16[1024,1024]{1,0:T(8,128)(2,1)S(1)}, bf16[1024,512]{1,0:T(8,128)(2,1)S(1)}, bf16[1024,512]{1,0:T(8,128)(2,1)S(1)}) custom-call(s32[1,1]{1,0:T(1,128)} %bitcast.348.len_ref, bf16[1024,1024]{1,0:T(8,128)(2,1)S(1)} %copy-done.26, bf16[1024,512]{1,0:T(8,128)(2,1)S(1)} %copy-done.30, ...), custom_call_target="tpu_custom_call", output_to_operand_aliasing={{0}: (8, {}), {1}: (9, {}), {2}: (10, {})} | custom-call | flops 24000000000 | bytes 8000000 | tf_op jit(solution)/shard_map/attend_back/pallas_call | solution.py:333
  743.6 8.0 collective-permute-done.45
  751.6 10.8 collective-permute-done.46
  781.7 11.3 %collective-permute-done.54 = f32[512,512]{1,0:T(8,128)S(1)} collective-permute-done((f32[512,512]{1,0:T(8,128)S(1)}, f32[512,512]{1,0:T(8,128)S(1)}, u32[]{:S(2)}, u32[]{:S(2)}) %collective-permute-start.54) | collective-permute-done | bytes 1048608 | tf_op jit(solution)/shard_map/ppermute | solution.py:75
  846.7 12.7 %all-to-all-done.1 = bf16[4,128,1024]{2,1,0:T(8,128)(2,1)} async-done(((bf16[4,128,1024]{2,1,0:T(8,128)(2,1)}), bf16[4,128,1024]{2,1,0:T(8,128)(2,1)}, u32[]{:S(2)}, u32[]{:S(2)}) %all-to-all-start.1) | async-done | bytes 1048608 | tf_op jit(solution)/shard_map/all_to_all | solution.py:711
  942.3 9.6 fusion.34
  951.9 8.2 fusion.36
  975.5 8.1 fusion.37
  1030.4 8.2 multiply_add_fusion
  1046.0 8.0 fusion.40
  1071.0 10.9 all-to-all-done.3
  (599 shorter events, 506.1 us)
Async XLA Ops:
  7.2 123.7 %all-gather.2.cloned.1.call-start = ((), (), s32[]{:S(2)}) async-start(), calls=%async_computation.4 | async-start | bytes 6758400 | tf_op jit(solution)/shard_map/all_gather | solution.py:657
  15.4 69.6 %collective-permute-start = (bf16[2,512,512]{2,1,0:T(8,128)(2,1)}, bf16[2,512,512]{2,1,0:T(8,128)(2,1)}, u32[]{:S(2)}, u32[]{:S(2)}) collective-permute-start(bf16[2,512,512]{2,1,0:T(8,128)(2,1)} %get-tuple-element.272), channel_id=1, source_target_pairs={{0,2},{1,3},{2,0},{3,1},{4,6},{5,7},{6,4},{7,5},{8,10},{9,11},{10,... | collective-permute-start | bytes 3145736 | tf_op jit(solution)/shard_map/ppermute | solution.py:75
  20.4 134.6 %all-to-all-start = ((f32[4,32,1024]{2,1,0:T(8,128)}), f32[4,32,1024]{2,1,0:T(8,128)S(1)}, u32[]{:S(2)}, u32[]{:S(2)}) async-start(f32[4,32,1024]{2,1,0:T(8,128)} %pad_maximum_fusion.15), calls=%async_computation | async-start | bytes 1048576 | tf_op jit(solution)/shard_map/all_to_all | solution.py:711
  133.9 64.8 %collective-permute-start.2 = (bf16[2,2,512,512]{3,2,1,0:T(8,128)(2,1)}, bf16[2,2,512,512]{3,2,1,0:T(8,128)(2,1)}, u32[]{:S(2)}, u32[]{:S(2)}) collective-permute-start(bf16[2,2,512,512]{3,2,1,0:T(8,128)(2,1)} %copy.221.refs_4_), channel_id=1, source_target_pairs={{0,1},{1,0},{2,3},{3,2},{4,5},{5,4},{6,7},{7,6},{8,9},{9,8},{10,11... | collective-permute-start | bytes 6291464 | tf_op jit(solution)/shard_map/ppermute | solution.py:75
  154.2 83.8 %collective-permute-start.7 = (bf16[1024,1024]{1,0:T(8,128)(2,1)}, bf16[1024,1024]{1,0:T(8,128)(2,1)}, u32[]{:S(2)}, u32[]{:S(2)}) collective-permute-start(bf16[1024,1024]{1,0:T(8,128)(2,1)} %maximum_select_fusion.3), channel_id=1, source_target_pairs={{0,4},{1,5},{2,6},{3,7},{4,0},{5,1},{6,2},{7,3},{8,12},{9,13},{10,... | collective-permute-start | bytes 6291464 | tf_op jit(solution)/shard_map/ppermute | solution.py:75
  241.3 79.2 %collective-permute-start.13 = (bf16[1,2,512,512]{3,2,1,0:T(8,128)(2,1)}, bf16[1,2,512,512]{3,2,1,0:T(8,128)(2,1)}, u32[]{:S(2)}, u32[]{:S(2)}) collective-permute-start(bf16[1,2,512,512]{3,2,1,0:T(8,128)(2,1)} %collective-permute-done.10.refs_9_.refs_6_), channel_id=1, source_target_pairs={{0,1},{1,0},{2,3},{3,2},{4,5},{5,4},{6,7},{7,6},{8,9},{9,8},{10,11... | collective-permute-start | bytes 3145736 | tf_op jit(solution)/shard_map/ppermute | solution.py:75
  243.5 79.0 %collective-permute-start.17 = (bf16[1,2,512,512]{3,2,1,0:T(8,128)(2,1)}, bf16[1,2,512,512]{3,2,1,0:T(8,128)(2,1)}, u32[]{:S(2)}, u32[]{:S(2)}) collective-permute-start(bf16[1,2,512,512]{3,2,1,0:T(8,128)(2,1)} %collective-permute-done.10.refs_9_.refs_6_), channel_id=1, source_target_pairs={{0,16},{1,17},{2,18},{3,19},{4,20},{5,21},{6,22},{7,23},{8,24},{9,... | collective-permute-start | bytes 3145736 | tf_op jit(solution)/shard_map/ppermute | solution.py:75
  244.0 77.0 %collective-permute-start.18 = (bf16[1,2,512,512]{3,2,1,0:T(8,128)(2,1)}, bf16[1,2,512,512]{3,2,1,0:T(8,128)(2,1)}, u32[]{:S(2)}, u32[]{:S(2)}) collective-permute-start(bf16[1,2,512,512]{3,2,1,0:T(8,128)(2,1)} %collective-permute-done.11.refs_11_.refs_6_), channel_id=1, source_target_pairs={{0,1},{1,0},{2,3},{3,2},{4,5},{5,4},{6,7},{7,6},{8,9},{9,8},{10,11... | collective-permute-start | bytes 3145736 | tf_op jit(solution)/shard_map/ppermute | solution.py:75
  322.5 71.3 %collective-permute-start.21 = (bf16[2,1024,1024]{2,1,0:T(8,128)(2,1)}, bf16[2,1024,1024]{2,1,0:T(8,128)(2,1)}, u32[]{:S(2)}, u32[]{:S(2)}) collective-permute-start(bf16[2,1024,1024]{2,1,0:T(8,128)(2,1)} %get-tuple-element.90), channel_id=1, source_target_pairs={{0,4},{1,5},{2,6},{3,7},{4,0},{5,1},{6,2},{7,3},{8,12},{9,13},{10,... | collective-permute-start | bytes 12582920 | tf_op jit(solution)/shard_map/ppermute | solution.py:75
  322.6 71.3 %collective-permute-start.20 = (bf16[3,2,512,512]{3,2,1,0:T(8,128)(2,1)}, bf16[3,2,512,512]{3,2,1,0:T(8,128)(2,1)}, u32[]{:S(2)}, u32[]{:S(2)}) collective-permute-start(bf16[3,2,512,512]{3,2,1,0:T(8,128)(2,1)} %get-tuple-element.89), channel_id=1, source_target_pairs={{0,1},{1,0},{2,3},{3,2},{4,5},{5,4},{6,7},{7,6},{8,9},{9,8},{10,11... | collective-permute-start | bytes 9437192 | tf_op jit(solution)/shard_map/ppermute | solution.py:75
  323.7 66.2 %collective-permute-start.16 = (bf16[2,2,512,512]{3,2,1,0:T(8,128)(2,1)S(1)}, bf16[2,2,512,512]{3,2,1,0:T(8,128)(2,1)}, u32[]{:S(2)}, u32[]{:S(2)}) collective-permute-start(bf16[2,2,512,512]{3,2,1,0:T(8,128)(2,1)S(1)} %collective-permute-done.15.refs_5_), channel_id=1, source_target_pairs={{0,8},{1,9},{2,10},{3,11},{4,12},{5,13},{6,14},{7,15},{8,0},{9,1},... | collective-permute-start | bytes 6291464 | tf_op jit(solution)/shard_map/ppermute | solution.py:75
  378.1 82.7 %collective-permute-start.23 = (bf16[2,1024,1024]{2,1,0:T(8,128)(2,1)}, bf16[2,1024,1024]{2,1,0:T(8,128)(2,1)}, u32[]{:S(2)}, u32[]{:S(2)}) collective-permute-start(bf16[2,1024,1024]{2,1,0:T(8,128)(2,1)} %get-tuple-element.93), channel_id=1, source_target_pairs={{0,4},{1,5},{2,6},{3,7},{4,0},{5,1},{6,2},{7,3},{8,12},{9,13},{10,... | collective-permute-start | bytes 12582920 | tf_op jit(solution)/shard_map/ppermute | solution.py:75
  378.4 82.4 %collective-permute-start.22 = (bf16[3,2,512,512]{3,2,1,0:T(8,128)(2,1)}, bf16[3,2,512,512]{3,2,1,0:T(8,128)(2,1)}, u32[]{:S(2)}, u32[]{:S(2)}) collective-permute-start(bf16[3,2,512,512]{3,2,1,0:T(8,128)(2,1)} %get-tuple-element.92), channel_id=1, source_target_pairs={{0,1},{1,0},{2,3},{3,2},{4,5},{5,4},{6,7},{7,6},{8,9},{9,8},{10,11... | collective-permute-start | bytes 9437192 | tf_op jit(solution)/shard_map/ppermute | solution.py:75
  447.5 72.9 %collective-permute-start.26 = (bf16[2,1024,1024]{2,1,0:T(8,128)(2,1)}, bf16[2,1024,1024]{2,1,0:T(8,128)(2,1)}, u32[]{:S(2)}, u32[]{:S(2)}) collective-permute-start(bf16[2,1024,1024]{2,1,0:T(8,128)(2,1)} %get-tuple-element.100), channel_id=1, source_target_pairs={{0,4},{1,5},{2,6},{3,7},{4,0},{5,1},{6,2},{7,3},{8,12},{9,13},{10,... | collective-permute-start | bytes 12582920 | tf_op jit(solution)/shard_map/ppermute | solution.py:75
  447.6 72.8 %collective-permute-start.24 = (bf16[3,2,512,512]{3,2,1,0:T(8,128)(2,1)}, bf16[3,2,512,512]{3,2,1,0:T(8,128)(2,1)}, u32[]{:S(2)}, u32[]{:S(2)}) collective-permute-start(bf16[3,2,512,512]{3,2,1,0:T(8,128)(2,1)} %get-tuple-element.98), channel_id=1, source_target_pairs={{0,8},{1,9},{2,10},{3,11},{4,12},{5,13},{6,14},{7,15},{8,0},{9,1},... | collective-permute-start | bytes 9437192 | tf_op jit(solution)/shard_map/ppermute | solution.py:75
  448.1 72.2 %collective-permute-start.25 = (bf16[3,2,512,512]{3,2,1,0:T(8,128)(2,1)}, bf16[3,2,512,512]{3,2,1,0:T(8,128)(2,1)}, u32[]{:S(2)}, u32[]{:S(2)}) collective-permute-start(bf16[3,2,512,512]{3,2,1,0:T(8,128)(2,1)} %get-tuple-element.99), channel_id=1, source_target_pairs={{0,16},{1,17},{2,18},{3,19},{4,20},{5,21},{6,22},{7,23},{8,24},{9,... | collective-permute-start | bytes 9437192 | tf_op jit(solution)/shard_map/ppermute | solution.py:75
  529.2 111.5 %collective-permute-start.32 = (bf16[3,2,512,512]{3,2,1,0:T(8,128)(2,1)}, bf16[3,2,512,512]{3,2,1,0:T(8,128)(2,1)}, u32[]{:S(2)}, u32[]{:S(2)}) collective-permute-start(bf16[3,2,512,512]{3,2,1,0:T(8,128)(2,1)} %add_convert_fusion), channel_id=1, source_target_pairs={{0,8},{1,9},{2,10},{3,11},{4,12},{5,13},{6,14},{7,15},{8,0},{9,1},... | collective-permute-start | bytes 9437192 | tf_op jit(solution)/shard_map/ppermute | solution.py:75
  536.4 68.3 %collective-permute-start.31 = (bf16[2,512,512]{2,1,0:T(8,128)(2,1)}, bf16[2,512,512]{2,1,0:T(8,128)(2,1)}, u32[]{:S(2)}, u32[]{:S(2)}) collective-permute-start(bf16[2,512,512]{2,1,0:T(8,128)(2,1)} %get-tuple-element.253), channel_id=1, source_target_pairs={{0,1},{1,0},{2,3},{3,2},{4,5},{5,4},{6,7},{7,6},{8,9},{9,8},{10,11... | collective-permute-start | bytes 3145736 | tf_op jit(solution)/shard_map/ppermute | solution.py:75
  609.7 85.8 %collective-permute-start.33 = (bf16[2,512,512]{2,1,0:T(8,128)(2,1)}, bf16[2,512,512]{2,1,0:T(8,128)(2,1)}, u32[]{:S(2)}, u32[]{:S(2)}) collective-permute-start(bf16[2,512,512]{2,1,0:T(8,128)(2,1)} %get-tuple-element.265), channel_id=1, source_target_pairs={{0,16},{1,17},{2,18},{3,19},{4,20},{5,21},{6,22},{7,23},{8,24},{9,... | collective-permute-start | bytes 3145736 | tf_op jit(solution)/shard_map/ppermute | solution.py:75
  610.2 85.4 %collective-permute-start.34 = (bf16[2,512,512]{2,1,0:T(8,128)(2,1)}, bf16[2,512,512]{2,1,0:T(8,128)(2,1)}, u32[]{:S(2)}, u32[]{:S(2)}) collective-permute-start(bf16[2,512,512]{2,1,0:T(8,128)(2,1)} %get-tuple-element.264), channel_id=1, source_target_pairs={{0,16},{1,17},{2,18},{3,19},{4,20},{5,21},{6,22},{7,23},{8,24},{9,... | collective-permute-start | bytes 3145736 | tf_op jit(solution)/shard_map/ppermute | solution.py:75
  705.9 66.7 %collective-permute-start.36 = (bf16[4,128,1024]{2,1,0:T(8,128)(2,1)}, bf16[4,128,1024]{2,1,0:T(8,128)(2,1)}, u32[]{:S(2)}, u32[]{:S(2)}) collective-permute-start(bf16[4,128,1024]{2,1,0:T(8,128)(2,1)} %dynamic-slice_bitcast_fusion.2), channel_id=1, source_target_pairs={{0,4},{1,5},{2,6},{3,7},{4,0},{5,1},{6,2},{7,3},{8,12},{9,13},{10,... | collective-permute-start | bytes 3145736 | tf_op jit(solution)/shard_map/ppermute | solution.py:75
  706.9 68.5 %collective-permute-start.42 = (bf16[4,128,1024]{2,1,0:T(8,128)(2,1)}, bf16[4,128,1024]{2,1,0:T(8,128)(2,1)}, u32[]{:S(2)}, u32[]{:S(2)}) collective-permute-start(bf16[4,128,1024]{2,1,0:T(8,128)(2,1)} %dynamic-slice_bitcast_fusion.1), channel_id=1, source_target_pairs={{0,4},{1,5},{2,6},{3,7},{4,0},{5,1},{6,2},{7,3},{8,12},{9,13},{10,... | collective-permute-start | bytes 3145736 | tf_op jit(solution)/shard_map/ppermute | solution.py:75
  772.6 64.6 %collective-permute-start.56 = (f32[512,512]{1,0:T(8,128)}, f32[512,512]{1,0:T(8,128)}, u32[]{:S(2)}, u32[]{:S(2)}) collective-permute-start(f32[512,512]{1,0:T(8,128)} %get-tuple-element.261), channel_id=1, source_target_pairs={{0,1},{1,0},{2,3},{3,2},{4,5},{5,4},{6,7},{7,6},{8,9},{9,8},{10,11... | collective-permute-start | bytes 3145736 | tf_op jit(solution)/shard_map/ppermute | solution.py:75
  886.7 175.7 %all-to-all-start.2 = ((f32[4,32,1024]{2,1,0:T(8,128)}), f32[4,32,1024]{2,1,0:T(8,128)}, u32[]{:S(2)}, u32[]{:S(2)}) async-start(f32[4,32,1024]{2,1,0:T(8,128)} %multiply_add_fusion.6), calls=%async_computation.2 | async-start | bytes 1048576 | tf_op jit(solution)/shard_map/all_to_all | solution.py:711
  (164 other events, 2685.7 us)
Sparse Core Ops, SparseCore 0:
  11.4 116.9 all-gather.1

commit v2 on v1

--- a/solution.py
+++ b/solution.py
@@ -377,17 +377,22 @@
 
 
 def expert_kernel(waits, first, *refs):
-    n2_ref, n2t_ref, dy_ref, gate_ref = refs[:4]
-    wb_own_ref, wb_other_ref, wg_own_ref, wg_other_ref = refs[4:8]
-    outs = refs[8 + waits :]
+    n2_ref, dy_ref, gate_ref = refs[:3]
+    wg_own_ref, wg_other_ref, wb_own_ref, wb_other_ref = refs[3:7]
+    outs = refs[7 + waits :]
     own_ref, pair_ref, dgate_ref, grad_own_ref, grad_other_ref = outs[:5]
-    m_acc, dn_acc, g_acc, u_acc, d_acc = outs[5:]
+    m_acc, dn_acc, g_acc, u_acc, d_acc, turned_ref = outs[5:]
     step = pl.program_id(0)
     block = pl.program_id(1)
     blocks = pl.num_programs(1)
     rows = n2_ref.shape[0]
     place = pl.ds(pl.multiple_of(block * rows, rows), rows)
     lane = lax.broadcasted_iota(jnp.int32, (rows, PACK), 1)
+
+    @pl.when(step == 0)
+    def _():
+        turned_ref[:, place] = n2_ref[...].T
+
     wg_own, wg_other = wg_own_ref[0, 0], wg_other_ref[0, 0]
     wu_own, wu_other = wb_own_ref[0, 0], wb_other_ref[0, 0]
     wd_own, wd_other = wb_own_ref[1, 0], wb_other_ref[1, 0]
@@ -405,7 +410,7 @@
     duu = (dh * silu).astype(jnp.bfloat16)
     y_own = dot_nt(hidden, wd_own)
     y_other = dot_nt(hidden, wd_other)
-    n2t = n2t_ref[...]
+    n2t = turned_ref[:, place]
     g_acc[...] = jnp.where(block == 0, 0.0, g_acc[...]) + dot_nn(n2t, dug)
     dgate = jnp.sum(dm[:, :HALF] * y_own, axis=1, keepdims=True) + jnp.sum(
         dm[:, HALF:] * y_other, axis=1, keepdims=True
@@ -447,7 +452,7 @@
         grad_other_ref[2, 0] = d_acc[:, HALF:].astype(jnp.bfloat16)
 
 
-def expert_call(first, n2, n2t, dy, gates, weights, done):
+def expert_call(first, n2, dy, gates, weights, done):
     tokens_all = n2.shape[0]
     rows = min(512, tokens_all // 2)
     half_blocks = tokens_all // rows // 2
@@ -471,13 +476,12 @@
         grid=(steps, 2 * half_blocks),
         in_specs=[
             pl.BlockSpec((rows, D), lambda s, b: (b, 0)),
-            pl.BlockSpec((D, rows), lambda s, b: (0, b)),
             pl.BlockSpec((rows, D), lambda s, b: (b, 0)),
             pl.BlockSpec((rows, PACK), lambda s, b: (b, 0)),
+            pieces(1),
+            pieces(1),
             pieces(2),
             pieces(2),
-            pieces(1),
-            pieces(1),
         ]
         + [pl.BlockSpec(memory_space=pl.ANY)] * len(done),
         out_specs=[
@@ -500,9 +504,10 @@
             pltpu.VMEM((D, FF), jnp.float32),
             pltpu.VMEM((D, FF), jnp.float32),
             pltpu.VMEM((FF, D), jnp.float32),
+            pltpu.VMEM((D, tokens_all), low),
         ],
         compiler_params=pltpu.CompilerParams(
-            dimension_semantics=("arbitrary", "arbitrary"), vmem_limit_bytes=60 * 1024 * 1024
+            dimension_semantics=("arbitrary", "arbitrary"), vmem_limit_bytes=62 * 1024 * 1024
         ),
         cost_estimate=pl.CostEstimate(
             flops=9 * 2 * tokens_all * D * FF * steps * 3 // 2,
@@ -510,49 +515,204 @@
             transcendentals=steps * tokens_all * FF,
         ),
         name="experts",
-    )(n2, n2t, dy, gates, *weights, *done)
+    )(n2, dy, gates, *weights, *done)
     return outputs
 
 
-def high_dot(left_side, right_side):
-    return jnp.matmul(left_side, right_side, precision=lax.Precision.HIGH)
-
-
-def gram_of(rows):
-    return jnp.einsum("...oe,...ol->...el", rows, rows, precision=lax.Precision.HIGH)
-
-
-def polynomial(gram):
-    eye = jnp.eye(gram.shape[-1], dtype=jnp.float32)
-    return POLY_ONE * eye + POLY_TWO * gram + POLY_THREE * high_dot(gram, gram)
-
-
-def ortho_rows(own_rows, all_rows):
-    squares = jnp.sum(all_rows * all_rows, axis=(-2, -1), keepdims=True)
-    scale = 1.0 / (jnp.sqrt(squares) + ORTHO_EPS)
-    gram = gram_of(all_rows * scale)
-    product = None
-    for iteration in range(5):
-        factor = polynomial(gram)
-        product = factor if product is None else high_dot(product, factor)
-        if iteration < 4:
-            gram = high_dot(high_dot(gram, factor), factor)
-    return high_dot(own_rows * scale, product)
-
-
-def ortho_block(block, gram_mask, halves):
-    squares = jnp.sum(block * block, axis=0)
-    width = squares.shape[0] // 2
-    lower, upper = jnp.sum(squares[:width]), jnp.sum(squares[width:])
-    column = jnp.arange(squares.shape[0])
-    own = jnp.where(column < width, lower, upper)
-    scale = 1.0 / (jnp.sqrt(jnp.where(halves, own, lower + upper)) + ORTHO_EPS)
-    iterate = block * scale[None, :]
-    for iteration in range(5):
-        gram = gram_of(iterate) * gram_mask
-        change = POLY_TWO * gram + POLY_THREE * high_dot(gram, gram)
-        iterate = POLY_ONE * iterate + high_dot(iterate, change)
-    return iterate
+def split_high(values):
+    high = values.astype(jnp.bfloat16)
+    return high, (values - high.astype(jnp.float32)).astype(jnp.bfloat16)
+
+
+def triple_dot(left_side, right_side):
+    left_high, left_low = left_side
+    right_high, right_low = right_side
+    return dot_nn(left_high, right_high) + (
+        dot_nn(left_high, right_low) + dot_nn(left_low, right_high)
+    )
+
+
+def symmetric_product(left_pair, right_pair, size, put):
+    tile = min(256, size)
+    for first in range(0, size, tile):
+        rows = slice(first, first + tile)
+        part = triple_dot(
+            tuple(side[rows, :] for side in left_pair),
+            tuple(side[:, first:] for side in right_pair),
+        )
+        put(rows, slice(first, size), part)
+        for second in range(first + tile, size, tile):
+            columns = slice(second, second + tile)
+            put(columns, rows, part[:, second - first : second - first + tile].T)
+
+
+def store_pair(pair, rows, columns, values):
+    high, low = split_high(values)
+    pair[0][rows, columns] = high
+    pair[1][rows, columns] = low
+
+
+def ortho_block_kernel(halves_ref, m_ref, x_ref, xh, xl, th, tl, gram, gh, gl, sh, sl):
+    size = m_ref.shape[0]
+    tile = 256
+    halves = halves_ref[0] == 1
+    half = size // 2
+
+    def square_sum(columns):
+        total = jnp.zeros((1, half), jnp.float32)
+        for first in range(0, size, tile):
+            piece = m_ref[first : first + tile, columns]
+            total = total + jnp.sum(piece * piece, axis=0, keepdims=True)
+        return jnp.sum(total)
+
+    lower, upper = square_sum(slice(0, half)), square_sum(slice(half, size))
+    whole = lower + upper
+
+    def scale_of(own):
+        squares = jnp.full((1, half), jnp.where(halves, own, whole), jnp.float32)
+        return 1.0 / (jnp.sqrt(squares) + ORTHO_EPS)
+
+    for columns, own in ((slice(0, half), lower), (slice(half, size), upper)):
+        scale = scale_of(own)
+        for first in range(0, size, tile):
+            rows = slice(first, first + tile)
+            x_ref[rows, columns] = m_ref[rows, columns] * scale
+
+    def mask(rows, columns, values):
+        row = rows.start + lax.broadcasted_iota(jnp.int32, values.shape, 0)
+        column = columns.start + lax.broadcasted_iota(jnp.int32, values.shape, 1)
+        return jnp.where(((row < half) != (column < half)) & halves, 0.0, values)
+
+    def put_gram(rows, columns, values):
+        values = mask(rows, columns, values)
+        gram[rows, columns] = values
+        store_pair((gh, gl), rows, columns, values)
+
+    def put_change(rows, columns, values):
+        values = POLY_TWO * gram[rows, columns] + POLY_THREE * values
+        store_pair((sh, sl), rows, columns, values)
+
+    def iterate(iteration, carry):
+        for first in range(0, size, tile):
+            rows = slice(first, first + tile)
+            high, low = split_high(x_ref[rows, :])
+            xh[rows, :] = high
+            xl[rows, :] = low
+            th[:, rows] = high.T
+            tl[:, rows] = low.T
+        symmetric_product((th, tl), (xh, xl), size, put_gram)
+        symmetric_product((gh, gl), (gh, gl), size, put_change)
+        for first in range(0, size, tile):
+            rows = slice(first, first + tile)
+            change = triple_dot((xh[rows, :], xl[rows, :]), (sh[...], sl[...]))
+            x_ref[rows, :] = POLY_ONE * x_ref[rows, :] + change
+        return carry
+
+    lax.fori_loop(0, 5, iterate, 0)
+
+
+def ortho_block_call(block, halves):
+    size = block.shape[0]
+    low = pltpu.VMEM((size, size), jnp.bfloat16)
+    return pl.pallas_call(
+        ortho_block_kernel,
+        in_specs=[
+            pl.BlockSpec(memory_space=pltpu.SMEM),
+            pl.BlockSpec(memory_space=pltpu.VMEM),
+        ],
+        out_specs=pl.BlockSpec(memory_space=pltpu.VMEM),
+        out_shape=jax.ShapeDtypeStruct((size, size), jnp.float32),
+        scratch_shapes=[low] * 4 + [pltpu.VMEM((size, size), jnp.float32)] + [low] * 4,
+        compiler_params=pltpu.CompilerParams(vmem_limit_bytes=56 * 1024 * 1024),
+        cost_estimate=pl.CostEstimate(
+            flops=5 * 9 * 2 * size**3, bytes_accessed=8 * size * size, transcendentals=0
+        ),
+        name="ortho_block",
+    )(halves.reshape(1), block)
+
+
+def ortho_rows_kernel(m_ref, o_ref, xh, xl, th, tl, gram, pair_g, pair_p, pair_t, product, pair_q):
+    rows_all, size = m_ref.shape[1:]
+    own = o_ref.shape[1]
+    tile = 256
+    squares = jnp.zeros((1, size), jnp.float32)
+    for first in range(0, rows_all, tile):
+        piece = m_ref[0, first : first + tile, :]
+        squares = squares + jnp.sum(piece * piece, axis=0, keepdims=True)
+    total = jnp.full((1, size), jnp.sum(squares), jnp.float32)
+    scale = 1.0 / (jnp.sqrt(total) + ORTHO_EPS)
+    for first in range(0, rows_all, tile):
+        rows = slice(first, first + tile)
+        high, low = split_high(m_ref[0, rows, :] * scale)
+        xh[rows, :] = high
+        xl[rows, :] = low
+        th[:, rows] = high.T
+        tl[:, rows] = low.T
+    pair_g, pair_p, pair_t, pair_q = [
+        (pair.at[0], pair.at[1]) for pair in (pair_g, pair_p, pair_t, pair_q)
+    ]
+
+    def put_gram(rows, columns, values):
+        gram[rows, columns] = values
+        store_pair(pair_g, rows, columns, values)
+
+    def put_factor(rows, columns, values):
+        row = rows.start + lax.broadcasted_iota(jnp.int32, values.shape, 0)
+        column = columns.start + lax.broadcasted_iota(jnp.int32, values.shape, 1)
+        values = POLY_TWO * gram[rows, columns] + POLY_THREE * values
+        values = values + jnp.where(row == column, POLY_ONE, 0.0)
+        product[rows, columns] = values
+        store_pair(pair_p, rows, columns, values)
+
+    def put_turn(rows, columns, values):
+        store_pair(pair_t, rows, columns, values)
+
+    def put_product(rows, columns, values):
+        product[rows, columns] = values
+
+    def keep_product():
+        for first in range(0, size, tile):
+            rows = slice(first, first + tile)
+            store_pair(pair_q, rows, slice(0, size), product[rows, :])
+
+    symmetric_product((th, tl), (xh, xl), size, put_gram)
+    symmetric_product(pair_g, pair_g, size, put_factor)
+    keep_product()
+
+    def iterate(iteration, carry):
+        symmetric_product(pair_g, pair_p, size, put_turn)
+        symmetric_product(pair_t, pair_p, size, put_gram)
+        symmetric_product(pair_g, pair_g, size, put_factor)
+        symmetric_product(pair_q, pair_p, size, put_product)
+        keep_product()
+        return carry
+
+    lax.fori_loop(0, 4, iterate, 0)
+    o_ref[0] = triple_dot((xh[:own, :], xl[:own, :]), (pair_q[0][...], pair_q[1][...]))
+
+
+def ortho_rows_call(group_rows, own_rows):
+    kinds, rows_all, size = group_rows.shape
+    low = jnp.bfloat16
+    pair = pltpu.VMEM((2, size, size), low)
+    square = pltpu.VMEM((size, size), jnp.float32)
+    return pl.pallas_call(
+        ortho_rows_kernel,
+        grid=(kinds,),
+        in_specs=[pl.BlockSpec((1, rows_all, size), lambda k: (k, 0, 0))],
+        out_specs=pl.BlockSpec((1, own_rows, size), lambda k: (k, 0, 0)),
+        out_shape=jax.ShapeDtypeStruct((kinds, own_rows, size), jnp.float32),
+        scratch_shapes=[pltpu.VMEM((rows_all, size), low)] * 2
+        + [pltpu.VMEM((size, rows_all), low)] * 2
+        + [square, pair, pair, pair, square, pair],
+        compiler_params=pltpu.CompilerParams(
+            dimension_semantics=("arbitrary",), vmem_limit_bytes=40 * 1024 * 1024
+        ),
+        cost_estimate=pl.CostEstimate(
+            flops=kinds * 60 * 2 * size**3, bytes_accessed=16 * size * size, transcendentals=0
+        ),
+        name="ortho_rows",
+    )(group_rows)
 
 
 def take_half(values, axis, own):
@@ -666,8 +826,8 @@
     own_half = gather_rows(expert_weight.astype(jnp.bfloat16), 1, count, place, early_bits)
     level_one = (((1, 0, 0), half_bit), ((0, 1, 0), bit_x), ((0, 0, 1), bit_y))
     gather_last = (
+        {(1, 1, 0): half_bit, (0, 1, 1): bit_y, (1, 0, 1): half_bit, (1, 1, 1): bit_x},
         {(1, 1, 0): bit_x, (0, 1, 1): bit_y, (1, 0, 1): bit_y, (1, 1, 1): bit_x},
-        {(1, 1, 0): half_bit, (0, 1, 1): bit_y, (1, 0, 1): half_bit, (1, 1, 1): bit_x},
     )
     hop_of = {half_bit: 0, bit_x: 1, bit_y: 2}
 
@@ -678,12 +838,11 @@
 
     chunks = [{}, {}]
     before = None
-    for part, kinds in enumerate((slice(1, 3), slice(0, 1))):
+    for part, kinds in enumerate((slice(0, 1), slice(1, 3))):
         own = own_half[kinds]
-        if before is not None:
-            own = after(own, before)
+        own = after(own, full_packed if before is None else before)
         before = swap_bit(own, count, bit_z)
-        chunks[part][0, 0, 0] = after(jnp.stack([own, before], axis=1), full_packed)
+        chunks[part][0, 0, 0] = jnp.stack([own, before], axis=1)
         for chunk, bit in level_one:
             chunks[part][chunk] = swap_bit(chunks[part][0, 0, 0], count, bit)
     for chunk in ((1, 1, 0), (0, 1, 1), (1, 0, 1), (1, 1, 1)):
@@ -723,10 +882,10 @@
         key_rows,
         value_rows,
         seq_len,
-        [chunks[1][0, 0, 0], old_tasks],
+        [chunks[0][0, 0, 0], old_tasks],
     )
     branch = plain_dot(attended, w_out, 1, 1)
-    branch = after(branch, *[chunks[0][chunk] for chunk, _ in level_one])
+    branch = after(branch, chunks[1][0, 0, 0], *[chunks[0][chunk] for chunk, _ in level_one])
     hidden_state = inputs + RESID_MULT * branch
     scale_two = lax.rsqrt(jnp.mean(hidden_state * hidden_state, axis=-1, keepdims=True) + NORM_EPS)
     unit_two = hidden_state * scale_two
@@ -746,8 +905,6 @@
     gates_there = jnp.pad(gate_weights[:, 8:], ((0, 0), (0, PACK - 8)))
     other_gates = swap_bit(gates_there, count, pair_bit)
     both_second = jnp.concatenate([second, other_second])
-    turned = second.T
-    both_turned = jnp.concatenate([turned, swap_bit(turned, count, pair_bit)], axis=1)
     both_gates = jnp.concatenate([gates_here, other_gates])
     own_parts, pair_parts, dgates = [], [], []
     grads, moved = {}, {}
@@ -767,7 +924,6 @@
         own_part, pair_part, dgate, grad_own, grad_other = expert_call(
             2 * turn_index,
             both_second,
-            both_turned,
             both_grad,
             both_gates,
             weights,
@@ -849,10 +1005,6 @@
     grad_attended = jnp.dot(grad_branch, w_out, preferred_element_type=jnp.float32).astype(
         jnp.bfloat16
     )
-    last_own = after(grads[0, 0, 1], grad_attended)
-    from_y = [
-        swap_bit(total_of(last_own[kind], half_y[kind]), count, bit_y) for kind in range(3)
-    ]
     def attend_back(part, held, done):
         return attend_back_call(
             part,
@@ -868,8 +1020,13 @@
             done,
         )
 
+    first_heads = attend_back(0, [], [])
+    last_own, half_y, _ = lax.optimization_barrier((grads[0, 0, 1], half_y, first_heads[0]))
+    from_y = [
+        swap_bit(total_of(last_own[kind], half_y[kind]), count, bit_y) for kind in range(3)
+    ]
     grad_query, grad_key, grad_value = attend_back(
-        1, attend_back(0, [], half_y), [moved[0, 1, 0]]
+        1, first_heads, half_y + [moved[0, 1, 0]]
     )
     late_parts = after(tuple(own_parts + pair_parts), grad_query)
     block_out = (hidden_state + RESID_MULT * gather_sum([part[0] for part in late_parts])).astype(
@@ -879,7 +1036,7 @@
         pin(plain_dot(normed_one, piece, 0, 0).astype(jnp.bfloat16))
         for piece in (grad_query, grad_key, grad_value)
     ]
-    nearest = after(grads[0, 0, 0], low_grad[0])
+    nearest, from_y, _ = lax.optimization_barrier((grads[0, 0, 0], from_y, low_grad[0]))
     expert_sums = [
         total_of(nearest[kind], moved[1, 0, 0][kind], moved[0, 1, 0][kind], from_y[kind])
         for kind in range(3)
@@ -902,9 +1059,11 @@
         ],
         axis=1,
     ).astype(jnp.bfloat16)
-    query_sum = to_dp(low_grad[0], first_x)
+    wide_sum = to_dp(
+        jnp.concatenate([low_grad[0], after(low_grad_out, grad_query)], axis=1), first_x
+    )
+    query_sum, out_sum = wide_sum[:, :query_width], wide_sum[:, query_width:]
     shared_sum = to_dp(jnp.concatenate([low_grad[1], low_grad[2], pin(grad_small)], axis=1), first_y)
-    out_sum = to_dp(after(low_grad_out, grad_query), first_x)
 
     def as_tasks(first, second, third, small):
         small = jnp.pad(small, ((0, 0), (0, block_width - PACK)))
@@ -928,32 +1087,28 @@
         gather_from_owners(task_block[:, : block_width // 2], count, place, wide_x),
         gather_from_owners(task_block[:, block_width // 2 :], count, place, wide_y),
     ]
-    moment_expert, ortho_expert = [], []
+    attn_block = jnp.concatenate(
+        [gather_from_owners(side, count, place, [pair_bit], wide_x) for side in sides], axis=1
+    )
+    moment_expert, group_rows = [], []
     for kind in range(3):
-        total = expert_sums[kind]
-        total = total[0].astype(jnp.float32) + swap_bit(total[1], count, bit_z).astype(jnp.float32)
+        total = after(expert_sums[kind], wide_sum, shared_sum)
+        from_z = after(swap_bit(expert_sums[kind][1], count, bit_z), wide_sum, shared_sum)
+        total = total[0].astype(jnp.float32) + from_z.astype(jnp.float32)
         total = total.T if kind == 2 else total
         if early_bits:
             total = reduce_rows(total.astype(jnp.bfloat16), count, place, early_bits[::-1])
         moment = MOMENTUM * expert_moment[kind] + total.astype(jnp.float32)
-        group_rows = moment
-        for bit in low_bits:
-            group_rows = jnp.concatenate([group_rows, swap_bit(group_rows, count, bit)])
-        if kind == 1:
-            group_rows = after(group_rows, task_block)
-        if kind == 2:
-            group_rows = after(group_rows, *sides)
+        rows = pin(moment)
+        for bit in low_bits[:-1]:
+            rows = jnp.concatenate([rows, swap_bit(rows, count, bit)])
         moment_expert.append(moment)
-        ortho_expert.append(ortho_rows(moment, group_rows))
-    attn_block = jnp.concatenate(
-        [gather_from_owners(side, count, place, [pair_bit], wide_x) for side in sides], axis=1
-    )
-    column_half = jnp.arange(block_width) >= block_width // 2
-    halves = lax.axis_index("blk") == 1
-    gram_mask = jnp.where(
-        (column_half[:, None] == column_half[None, :]) | ~halves, 1.0, 0.0
-    ).astype(jnp.float32)
-    attn_iter = ortho_block(attn_block, gram_mask, halves)
+        group_rows.append((rows, swap_bit(rows, count, low_bits[-1])))
+    attn_block = after(attn_block, *moment_expert)
+    attn_iter = ortho_block_call(attn_block, (lax.axis_index("blk") == 1).astype(jnp.int32))
+    group_rows = after(tuple(group_rows), attn_iter)
+    group_rows = jnp.stack([jnp.concatenate(pieces) for pieces in group_rows])
+    ortho_expert = ortho_rows_call(group_rows, own_rows)
     returned = lax.dynamic_slice_in_dim(
         attn_iter, lax.axis_index("dp") * (n_blk * rows_each), n_blk * rows_each, 0
     )
@@ -963,7 +1118,7 @@
     moment_expert = jnp.stack(moment_expert)
     attn_new = muon_update(attn_weight, ortho_attn)
     router_new = muon_update(router_weight, ortho_router)
-    expert_new = muon_update(expert_weight, jnp.stack(ortho_expert))
+    expert_new = muon_update(expert_weight, ortho_expert)
     first_new = BETA_ONE * gain_first + (1.0 - BETA_ONE) * gain_grad
     second_new = BETA_TWO * gain_second + (1.0 - BETA_TWO) * gain_grad * gain_grad
     corrected_first = first_new / (1.0 - BETA_ONE**STEP)

time: 1100 us -> 1000 us (0.909)
  matrix products: 233 us -> 29.5 us
  Pallas kernels: 303 us -> 439 us
  local copies, waits for them, and re-layouts: 100 us -> 74.2 us
    dot_general x72 -> x0, matrix products: 189 us -> none  [the longest x64 142 us: high_dot(): return jnp.matmul(left_side, right_side, precision=lax.Precision.HIGH)]
    pallas_call x0 -> x2, Pallas kernels: none -> 131 us  [the longest x1 80 us: ortho_block_call(): pl.pallas_call(ortho_block_kernel, in_specs=[pl.BlockSpec(memory_space=pl...]
    all_gather x1, waiting for transfers between devices: 0.01 us -> 56.8 us  [shards(): lax.all_gather(jnp.concatenate([attn_low, small_low], axis=1), AXES, axis...]
    ppermute x57 -> x53, waiting for transfers between devices: 217 us -> 176 us  [swap_bit(): return pin(lax.ppermute(pin(values), AXES, pairs))]
    unnamed x262 -> x164, local copies, waits for them, and re-layouts: 46.8 us -> 31.9 us
    all_to_all x4, waiting for transfers between devices: 23.6 us -> 11.3 us  [spread(): lax.all_to_all(values, 'blk', split_axis=0, concat_axis=0, tiled=True)]
    ppermute x57 -> x53, starting transfers between devices: 49.8 us -> 44.7 us  [swap_bit(): return pin(lax.ppermute(pin(values), AXES, pairs))]
  transfers between devices with their start and end apart: 62 -> 58, of which waited for: 17 -> 21; matrix products, arithmetic and copies ran while one was open for 36% -> 19% of each run, Pallas kernels for 28% -> 44%
where the time goes in v2:
time: 1000 us; the launch traced here: 992 us
  Pallas kernels  439 us (44%)
  waiting for transfers between devices  244 us (24%)
  other arithmetic  124 us (12%)
  local copies, waits for them, and re-layouts  74.2 us (7%)
  starting transfers between devices  63.6 us (6%)
  matrix products  29.5 us (3%)
  between operations  16.7 us (2%)
    pallas_call x4, Pallas kernels, expert_call(): pl.pallas_call(functools.partial(expert_kernel, len(done), first), grid=(...  220 us
    ppermute x53, waiting for transfers between devices, swap_bit(): return pin(lax.ppermute(pin(values), AXES, pairs))  176 us
    pallas_call x1, Pallas kernels, ortho_block_call(): pl.pallas_call(ortho_block_kernel, in_specs=[pl.BlockSpec(memory_space=pl...  80 us
    all_gather x1, waiting for transfers between devices, shards(): lax.all_gather(jnp.concatenate([attn_low, small_low], axis=1), AXES, axis...  56.8 us
    pallas_call x1, Pallas kernels, ortho_rows_call(): pl.pallas_call(ortho_rows_kernel, grid=(kinds,), in_specs=[pl.BlockSpec((...  50.5 us
    pallas_call x2, Pallas kernels, attend_back_call(): pl.pallas_call(attend_back_kernel, grid=(seqs, groups), in_specs=[pl.Bloc...  46.9 us
    ppermute x53, starting transfers between devices, swap_bit(): return pin(lax.ppermute(pin(values), AXES, pairs))  44.7 us
    pallas_call x1, Pallas kernels, attend_call(): pl.pallas_call(attend_kernel, grid=(seqs, groups), in_specs=[pl.BlockSpec...  33.6 us
  transfers between devices with their start and end apart: 58, of which 21 were waited for; matrix products, arithmetic and copies ran while one was open for 19% of the time, Pallas kernels for 44%

profile of v2, /device:TPU:0, one launch (start us, length us, event | category | flops | bytes accessed | tf_op | source)
XLA Modules:
  0.0 991.6 jit_solution(9346935086853373004)
XLA Ops:
  13.3 6.3 all-to-all-start
  32.5 56.8 %all-gather.2.cloned.1.call-done.wq_ref.wkv_ref = bf16[1024,3200]{1,0:T(8,128)(2,1)} async-done(((bf16[32,3200]{1,0:T(8,128)(2,1)}), bf16[1024,3200]{1,0:T(8,128)(2,1)}) %all-gather.2.cloned.1.call-update) | async-done | bytes 6553616 | tf_op jit(solution)/shard_map/all_gather | solution.py:817
  95.3 7.8 project.1
  108.6 10.3 %collective-permute-done = bf16[1,512,512]{2,1,0:T(8,128)(2,1)S(1)} collective-permute-done((bf16[1,512,512]{2,1,0:T(8,128)(2,1)}, bf16[1,512,512]{2,1,0:T(8,128)(2,1)S(1)}, u32[]{:S(2)}, u32[]{:S(2)}) %collective-permute-start) | collective-permute-done | bytes 524320 | tf_op jit(solution)/shard_map/ppermute | solution.py:75
  128.4 33.6 %attend.1 = (bf16[1024,1024]{1,0:T(8,128)(2,1)S(1)}, f32[4,8,1024]{2,1,0:T(8,128)S(1)}) custom-call(s32[1,1]{1,0:T(1,128)} %bitcast.224.len_ref, bf16[1024,1024]{1,0:T(8,128)(2,1)S(1)} %copy-done.10, bf16[1024,512]{1,0:T(8,128)(2,1)S(1)} %copy-done.13, bf16[1024,512]{1,0:T(8,128)(2,1)S(1)} %copy-done.16, ...), custom_call_target="tpu_custom_call" | custom-call | flops 20000000000 | bytes 8000000 | tf_op jit(solution)/shard_map/attend/pallas_call | solution.py:234
  198.9 45.2 %collective-permute-done.14.refs_4_ = bf16[1,2,512,512]{3,2,1,0:T(8,128)(2,1)} collective-permute-done((bf16[1,2,512,512]{3,2,1,0:T(8,128)(2,1)}, bf16[1,2,512,512]{3,2,1,0:T(8,128)(2,1)}, u32[]{:S(2)}, u32[]{:S(2)}) %collective-permute-start.14) | collective-permute-done | bytes 1048608 | tf_op jit(solution)/shard_map/ppermute | solution.py:75
  248.2 55.4 %experts.4 = (bf16[2,1024,1024]{2,1,0:T(8,128)(2,1)}, bf16[2,1024,1024]{2,1,0:T(8,128)(2,1)}, f32[2048,128]{1,0:T(8,128)}, bf16[3,2,512,512]{3,2,1,0:T(8,128)(2,1)}, bf16[3,2,512,512]{3,2,1,0:T(8,128)(2,1)}) custom-call(bf16[2048,1024]{1,0:T(8,128)(2,1)} %pad_maximum_fusion.1.refs_0_, bf16[2048,1024]{1,0:T(8,128)(2,1)} %copy-done.48, ...), custom_call_target="tpu_custom_call" | custom-call | flops 57982058496 | bytes 50331648 | tf_op jit(solution)/shard_map/experts/pallas_call | solution.py:474
  309.2 54.8 %experts.5 = (bf16[2,1024,1024]{2,1,0:T(8,128)(2,1)}, bf16[2,1024,1024]{2,1,0:T(8,128)(2,1)}, f32[2048,128]{1,0:T(8,128)}, bf16[3,2,512,512]{3,2,1,0:T(8,128)(2,1)}, bf16[3,2,512,512]{3,2,1,0:T(8,128)(2,1)}) custom-call(bf16[2048,1024]{1,0:T(8,128)(2,1)} %pad_maximum_fusion.1.refs_0_, bf16[2048,1024]{1,0:T(8,128)(2,1)} %copy-done.48, ...), custom_call_target="tpu_custom_call" | custom-call | flops 57982058496 | bytes 50331648 | tf_op jit(solution)/shard_map/experts/pallas_call | solution.py:474
  366.7 8.2 collective-permute-done.19.refs_7_
  375.0 55.1 %experts.6 = (bf16[2,1024,1024]{2,1,0:T(8,128)(2,1)}, bf16[2,1024,1024]{2,1,0:T(8,128)(2,1)}, f32[2048,128]{1,0:T(8,128)}, bf16[3,2,512,512]{3,2,1,0:T(8,128)(2,1)}, bf16[3,2,512,512]{3,2,1,0:T(8,128)(2,1)}) custom-call(bf16[2048,1024]{1,0:T(8,128)(2,1)} %pad_maximum_fusion.1.refs_0_, bf16[2048,1024]{1,0:T(8,128)(2,1)} %copy-done.48, ...), custom_call_target="tpu_custom_call" | custom-call | flops 57982058496 | bytes 50331648 | tf_op jit(solution)/shard_map/experts/pallas_call | solution.py:474
  432.1 9.8 collective-permute-done.21.refs_7_
  441.9 54.9 %experts.7 = (bf16[2,1024,1024]{2,1,0:T(8,128)(2,1)}, bf16[2,1024,1024]{2,1,0:T(8,128)(2,1)}, f32[2048,128]{1,0:T(8,128)}, bf16[3,2,512,512]{3,2,1,0:T(8,128)(2,1)}, bf16[3,2,512,512]{3,2,1,0:T(8,128)(2,1)}) custom-call(bf16[2048,1024]{1,0:T(8,128)(2,1)} %pad_maximum_fusion.1.refs_0_, bf16[2048,1024]{1,0:T(8,128)(2,1)} %copy-done.48, ...), custom_call_target="tpu_custom_call" | custom-call | flops 57982058496 | bytes 50331648 | tf_op jit(solution)/shard_map/experts/pallas_call | solution.py:474
  522.2 7.7 add_bitcast_fusion.1
  541.1 23.1 %attend_back.2 = (bf16[1024,1024]{1,0:T(8,128)(2,1)S(1)}, bf16[1024,512]{1,0:T(8,128)(2,1)S(1)}, bf16[1024,512]{1,0:T(8,128)(2,1)S(1)}) custom-call(s32[1,1]{1,0:T(1,128)} %bitcast.225.len_ref, bf16[1024,1024]{1,0:T(8,128)(2,1)S(1)} %copy-done.11, bf16[1024,512]{1,0:T(8,128)(2,1)S(1)} %copy-done.14, bf16[1024,512]{1,0:T(8,128)(2,1)S(1)} %copy-done.17, ...), custom_call_target="tpu_custom_call" | custom-call | flops 24000000000 | bytes 8000000 | tf_op jit(solution)/shard_map/attend_back/pallas_call | solution.py:333
  565.1 21.7 %collective-permute-done.30.refs_5_ = bf16[2,512,512]{2,1,0:T(8,128)(2,1)} collective-permute-done((bf16[2,512,512]{2,1,0:T(8,128)(2,1)}, bf16[2,512,512]{2,1,0:T(8,128)(2,1)}, u32[]{:S(2)}, u32[]{:S(2)}) %collective-permute-start.30) | collective-permute-done | bytes 1048608 | tf_op jit(solution)/shard_map/ppermute | solution.py:75
  595.7 23.8 %attend_back.3 = (bf16[1024,1024]{1,0:T(8,128)(2,1)S(1)}, bf16[1024,512]{1,0:T(8,128)(2,1)S(1)}, bf16[1024,512]{1,0:T(8,128)(2,1)S(1)}) custom-call(s32[1,1]{1,0:T(1,128)} %bitcast.226.len_ref, bf16[1024,1024]{1,0:T(8,128)(2,1)S(1)} %copy-done.11, bf16[1024,512]{1,0:T(8,128)(2,1)S(1)} %copy-done.14, ...), custom_call_target="tpu_custom_call", output_to_operand_aliasing={{0}: (8, {}), {1}: (9, {}), {2}: (10, {})} | custom-call | flops 24000000000 | bytes 8000000 | tf_op jit(solution)/shard_map/attend_back/pallas_call | solution.py:333
  624.0 15.3 %collective-permute-done.33 = bf16[2,512,512]{2,1,0:T(8,128)(2,1)} collective-permute-done((bf16[2,512,512]{2,1,0:T(8,128)(2,1)}, bf16[2,512,512]{2,1,0:T(8,128)(2,1)}, u32[]{:S(2)}, u32[]{:S(2)}) %collective-permute-start.33) | collective-permute-done | bytes 1048608 | tf_op jit(solution)/shard_map/ppermute | solution.py:75
  639.3 20.7 %collective-permute-done.34 = bf16[2,512,512]{2,1,0:T(8,128)(2,1)} collective-permute-done((bf16[2,512,512]{2,1,0:T(8,128)(2,1)}, bf16[2,512,512]{2,1,0:T(8,128)(2,1)}, u32[]{:S(2)}, u32[]{:S(2)}) %collective-permute-start.34) | collective-permute-done | bytes 1048608 | tf_op jit(solution)/shard_map/ppermute | solution.py:75
  712.2 8.0 add_bitcast_fusion
  723.0 13.8 %collective-permute-done.36 = bf16[2,128,2048]{2,1,0:T(8,128)(2,1)S(1)} collective-permute-done((bf16[2,128,2048]{2,1,0:T(8,128)(2,1)S(1)}, bf16[2,128,2048]{2,1,0:T(8,128)(2,1)S(1)}, u32[]{:S(2)}, u32[]{:S(2)}) %collective-permute-start.36) | collective-permute-done | bytes 1048608 | tf_op jit(solution)/shard_map/ppermute | solution.py:75
  741.3 6.4 collective-permute-done.37
  772.7 11.3 %all-to-all-done.1 = bf16[4,128,1024]{2,1,0:T(8,128)(2,1)} async-done(((bf16[4,128,1024]{2,1,0:T(8,128)(2,1)}), bf16[4,128,1024]{2,1,0:T(8,128)(2,1)}, u32[]{:S(2)}, u32[]{:S(2)}) %all-to-all-start.1) | async-done | bytes 1048608 | tf_op jit(solution)/shard_map/all_to_all | solution.py:870
  827.3 80.0 %ortho_block.1 = f32[1024,1024]{1,0:T(8,128)} custom-call(s32[1]{0:T(128)} %bitcast.79.halves_ref, f32[1024,1024]{1,0:T(8,128)} %pad_maximum_fusion.3.m_ref), custom_call_target="tpu_custom_call" | custom-call | flops 96636764160 | bytes 8388608 | tf_op jit(solution)/shard_map/ortho_block/pallas_call | solution.py:617
  918.4 50.5 %ortho_rows.1 = f32[3,512,512]{2,1,0:T(8,128)S(1)} custom-call(f32[3,1024,512]{2,1,0:T(8,128)S(1)} %pad_maximum_fusion.m_ref), custom_call_target="tpu_custom_call" | custom-call | flops 48318382080 | bytes 4194304 | tf_op jit(solution)/shard_map/ortho_rows/pallas_call | solution.py:699
  (409 shorter events, 294.3 us)
Async XLA Ops:
  7.2 82.1 %all-gather.2.cloned.1.call-start = ((), (), s32[]{:S(2)}) async-start(), calls=%async_computation.4 | async-start | bytes 6758400 | tf_op jit(solution)/shard_map/all_gather | solution.py:817
  13.3 111.1 %all-to-all-start = ((f32[4,32,1024]{2,1,0:T(8,128)}), f32[4,32,1024]{2,1,0:T(8,128)S(1)}, u32[]{:S(2)}, u32[]{:S(2)}) async-start(f32[4,32,1024]{2,1,0:T(8,128)} %pad_maximum_fusion.10), calls=%async_computation | async-start | bytes 1048576 | tf_op jit(solution)/shard_map/all_to_all | solution.py:870
  106.4 78.5 %collective-permute-start.6 = (bf16[1024,1024]{1,0:T(8,128)(2,1)}, bf16[1024,1024]{1,0:T(8,128)(2,1)}, u32[]{:S(2)}, u32[]{:S(2)}) collective-permute-start(bf16[1024,1024]{1,0:T(8,128)(2,1)} %maximum_select_fusion.3), channel_id=1, source_target_pairs={{0,4},{1,5},{2,6},{3,7},{4,0},{5,1},{6,2},{7,3},{8,12},{9,13},{10,... | collective-permute-start | bytes 6291464 | tf_op jit(solution)/shard_map/ppermute | solution.py:75
  172.8 72.6 %collective-permute-start.8 = (bf16[2,2,512,512]{3,2,1,0:T(8,128)(2,1)}, bf16[2,2,512,512]{3,2,1,0:T(8,128)(2,1)}, u32[]{:S(2)}, u32[]{:S(2)}) collective-permute-start(bf16[2,2,512,512]{3,2,1,0:T(8,128)(2,1)} %pad_maximum_fusion.5.refs_5_), channel_id=1, source_target_pairs={{0,1},{1,0},{2,3},{3,2},{4,5},{5,4},{6,7},{7,6},{8,9},{9,8},{10,11... | collective-permute-start | bytes 6291464 | tf_op jit(solution)/shard_map/ppermute | solution.py:75
  172.8 73.4 %collective-permute-start.9 = (bf16[2,2,512,512]{3,2,1,0:T(8,128)(2,1)}, bf16[2,2,512,512]{3,2,1,0:T(8,128)(2,1)}, u32[]{:S(2)}, u32[]{:S(2)}) collective-permute-start(bf16[2,2,512,512]{3,2,1,0:T(8,128)(2,1)} %pad_maximum_fusion.5.refs_5_), channel_id=1, source_target_pairs={{0,8},{1,9},{2,10},{3,11},{4,12},{5,13},{6,14},{7,15},{8,0},{9,1},... | collective-permute-start | bytes 6291464 | tf_op jit(solution)/shard_map/ppermute | solution.py:75
  174.2 73.2 %collective-permute-start.10 = (bf16[2,2,512,512]{3,2,1,0:T(8,128)(2,1)}, bf16[2,2,512,512]{3,2,1,0:T(8,128)(2,1)}, u32[]{:S(2)}, u32[]{:S(2)}) collective-permute-start(bf16[2,2,512,512]{3,2,1,0:T(8,128)(2,1)} %pad_maximum_fusion.5.refs_5_), channel_id=1, source_target_pairs={{0,16},{1,17},{2,18},{3,19},{4,20},{5,21},{6,22},{7,23},{8,24},{9,... | collective-permute-start | bytes 6291464 | tf_op jit(solution)/shard_map/ppermute | solution.py:75
  194.9 108.7 %collective-permute-start.11 = (bf16[1,2,512,512]{3,2,1,0:T(8,128)(2,1)}, bf16[1,2,512,512]{3,2,1,0:T(8,128)(2,1)}, u32[]{:S(2)}, u32[]{:S(2)}) collective-permute-start(bf16[1,2,512,512]{3,2,1,0:T(8,128)(2,1)} %collective-permute-done.3.refs_7_.refs_3_), channel_id=1, source_target_pairs={{0,1},{1,0},{2,3},{3,2},{4,5},{5,4},{6,7},{7,6},{8,9},{9,8},{10,11... | collective-permute-start | bytes 3145736 | tf_op jit(solution)/shard_map/ppermute | solution.py:75
  245.4 118.7 %collective-permute-start.15 = (bf16[1,2,512,512]{3,2,1,0:T(8,128)(2,1)}, bf16[1,2,512,512]{3,2,1,0:T(8,128)(2,1)}, u32[]{:S(2)}, u32[]{:S(2)}) collective-permute-start(bf16[1,2,512,512]{3,2,1,0:T(8,128)(2,1)} %collective-permute-done.14.refs_4_), channel_id=1, source_target_pairs={{0,8},{1,9},{2,10},{3,11},{4,12},{5,13},{6,14},{7,15},{8,0},{9,1},... | collective-permute-start | bytes 3145736 | tf_op jit(solution)/shard_map/ppermute | solution.py:75
  303.6 71.4 %collective-permute-start.20 = (bf16[2,1024,1024]{2,1,0:T(8,128)(2,1)}, bf16[2,1024,1024]{2,1,0:T(8,128)(2,1)}, u32[]{:S(2)}, u32[]{:S(2)}) collective-permute-start(bf16[2,1024,1024]{2,1,0:T(8,128)(2,1)} %get-tuple-element.105), channel_id=1, source_target_pairs={{0,4},{1,5},{2,6},{3,7},{4,0},{5,1},{6,2},{7,3},{8,12},{9,13},{10,... | collective-permute-start | bytes 12582920 | tf_op jit(solution)/shard_map/ppermute | solution.py:75
  303.7 71.3 %collective-permute-start.19 = (bf16[3,2,512,512]{3,2,1,0:T(8,128)(2,1)}, bf16[3,2,512,512]{3,2,1,0:T(8,128)(2,1)}, u32[]{:S(2)}, u32[]{:S(2)}) collective-permute-start(bf16[3,2,512,512]{3,2,1,0:T(8,128)(2,1)} %get-tuple-element.104), channel_id=1, source_target_pairs={{0,1},{1,0},{2,3},{3,2},{4,5},{5,4},{6,7},{7,6},{8,9},{9,8},{10,11... | collective-permute-start | bytes 9437192 | tf_op jit(solution)/shard_map/ppermute | solution.py:75
  364.1 77.8 %collective-permute-start.22 = (bf16[2,1024,1024]{2,1,0:T(8,128)(2,1)}, bf16[2,1024,1024]{2,1,0:T(8,128)(2,1)}, u32[]{:S(2)}, u32[]{:S(2)}) collective-permute-start(bf16[2,1024,1024]{2,1,0:T(8,128)(2,1)} %get-tuple-element.108), channel_id=1, source_target_pairs={{0,4},{1,5},{2,6},{3,7},{4,0},{5,1},{6,2},{7,3},{8,12},{9,13},{10,... | collective-permute-start | bytes 12582920 | tf_op jit(solution)/shard_map/ppermute | solution.py:75
  364.2 77.7 %collective-permute-start.21 = (bf16[3,2,512,512]{3,2,1,0:T(8,128)(2,1)}, bf16[3,2,512,512]{3,2,1,0:T(8,128)(2,1)}, u32[]{:S(2)}, u32[]{:S(2)}) collective-permute-start(bf16[3,2,512,512]{3,2,1,0:T(8,128)(2,1)} %get-tuple-element.107), channel_id=1, source_target_pairs={{0,1},{1,0},{2,3},{3,2},{4,5},{5,4},{6,7},{7,6},{8,9},{9,8},{10,11... | collective-permute-start | bytes 9437192 | tf_op jit(solution)/shard_map/ppermute | solution.py:75
  430.0 72.0 %collective-permute-start.25 = (bf16[2,1024,1024]{2,1,0:T(8,128)(2,1)}, bf16[2,1024,1024]{2,1,0:T(8,128)(2,1)}, u32[]{:S(2)}, u32[]{:S(2)}) collective-permute-start(bf16[2,1024,1024]{2,1,0:T(8,128)(2,1)} %get-tuple-element.115), channel_id=1, source_target_pairs={{0,4},{1,5},{2,6},{3,7},{4,0},{5,1},{6,2},{7,3},{8,12},{9,13},{10,... | collective-permute-start | bytes 12582920 | tf_op jit(solution)/shard_map/ppermute | solution.py:75
  430.0 71.8 %collective-permute-start.23 = (bf16[3,2,512,512]{3,2,1,0:T(8,128)(2,1)}, bf16[3,2,512,512]{3,2,1,0:T(8,128)(2,1)}, u32[]{:S(2)}, u32[]{:S(2)}) collective-permute-start(bf16[3,2,512,512]{3,2,1,0:T(8,128)(2,1)} %get-tuple-element.113), channel_id=1, source_target_pairs={{0,8},{1,9},{2,10},{3,11},{4,12},{5,13},{6,14},{7,15},{8,0},{9,1},... | collective-permute-start | bytes 9437192 | tf_op jit(solution)/shard_map/ppermute | solution.py:75
  431.6 70.5 %collective-permute-start.24 = (bf16[3,2,512,512]{3,2,1,0:T(8,128)(2,1)}, bf16[3,2,512,512]{3,2,1,0:T(8,128)(2,1)}, u32[]{:S(2)}, u32[]{:S(2)}) collective-permute-start(bf16[3,2,512,512]{3,2,1,0:T(8,128)(2,1)} %get-tuple-element.114), channel_id=1, source_target_pairs={{0,16},{1,17},{2,18},{3,19},{4,20},{5,21},{6,22},{7,23},{8,24},{9,... | collective-permute-start | bytes 9437192 | tf_op jit(solution)/shard_map/ppermute | solution.py:75
  510.9 84.7 %collective-permute-start.31 = (bf16[3,2,512,512]{3,2,1,0:T(8,128)(2,1)}, bf16[3,2,512,512]{3,2,1,0:T(8,128)(2,1)}, u32[]{:S(2)}, u32[]{:S(2)}) collective-permute-start(bf16[3,2,512,512]{3,2,1,0:T(8,128)(2,1)} %add_convert_fusion), channel_id=1, source_target_pairs={{0,8},{1,9},{2,10},{3,11},{4,12},{5,13},{6,14},{7,15},{8,0},{9,1},... | collective-permute-start | bytes 9437192 | tf_op jit(solution)/shard_map/ppermute | solution.py:75
  518.4 68.4 %collective-permute-start.30 = (bf16[2,512,512]{2,1,0:T(8,128)(2,1)}, bf16[2,512,512]{2,1,0:T(8,128)(2,1)}, u32[]{:S(2)}, u32[]{:S(2)}) collective-permute-start(bf16[2,512,512]{2,1,0:T(8,128)(2,1)} %get-tuple-element.283), channel_id=1, source_target_pairs={{0,1},{1,0},{2,3},{3,2},{4,5},{5,4},{6,7},{7,6},{8,9},{9,8},{10,11... | collective-permute-start | bytes 3145736 | tf_op jit(solution)/shard_map/ppermute | solution.py:75
  592.5 67.5 %collective-permute-start.34 = (bf16[2,512,512]{2,1,0:T(8,128)(2,1)}, bf16[2,512,512]{2,1,0:T(8,128)(2,1)}, u32[]{:S(2)}, u32[]{:S(2)}) collective-permute-start(bf16[2,512,512]{2,1,0:T(8,128)(2,1)} %get-tuple-element.293), channel_id=1, source_target_pairs={{0,16},{1,17},{2,18},{3,19},{4,20},{5,21},{6,22},{7,23},{8,24},{9,... | collective-permute-start | bytes 3145736 | tf_op jit(solution)/shard_map/ppermute | solution.py:75
  624.0 83.8 %collective-permute-start.35 = (bf16[4,128,2048]{2,1,0:T(8,128)(2,1)}, bf16[4,128,2048]{2,1,0:T(8,128)(2,1)}, u32[]{:S(2)}, u32[]{:S(2)}) collective-permute-start(bf16[4,128,2048]{2,1,0:T(8,128)(2,1)} %dynamic-slice_bitcast_fusion), channel_id=1, source_target_pairs={{0,4},{1,5},{2,6},{3,7},{4,0},{5,1},{6,2},{7,3},{8,12},{9,13},{10,... | collective-permute-start | bytes 6291464 | tf_op jit(solution)/shard_map/ppermute | solution.py:75
  690.0 74.4 %collective-permute-start.42 = (bf16[512,512]{1,0:T(8,128)(2,1)}, bf16[512,512]{1,0:T(8,128)(2,1)}, u32[]{:S(2)}, u32[]{:S(2)}) collective-permute-start(bf16[512,512]{1,0:T(8,128)(2,1)} %slice_bitcast_fusion.1), channel_id=1, source_target_pairs={{0,2},{1,3},{2,0},{3,1},{4,6},{5,7},{6,4},{7,5},{8,10},{9,11},{10,... | collective-permute-start | bytes 1572872 | tf_op jit(solution)/shard_map/ppermute | solution.py:75
  704.2 68.4 %collective-permute-start.41 = (bf16[512,512]{1,0:T(8,128)(2,1)}, bf16[512,512]{1,0:T(8,128)(2,1)S(1)}, u32[]{:S(2)}, u32[]{:S(2)}) collective-permute-start(bf16[512,512]{1,0:T(8,128)(2,1)} %slice_bitcast_fusion.2), channel_id=1, source_target_pairs={{0,2},{1,3},{2,0},{3,1},{4,6},{5,7},{6,4},{7,5},{8,10},{9,11},{10,... | collective-permute-start | bytes 1572872 | tf_op jit(solution)/shard_map/ppermute | solution.py:75
  799.6 107.8 %collective-permute-start.50 = (f32[512,512]{1,0:T(8,128)S(1)}, f32[512,512]{1,0:T(8,128)}, u32[]{:S(2)}, u32[]{:S(2)}) collective-permute-start(f32[512,512]{1,0:T(8,128)S(1)} %get-tuple-element.161), channel_id=1, source_target_pairs={{0,1},{1,0},{2,3},{3,2},{4,5},{5,4},{6,7},{7,6},{8,9},{9,8},{10,11... | collective-permute-start | bytes 3145736 | tf_op jit(solution)/shard_map/ppermute | solution.py:75
  800.6 106.8 %collective-permute-start.51 = (f32[512,512]{1,0:T(8,128)S(1)}, f32[512,512]{1,0:T(8,128)}, u32[]{:S(2)}, u32[]{:S(2)}) collective-permute-start(f32[512,512]{1,0:T(8,128)S(1)} %get-tuple-element.163), channel_id=1, source_target_pairs={{0,1},{1,0},{2,3},{3,2},{4,5},{5,4},{6,7},{7,6},{8,9},{9,8},{10,11... | collective-permute-start | bytes 3145736 | tf_op jit(solution)/shard_map/ppermute | solution.py:75
  801.7 105.7 %collective-permute-start.52 = (f32[512,512]{1,0:T(8,128)S(1)}, f32[512,512]{1,0:T(8,128)}, u32[]{:S(2)}, u32[]{:S(2)}) collective-permute-start(f32[512,512]{1,0:T(8,128)S(1)} %get-tuple-element.165), channel_id=1, source_target_pairs={{0,1},{1,0},{2,3},{3,2},{4,5},{5,4},{6,7},{7,6},{8,9},{9,8},{10,11... | collective-permute-start | bytes 3145736 | tf_op jit(solution)/shard_map/ppermute | solution.py:75
  (111 other events, 2200.5 us)
Sparse Core Ops, SparseCore 0:
  11.4 77.7 all-gather.1

commit v3 on v2

--- a/solution.py
+++ b/solution.py
@@ -378,8 +378,8 @@
 
 def expert_kernel(waits, first, *refs):
     n2_ref, dy_ref, gate_ref = refs[:3]
-    wg_own_ref, wg_other_ref, wb_own_ref, wb_other_ref = refs[3:7]
-    outs = refs[7 + waits :]
+    own_w_ref, other_w_ref = refs[3:5]
+    outs = refs[5 + waits :]
     own_ref, pair_ref, dgate_ref, grad_own_ref, grad_other_ref = outs[:5]
     m_acc, dn_acc, g_acc, u_acc, d_acc, turned_ref = outs[5:]
     step = pl.program_id(0)
@@ -393,9 +393,9 @@
     def _():
         turned_ref[:, place] = n2_ref[...].T
 
-    wg_own, wg_other = wg_own_ref[0, 0], wg_other_ref[0, 0]
-    wu_own, wu_other = wb_own_ref[0, 0], wb_other_ref[0, 0]
-    wd_own, wd_other = wb_own_ref[1, 0], wb_other_ref[1, 0]
+    wg_own, wg_other = own_w_ref[0, 0], other_w_ref[0, 0]
+    wu_own, wu_other = own_w_ref[1, 0], other_w_ref[1, 0]
+    wd_own, wd_other = own_w_ref[2, 0], other_w_ref[2, 0]
     column = lane == step + first
     gate = jnp.sum(jnp.where(column, gate_ref[...], 0.0), axis=1, keepdims=True)
     dm = RESID_MULT * dy_ref[...].astype(jnp.float32)
@@ -478,10 +478,8 @@
             pl.BlockSpec((rows, D), lambda s, b: (b, 0)),
             pl.BlockSpec((rows, D), lambda s, b: (b, 0)),
             pl.BlockSpec((rows, PACK), lambda s, b: (b, 0)),
-            pieces(1),
-            pieces(1),
-            pieces(2),
-            pieces(2),
+            pieces(3),
+            pieces(3),
         ]
         + [pl.BlockSpec(memory_space=pl.ANY)] * len(done),
         out_specs=[
@@ -825,10 +823,7 @@
     early_bits = bits_below(1, half_bit)
     own_half = gather_rows(expert_weight.astype(jnp.bfloat16), 1, count, place, early_bits)
     level_one = (((1, 0, 0), half_bit), ((0, 1, 0), bit_x), ((0, 0, 1), bit_y))
-    gather_last = (
-        {(1, 1, 0): half_bit, (0, 1, 1): bit_y, (1, 0, 1): half_bit, (1, 1, 1): bit_x},
-        {(1, 1, 0): bit_x, (0, 1, 1): bit_y, (1, 0, 1): bit_y, (1, 1, 1): bit_x},
-    )
+    level_two = (((1, 1, 0), bit_x), ((0, 1, 1), bit_y), ((1, 0, 1), half_bit))
     hop_of = {half_bit: 0, bit_x: 1, bit_y: 2}
 
     def before_hop(chunk, bit):
@@ -836,19 +831,9 @@
             side ^ 1 if index == hop_of[bit] else side for index, side in enumerate(chunk)
         )
 
-    chunks = [{}, {}]
-    before = None
-    for part, kinds in enumerate((slice(0, 1), slice(1, 3))):
-        own = own_half[kinds]
-        own = after(own, full_packed if before is None else before)
-        before = swap_bit(own, count, bit_z)
-        chunks[part][0, 0, 0] = jnp.stack([own, before], axis=1)
-        for chunk, bit in level_one:
-            chunks[part][chunk] = swap_bit(chunks[part][0, 0, 0], count, bit)
-    for chunk in ((1, 1, 0), (0, 1, 1), (1, 0, 1), (1, 1, 1)):
-        for part in range(2):
-            bit = gather_last[part][chunk]
-            chunks[part][chunk] = swap_bit(chunks[part][before_hop(chunk, bit)], count, bit)
+    chunks = {(0, 0, 0): jnp.stack([own_half, swap_bit(own_half, count, bit_z)], axis=1)}
+    for chunk, bit in level_one:
+        chunks[chunk] = swap_bit(chunks[before_hop(chunk, bit)], count, bit)
     gain_one = full_gains[0].astype(jnp.float32)
     gain_two = full_gains[1].astype(jnp.float32)
     inputs = tokens.astype(jnp.float32)
@@ -882,10 +867,11 @@
         key_rows,
         value_rows,
         seq_len,
-        [chunks[0][0, 0, 0], old_tasks],
+        [chunks[0, 0, 0], old_tasks],
     )
     branch = plain_dot(attended, w_out, 1, 1)
-    branch = after(branch, chunks[1][0, 0, 0], *[chunks[0][chunk] for chunk, _ in level_one])
+    for chunk, bit in level_two:
+        chunks[chunk] = swap_bit(after(chunks[before_hop(chunk, bit)], branch), count, bit)
     hidden_state = inputs + RESID_MULT * branch
     scale_two = lax.rsqrt(jnp.mean(hidden_state * hidden_state, axis=-1, keepdims=True) + NORM_EPS)
     unit_two = hidden_state * scale_two
@@ -913,14 +899,13 @@
         moved[chunk] = swap_bit(grads[chunk], count, bit)
 
     waits = {
-        (0, 0): lambda: [chunks[part][0, 1, 0] for part in range(2)]
-        + [chunks[part][0, 0, 1] for part in range(2)],
-        (1, 0): lambda: [],
+        (0, 0): lambda: [chunks[0, 1, 0], chunks[0, 0, 1]],
+        (1, 0): lambda: [chunks[0, 1, 1], chunks[1, 0, 1]],
         (1, 1): lambda: [moved[1, 0, 0], pair_parts[0]],
         (0, 1): lambda: [moved[1, 1, 0], pair_parts[1]],
     }
     for turn_index, (far_x, far_y) in enumerate(groups):
-        weights = [chunks[part][half, far_x, far_y] for part in range(2) for half in range(2)]
+        weights = [chunks[half, far_x, far_y] for half in range(2)]
         own_part, pair_part, dgate, grad_own, grad_other = expert_call(
             2 * turn_index,
             both_second,
@@ -936,6 +921,7 @@
         grads[1, far_x, far_y] = grad_other
         if (far_x, far_y) == (0, 0):
             send((1, 0, 0), half_bit)
+            chunks[1, 1, 1] = swap_bit(after(chunks[1, 0, 1], own_part), count, bit_x)
         if (far_x, far_y) == (1, 0):
             send((1, 1, 0), half_bit)
         if (far_x, far_y) == (1, 1):
@@ -1021,31 +1007,30 @@
         )
 
     first_heads = attend_back(0, [], [])
-    last_own, half_y, _ = lax.optimization_barrier((grads[0, 0, 1], half_y, first_heads[0]))
+    last_own, half_y[:2], _ = lax.optimization_barrier(
+        (grads[0, 0, 1], half_y[:2], first_heads[0])
+    )
+    grad_query, grad_key, grad_value = attend_back(1, first_heads, half_y[:2] + [moved[0, 1, 0]])
+    half_y[2], _ = lax.optimization_barrier((half_y[2], grad_query))
     from_y = [
         swap_bit(total_of(last_own[kind], half_y[kind]), count, bit_y) for kind in range(3)
     ]
-    grad_query, grad_key, grad_value = attend_back(
-        1, first_heads, half_y + [moved[0, 1, 0]]
-    )
     late_parts = after(tuple(own_parts + pair_parts), grad_query)
     block_out = (hidden_state + RESID_MULT * gather_sum([part[0] for part in late_parts])).astype(
         jnp.bfloat16
     )
+    grad_query, from_y[0] = lax.optimization_barrier((grad_query, from_y[0]))
     low_grad = [
         pin(plain_dot(normed_one, piece, 0, 0).astype(jnp.bfloat16))
         for piece in (grad_query, grad_key, grad_value)
     ]
-    nearest, from_y, _ = lax.optimization_barrier((grads[0, 0, 0], from_y, low_grad[0]))
-    expert_sums = [
-        total_of(nearest[kind], moved[1, 0, 0][kind], moved[0, 1, 0][kind], from_y[kind])
-        for kind in range(3)
-    ]
-    late_query = after(grad_query, *from_y)
     grad_normed_one = (
-        plain_dot(late_query, w_query, 1, 1)
+        plain_dot(grad_query, w_query, 1, 1)
         + plain_dot(grad_key, w_shared[:, :kv_width], 1, 1)
         + plain_dot(grad_value, w_shared[:, kv_width:], 1, 1)
+    )
+    nearest, from_y[:2], grad_normed_one, low_grad[1:] = lax.optimization_barrier(
+        (grads[0, 0, 0], from_y[:2], grad_normed_one, low_grad[1:])
     )
     scale_one = lax.rsqrt(jnp.mean(inputs * inputs, axis=-1, keepdims=True) + NORM_EPS)
     unit_one = inputs * scale_one
@@ -1090,6 +1075,11 @@
     attn_block = jnp.concatenate(
         [gather_from_owners(side, count, place, [pair_bit], wide_x) for side in sides], axis=1
     )
+    from_y[2] = after(from_y[2], wide_sum)
+    expert_sums = [
+        total_of(nearest[kind], moved[1, 0, 0][kind], moved[0, 1, 0][kind], from_y[kind])
+        for kind in range(3)
+    ]
     moment_expert, group_rows = [], []
     for kind in range(3):
         total = after(expert_sums[kind], wide_sum, shared_sum)

time: 1000 us -> 1030 us (1.030)
  waiting for transfers between devices: 244 us -> 261 us
    ppermute x53 -> x45, waiting for transfers between devices: 176 us -> 225 us  [swap_bit(): return pin(lax.ppermute(pin(values), AXES, pairs))]
    all_gather x1, waiting for transfers between devices: 56.8 us -> 36.2 us  [shards(): lax.all_gather(jnp.concatenate([attn_low, small_low], axis=1), AXES, axis...]
    all_to_all x4, waiting for transfers between devices: 11.3 us -> 0.01 us  [spread(): lax.all_to_all(values, 'blk', split_axis=0, concat_axis=0, tiled=True)]
    ppermute x53 -> x45, starting transfers between devices: 44.7 us -> 41.2 us  [swap_bit(): return pin(lax.ppermute(pin(values), AXES, pairs))]
    unnamed x164 -> x184, local copies, waits for them, and re-layouts: 31.9 us -> 34.4 us
  transfers between devices with their start and end apart: 58 -> 50, of which waited for: 21 -> 21; matrix products, arithmetic and copies ran while one was open for 19% -> 20% of each run, Pallas kernels for 44% -> 43%
where the time goes in v3:
time: 1030 us; the launch traced here: 1020 us
  Pallas kernels  438 us (43%)
  waiting for transfers between devices  261 us (25%)
  other arithmetic  129 us (13%)
  local copies, waits for them, and re-layouts  83.3 us (8%)
  starting transfers between devices  60.6 us (6%)
  matrix products  34.9 us (3%)
  between operations  16.3 us (2%)
    ppermute x45, waiting for transfers between devices, swap_bit(): return pin(lax.ppermute(pin(values), AXES, pairs))  225 us
    pallas_call x4, Pallas kernels, expert_call(): pl.pallas_call(functools.partial(expert_kernel, len(done), first), grid=(...  220 us
    pallas_call x1, Pallas kernels, ortho_block_call(): pl.pallas_call(ortho_block_kernel, in_specs=[pl.BlockSpec(memory_space=pl...  80.1 us
    pallas_call x1, Pallas kernels, ortho_rows_call(): pl.pallas_call(ortho_rows_kernel, grid=(kinds,), in_specs=[pl.BlockSpec((...  50.5 us
    pallas_call x2, Pallas kernels, attend_back_call(): pl.pallas_call(attend_back_kernel, grid=(seqs, groups), in_specs=[pl.Bloc...  45.9 us
    ppermute x45, starting transfers between devices, swap_bit(): return pin(lax.ppermute(pin(values), AXES, pairs))  41.2 us
    all_gather x1, waiting for transfers between devices, shards(): lax.all_gather(jnp.concatenate([attn_low, small_low], axis=1), AXES, axis...  36.2 us
    unnamed x184, local copies, waits for them, and re-layouts  34.4 us
  transfers between devices with their start and end apart: 50, of which 21 were waited for; matrix products, arithmetic and copies ran while one was open for 20% of the time, Pallas kernels for 43%

profile of v3, /device:TPU:0, one launch (start us, length us, event | category | flops | bytes accessed | tf_op | source)
XLA Modules:
  0.0 1023.2 jit_solution(7858355508120908625)
XLA Ops:
  13.3 6.3 all-to-all-start
  33.2 81.7 %collective-permute-done = bf16[3,512,512]{2,1,0:T(8,128)(2,1)} collective-permute-done((bf16[3,512,512]{2,1,0:T(8,128)(2,1)}, bf16[3,512,512]{2,1,0:T(8,128)(2,1)}, u32[]{:S(2)}, u32[]{:S(2)}) %collective-permute-start) | collective-permute-done | bytes 1572896 | tf_op jit(solution)/shard_map/ppermute | solution.py:75
  121.4 36.2 %all-gather.2.cloned.1.call-done.wq_ref.wkv_ref = bf16[1024,3200]{1,0:T(8,128)(2,1)} async-done(((bf16[32,3200]{1,0:T(8,128)(2,1)}), bf16[1024,3200]{1,0:T(8,128)(2,1)}) %all-gather.2.cloned.1.call-update) | async-done | bytes 6553616 | tf_op jit(solution)/shard_map/all_gather | solution.py:815
  161.8 7.7 project.1
  178.2 33.5 %attend.1 = (bf16[1024,1024]{1,0:T(8,128)(2,1)S(1)}, f32[4,8,1024]{2,1,0:T(8,128)S(1)}) custom-call(s32[1,1]{1,0:T(1,128)} %bitcast.223.len_ref, bf16[1024,1024]{1,0:T(8,128)(2,1)S(1)} %copy-done.9, bf16[1024,512]{1,0:T(8,128)(2,1)S(1)} %copy-done.12, bf16[1024,512]{1,0:T(8,128)(2,1)S(1)} %copy-done.15, ...), custom_call_target="tpu_custom_call" | custom-call | flops 20000000000 | bytes 8000000 | tf_op jit(solution)/shard_map/attend/pallas_call | solution.py:234
  259.5 55.2 %experts.4 = (bf16[2,1024,1024]{2,1,0:T(8,128)(2,1)}, bf16[2,1024,1024]{2,1,0:T(8,128)(2,1)}, f32[2048,128]{1,0:T(8,128)}, bf16[3,2,512,512]{3,2,1,0:T(8,128)(2,1)}, bf16[3,2,512,512]{3,2,1,0:T(8,128)(2,1)}) custom-call(bf16[2048,1024]{1,0:T(8,128)(2,1)} %pad_maximum_fusion.1.refs_0_, bf16[2048,1024]{1,0:T(8,128)(2,1)} %constant_dynamic-update-slice_fusion.refs_1_, ...), custom_call_target="tpu_custom_call" | custom-call | flops 57982058496 | bytes 50331648 | tf_op jit(solution)/shard_map/experts/pallas_call | solution.py:474
  322.1 54.8 %experts.5 = (bf16[2,1024,1024]{2,1,0:T(8,128)(2,1)}, bf16[2,1024,1024]{2,1,0:T(8,128)(2,1)}, f32[2048,128]{1,0:T(8,128)}, bf16[3,2,512,512]{3,2,1,0:T(8,128)(2,1)}, bf16[3,2,512,512]{3,2,1,0:T(8,128)(2,1)}) custom-call(bf16[2048,1024]{1,0:T(8,128)(2,1)} %pad_maximum_fusion.1.refs_0_, bf16[2048,1024]{1,0:T(8,128)(2,1)} %constant_dynamic-update-slice_fusion.refs_1_, ...), custom_call_target="tpu_custom_call" | custom-call | flops 57982058496 | bytes 50331648 | tf_op jit(solution)/shard_map/experts/pallas_call | solution.py:474
  376.9 9.1 collective-permute-done.11.refs_5_
  388.1 55.0 %experts.6 = (bf16[2,1024,1024]{2,1,0:T(8,128)(2,1)}, bf16[2,1024,1024]{2,1,0:T(8,128)(2,1)}, f32[2048,128]{1,0:T(8,128)}, bf16[3,2,512,512]{3,2,1,0:T(8,128)(2,1)}, bf16[3,2,512,512]{3,2,1,0:T(8,128)(2,1)}) custom-call(bf16[2048,1024]{1,0:T(8,128)(2,1)} %pad_maximum_fusion.1.refs_0_, bf16[2048,1024]{1,0:T(8,128)(2,1)} %constant_dynamic-update-slice_fusion.refs_1_, ...), custom_call_target="tpu_custom_call" | custom-call | flops 57982058496 | bytes 50331648 | tf_op jit(solution)/shard_map/experts/pallas_call | solution.py:474
  444.9 8.1 collective-permute-done.13.refs_5_
  453.0 54.9 %experts.7 = (bf16[2,1024,1024]{2,1,0:T(8,128)(2,1)}, bf16[2,1024,1024]{2,1,0:T(8,128)(2,1)}, f32[2048,128]{1,0:T(8,128)}, bf16[3,2,512,512]{3,2,1,0:T(8,128)(2,1)}, bf16[3,2,512,512]{3,2,1,0:T(8,128)(2,1)}) custom-call(bf16[2048,1024]{1,0:T(8,128)(2,1)} %pad_maximum_fusion.1.refs_0_, bf16[2048,1024]{1,0:T(8,128)(2,1)} %constant_dynamic-update-slice_fusion.refs_1_, ...), custom_call_target="tpu_custom_call" | custom-call | flops 57982058496 | bytes 50331648 | tf_op jit(solution)/shard_map/experts/pallas_call | solution.py:474
  534.7 7.7 add_bitcast_fusion.1
  553.5 22.7 %attend_back.2 = (bf16[1024,1024]{1,0:T(8,128)(2,1)S(1)}, bf16[1024,512]{1,0:T(8,128)(2,1)S(1)}, bf16[1024,512]{1,0:T(8,128)(2,1)S(1)}) custom-call(s32[1,1]{1,0:T(1,128)} %bitcast.224.len_ref, bf16[1024,1024]{1,0:T(8,128)(2,1)S(1)} %copy-done.10, bf16[1024,512]{1,0:T(8,128)(2,1)S(1)} %copy-done.13, bf16[1024,512]{1,0:T(8,128)(2,1)S(1)} %copy-done.16, ...), custom_call_target="tpu_custom_call" | custom-call | flops 24000000000 | bytes 8000000 | tf_op jit(solution)/shard_map/attend_back/pallas_call | solution.py:333
  580.1 13.2 %collective-permute-done.22.refs_5_ = bf16[3,2,512,512]{3,2,1,0:T(8,128)(2,1)} collective-permute-done((bf16[3,2,512,512]{3,2,1,0:T(8,128)(2,1)}, bf16[3,2,512,512]{3,2,1,0:T(8,128)(2,1)}, u32[]{:S(2)}, u32[]{:S(2)}) %collective-permute-start.22) | collective-permute-done | bytes 3145760 | tf_op jit(solution)/shard_map/ppermute | solution.py:75
  593.3 23.2 %attend_back.3 = (bf16[1024,1024]{1,0:T(8,128)(2,1)S(1)}, bf16[1024,512]{1,0:T(8,128)(2,1)S(1)}, bf16[1024,512]{1,0:T(8,128)(2,1)S(1)}) custom-call(s32[1,1]{1,0:T(1,128)} %bitcast.225.len_ref, bf16[1024,1024]{1,0:T(8,128)(2,1)S(1)} %copy-done.10, bf16[1024,512]{1,0:T(8,128)(2,1)S(1)} %copy-done.13, ...), custom_call_target="tpu_custom_call", output_to_operand_aliasing={{0}: (8, {}), {1}: (9, {}), {2}: (10, {})} | custom-call | flops 24000000000 | bytes 8000000 | tf_op jit(solution)/shard_map/attend_back/pallas_call | solution.py:333
  630.5 15.7 %collective-permute-done.23 = bf16[2,512,512]{2,1,0:T(8,128)(2,1)S(1)} collective-permute-done((bf16[2,512,512]{2,1,0:T(8,128)(2,1)S(1)}, bf16[2,512,512]{2,1,0:T(8,128)(2,1)S(1)}, u32[]{:S(2)}, u32[]{:S(2)}) %collective-permute-start.23) | collective-permute-done | bytes 1048608 | tf_op jit(solution)/shard_map/ppermute | solution.py:75
  657.9 10.8 %collective-permute-done.24 = bf16[2,512,512]{2,1,0:T(8,128)(2,1)S(1)} collective-permute-done((bf16[2,512,512]{2,1,0:T(8,128)(2,1)}, bf16[2,512,512]{2,1,0:T(8,128)(2,1)S(1)}, u32[]{:S(2)}, u32[]{:S(2)}) %collective-permute-start.24) | collective-permute-done | bytes 1048608 | tf_op jit(solution)/shard_map/ppermute | solution.py:75
  676.3 7.6 add_bitcast_fusion
  721.4 9.4 collective-permute-done.26
  736.8 8.9 collective-permute-done.27
  768.5 42.2 %collective-permute-done.31 = bf16[512,512]{1,0:T(8,128)(2,1)} collective-permute-done((bf16[512,512]{1,0:T(8,128)(2,1)}, bf16[512,512]{1,0:T(8,128)(2,1)}, u32[]{:S(2)}, u32[]{:S(2)}) %collective-permute-start.31) | collective-permute-done | bytes 524320 | tf_op jit(solution)/shard_map/ppermute | solution.py:75
  810.7 10.1 collective-permute-done.35
  863.1 80.1 %ortho_block.1 = f32[1024,1024]{1,0:T(8,128)} custom-call(s32[1]{0:T(128)} %bitcast.77.halves_ref, f32[1024,1024]{1,0:T(8,128)} %pad_maximum_fusion.3.m_ref), custom_call_target="tpu_custom_call" | custom-call | flops 96636764160 | bytes 8388608 | tf_op jit(solution)/shard_map/ortho_block/pallas_call | solution.py:615
  954.8 50.5 %ortho_rows.1 = f32[3,512,512]{2,1,0:T(8,128)S(1)} custom-call(f32[3,1024,512]{2,1,0:T(8,128)S(1)} %pad_maximum_fusion.m_ref), custom_call_target="tpu_custom_call" | custom-call | flops 48318382080 | bytes 4194304 | tf_op jit(solution)/shard_map/ortho_rows/pallas_call | solution.py:697
  (412 shorter events, 302.4 us)
Async XLA Ops:
  7.2 150.4 %all-gather.2.cloned.1.call-start = ((), (), s32[]{:S(2)}) async-start(), calls=%async_computation.4 | async-start | bytes 6758400 | tf_op jit(solution)/shard_map/all_gather | solution.py:815
  13.3 160.9 %all-to-all-start = ((f32[4,32,1024]{2,1,0:T(8,128)}), f32[4,32,1024]{2,1,0:T(8,128)S(1)}, u32[]{:S(2)}, u32[]{:S(2)}) async-start(f32[4,32,1024]{2,1,0:T(8,128)} %pad_maximum_fusion.9), calls=%async_computation | async-start | bytes 1048576 | tf_op jit(solution)/shard_map/all_to_all | solution.py:855
  22.9 92.0 %collective-permute-start = (bf16[3,512,512]{2,1,0:T(8,128)(2,1)}, bf16[3,512,512]{2,1,0:T(8,128)(2,1)}, u32[]{:S(2)}, u32[]{:S(2)}) collective-permute-start(bf16[3,512,512]{2,1,0:T(8,128)(2,1)} %convert_element_type.467), channel_id=1, source_target_pairs={{0,2},{1,3},{2,0},{3,1},{4,6},{5,7},{6,4},{7,5},{8,10},{9,11},{10,... | collective-permute-start | bytes 4718600 | tf_op jit(solution)/shard_map/ppermute | solution.py:75
  118.4 125.1 %collective-permute-start.6 = (bf16[3,2,512,512]{3,2,1,0:T(8,128)(2,1)}, bf16[3,2,512,512]{3,2,1,0:T(8,128)(2,1)}, u32[]{:S(2)}, u32[]{:S(2)}) collective-permute-start(bf16[3,2,512,512]{3,2,1,0:T(8,128)(2,1)} %pad_maximum_fusion.4.refs_0_.refs_3_), channel_id=1, source_target_pairs={{0,16},{1,17},{2,18},{3,19},{4,20},{5,21},{6,22},{7,23},{8,24},{9,... | collective-permute-start | bytes 9437192 | tf_op jit(solution)/shard_map/ppermute | solution.py:75
  119.9 123.9 %collective-permute-start.5 = (bf16[3,2,512,512]{3,2,1,0:T(8,128)(2,1)}, bf16[3,2,512,512]{3,2,1,0:T(8,128)(2,1)}, u32[]{:S(2)}, u32[]{:S(2)}) collective-permute-start(bf16[3,2,512,512]{3,2,1,0:T(8,128)(2,1)} %pad_maximum_fusion.4.refs_0_.refs_3_), channel_id=1, source_target_pairs={{0,8},{1,9},{2,10},{3,11},{4,12},{5,13},{6,14},{7,15},{8,0},{9,1},... | collective-permute-start | bytes 9437192 | tf_op jit(solution)/shard_map/ppermute | solution.py:75
  121.4 126.0 %collective-permute-start.4 = (bf16[3,2,512,512]{3,2,1,0:T(8,128)(2,1)}, bf16[3,2,512,512]{3,2,1,0:T(8,128)(2,1)}, u32[]{:S(2)}, u32[]{:S(2)}) collective-permute-start(bf16[3,2,512,512]{3,2,1,0:T(8,128)(2,1)} %pad_maximum_fusion.4.refs_0_.refs_3_), channel_id=1, source_target_pairs={{0,1},{1,0},{2,3},{3,2},{4,5},{5,4},{6,7},{7,6},{8,9},{9,8},{10,11... | collective-permute-start | bytes 9437192 | tf_op jit(solution)/shard_map/ppermute | solution.py:75
  243.8 72.4 %collective-permute-start.9 = (bf16[3,2,512,512]{3,2,1,0:T(8,128)(2,1)}, bf16[3,2,512,512]{3,2,1,0:T(8,128)(2,1)}, u32[]{:S(2)}, u32[]{:S(2)}) collective-permute-start(bf16[3,2,512,512]{3,2,1,0:T(8,128)(2,1)} %collective-permute-done.6.refs_6_.refs_3_), channel_id=1, source_target_pairs={{0,1},{1,0},{2,3},{3,2},{4,5},{5,4},{6,7},{7,6},{8,9},{9,8},{10,11... | collective-permute-start | bytes 9437192 | tf_op jit(solution)/shard_map/ppermute | solution.py:75
  247.4 70.4 %collective-permute-start.8 = (bf16[3,2,512,512]{3,2,1,0:T(8,128)(2,1)}, bf16[3,2,512,512]{3,2,1,0:T(8,128)(2,1)}, u32[]{:S(2)}, u32[]{:S(2)}) collective-permute-start(bf16[3,2,512,512]{3,2,1,0:T(8,128)(2,1)} %collective-permute-done.5.refs_5_.refs_3_), channel_id=1, source_target_pairs={{0,16},{1,17},{2,18},{3,19},{4,20},{5,21},{6,22},{7,23},{8,24},{9,... | collective-permute-start | bytes 9437192 | tf_op jit(solution)/shard_map/ppermute | solution.py:75
  250.7 71.3 %collective-permute-start.7 = (bf16[3,2,512,512]{3,2,1,0:T(8,128)(2,1)}, bf16[3,2,512,512]{3,2,1,0:T(8,128)(2,1)}, u32[]{:S(2)}, u32[]{:S(2)}) collective-permute-start(bf16[3,2,512,512]{3,2,1,0:T(8,128)(2,1)} %collective-permute-done.4.refs_4_), channel_id=1, source_target_pairs={{0,8},{1,9},{2,10},{3,11},{4,12},{5,13},{6,14},{7,15},{8,0},{9,1},... | collective-permute-start | bytes 9437192 | tf_op jit(solution)/shard_map/ppermute | solution.py:75
  314.7 73.4 %collective-permute-start.12 = (bf16[2,1024,1024]{2,1,0:T(8,128)(2,1)}, bf16[2,1024,1024]{2,1,0:T(8,128)(2,1)}, u32[]{:S(2)}, u32[]{:S(2)}) collective-permute-start(bf16[2,1024,1024]{2,1,0:T(8,128)(2,1)} %get-tuple-element.111), channel_id=1, source_target_pairs={{0,4},{1,5},{2,6},{3,7},{4,0},{5,1},{6,2},{7,3},{8,12},{9,13},{10,... | collective-permute-start | bytes 12582920 | tf_op jit(solution)/shard_map/ppermute | solution.py:75
  314.7 71.3 %collective-permute-start.11 = (bf16[3,2,512,512]{3,2,1,0:T(8,128)(2,1)}, bf16[3,2,512,512]{3,2,1,0:T(8,128)(2,1)}, u32[]{:S(2)}, u32[]{:S(2)}) collective-permute-start(bf16[3,2,512,512]{3,2,1,0:T(8,128)(2,1)} %get-tuple-element.110), channel_id=1, source_target_pairs={{0,1},{1,0},{2,3},{3,2},{4,5},{5,4},{6,7},{7,6},{8,9},{9,8},{10,11... | collective-permute-start | bytes 9437192 | tf_op jit(solution)/shard_map/ppermute | solution.py:75
  316.2 71.9 %collective-permute-start.10 = (bf16[3,2,512,512]{3,2,1,0:T(8,128)(2,1)}, bf16[3,2,512,512]{3,2,1,0:T(8,128)(2,1)}, u32[]{:S(2)}, u32[]{:S(2)}) collective-permute-start(bf16[3,2,512,512]{3,2,1,0:T(8,128)(2,1)} %collective-permute-done.9.refs_6_.refs_4_), channel_id=1, source_target_pairs={{0,8},{1,9},{2,10},{3,11},{4,12},{5,13},{6,14},{7,15},{8,0},{9,1},... | collective-permute-start | bytes 9437192 | tf_op jit(solution)/shard_map/ppermute | solution.py:75
  376.8 76.1 %collective-permute-start.14 = (bf16[2,1024,1024]{2,1,0:T(8,128)(2,1)}, bf16[2,1024,1024]{2,1,0:T(8,128)(2,1)}, u32[]{:S(2)}, u32[]{:S(2)}) collective-permute-start(bf16[2,1024,1024]{2,1,0:T(8,128)(2,1)} %get-tuple-element.114), channel_id=1, source_target_pairs={{0,4},{1,5},{2,6},{3,7},{4,0},{5,1},{6,2},{7,3},{8,12},{9,13},{10,... | collective-permute-start | bytes 12582920 | tf_op jit(solution)/shard_map/ppermute | solution.py:75
  376.8 76.1 %collective-permute-start.13 = (bf16[3,2,512,512]{3,2,1,0:T(8,128)(2,1)}, bf16[3,2,512,512]{3,2,1,0:T(8,128)(2,1)}, u32[]{:S(2)}, u32[]{:S(2)}) collective-permute-start(bf16[3,2,512,512]{3,2,1,0:T(8,128)(2,1)} %get-tuple-element.113), channel_id=1, source_target_pairs={{0,1},{1,0},{2,3},{3,2},{4,5},{5,4},{6,7},{7,6},{8,9},{9,8},{10,11... | collective-permute-start | bytes 9437192 | tf_op jit(solution)/shard_map/ppermute | solution.py:75
  443.1 70.9 %collective-permute-start.17 = (bf16[2,1024,1024]{2,1,0:T(8,128)(2,1)}, bf16[2,1024,1024]{2,1,0:T(8,128)(2,1)}, u32[]{:S(2)}, u32[]{:S(2)}) collective-permute-start(bf16[2,1024,1024]{2,1,0:T(8,128)(2,1)} %get-tuple-element.121), channel_id=1, source_target_pairs={{0,4},{1,5},{2,6},{3,7},{4,0},{5,1},{6,2},{7,3},{8,12},{9,13},{10,... | collective-permute-start | bytes 12582920 | tf_op jit(solution)/shard_map/ppermute | solution.py:75
  443.2 70.8 %collective-permute-start.15 = (bf16[3,2,512,512]{3,2,1,0:T(8,128)(2,1)}, bf16[3,2,512,512]{3,2,1,0:T(8,128)(2,1)}, u32[]{:S(2)}, u32[]{:S(2)}) collective-permute-start(bf16[3,2,512,512]{3,2,1,0:T(8,128)(2,1)} %get-tuple-element.119), channel_id=1, source_target_pairs={{0,8},{1,9},{2,10},{3,11},{4,12},{5,13},{6,14},{7,15},{8,0},{9,1},... | collective-permute-start | bytes 9437192 | tf_op jit(solution)/shard_map/ppermute | solution.py:75
  443.5 70.5 %collective-permute-start.16 = (bf16[3,2,512,512]{3,2,1,0:T(8,128)(2,1)}, bf16[3,2,512,512]{3,2,1,0:T(8,128)(2,1)}, u32[]{:S(2)}, u32[]{:S(2)}) collective-permute-start(bf16[3,2,512,512]{3,2,1,0:T(8,128)(2,1)} %get-tuple-element.120), channel_id=1, source_target_pairs={{0,16},{1,17},{2,18},{3,19},{4,20},{5,21},{6,22},{7,23},{8,24},{9,... | collective-permute-start | bytes 9437192 | tf_op jit(solution)/shard_map/ppermute | solution.py:75
  522.9 70.4 %collective-permute-start.22 = (bf16[3,2,512,512]{3,2,1,0:T(8,128)(2,1)}, bf16[3,2,512,512]{3,2,1,0:T(8,128)(2,1)}, u32[]{:S(2)}, u32[]{:S(2)}) collective-permute-start(bf16[3,2,512,512]{3,2,1,0:T(8,128)(2,1)} %add_convert_fusion), channel_id=1, source_target_pairs={{0,8},{1,9},{2,10},{3,11},{4,12},{5,13},{6,14},{7,15},{8,0},{9,1},... | collective-permute-start | bytes 9437192 | tf_op jit(solution)/shard_map/ppermute | solution.py:75
  530.8 85.7 %collective-permute-start.33 = (bf16[2,512,512]{2,1,0:T(8,128)(2,1)}, bf16[2,512,512]{2,1,0:T(8,128)(2,1)}, u32[]{:S(2)}, u32[]{:S(2)}) collective-permute-start(bf16[2,512,512]{2,1,0:T(8,128)(2,1)} %get-tuple-element.293), channel_id=1, source_target_pairs={{0,1},{1,0},{2,3},{3,2},{4,5},{5,4},{6,7},{7,6},{8,9},{9,8},{10,11... | collective-permute-start | bytes 3145736 | tf_op jit(solution)/shard_map/ppermute | solution.py:75
  622.2 133.8 %collective-permute-start.34 = (bf16[2,512,512]{2,1,0:T(8,128)(2,1)}, bf16[2,512,512]{2,1,0:T(8,128)(2,1)}, u32[]{:S(2)}, u32[]{:S(2)}) collective-permute-start(bf16[2,512,512]{2,1,0:T(8,128)(2,1)} %get-tuple-element.303), channel_id=1, source_target_pairs={{0,16},{1,17},{2,18},{3,19},{4,20},{5,21},{6,22},{7,23},{8,24},{9,... | collective-permute-start | bytes 3145736 | tf_op jit(solution)/shard_map/ppermute | solution.py:75
  747.0 74.7 %all-to-all-start.1 = ((bf16[4,128,1024]{2,1,0:T(8,128)(2,1)}), bf16[4,128,1024]{2,1,0:T(8,128)(2,1)}, u32[]{:S(2)}, u32[]{:S(2)}) async-start(bf16[4,128,1024]{2,1,0:T(8,128)(2,1)} %pad_maximum_fusion.6), calls=%async_computation.1 | async-start | bytes 2097152 | tf_op jit(solution)/shard_map/all_to_all | solution.py:855
  836.5 106.7 %collective-permute-start.42 = (f32[512,512]{1,0:T(8,128)S(1)}, f32[512,512]{1,0:T(8,128)}, u32[]{:S(2)}, u32[]{:S(2)}) collective-permute-start(f32[512,512]{1,0:T(8,128)S(1)} %get-tuple-element.171), channel_id=1, source_target_pairs={{0,1},{1,0},{2,3},{3,2},{4,5},{5,4},{6,7},{7,6},{8,9},{9,8},{10,11... | collective-permute-start | bytes 3145736 | tf_op jit(solution)/shard_map/ppermute | solution.py:75
  838.5 104.8 %collective-permute-start.43 = (f32[512,512]{1,0:T(8,128)S(1)}, f32[512,512]{1,0:T(8,128)}, u32[]{:S(2)}, u32[]{:S(2)}) collective-permute-start(f32[512,512]{1,0:T(8,128)S(1)} %get-tuple-element.173), channel_id=1, source_target_pairs={{0,1},{1,0},{2,3},{3,2},{4,5},{5,4},{6,7},{7,6},{8,9},{9,8},{10,11... | collective-permute-start | bytes 3145736 | tf_op jit(solution)/shard_map/ppermute | solution.py:75
  838.6 104.6 %collective-permute-start.44 = (f32[512,512]{1,0:T(8,128)S(1)}, f32[512,512]{1,0:T(8,128)}, u32[]{:S(2)}, u32[]{:S(2)}) collective-permute-start(f32[512,512]{1,0:T(8,128)S(1)} %get-tuple-element.175), channel_id=1, source_target_pairs={{0,1},{1,0},{2,3},{3,2},{4,5},{5,4},{6,7},{7,6},{8,9},{9,8},{10,11... | collective-permute-start | bytes 3145736 | tf_op jit(solution)/shard_map/ppermute | solution.py:75
  (113 other events, 1765.3 us)
Sparse Core Ops, SparseCore 0:
  11.4 146.1 all-gather.1

commit v4 on v3

--- a/solution.py
+++ b/solution.py
@@ -550,7 +550,7 @@
     pair[1][rows, columns] = low
 
 
-def ortho_block_kernel(halves_ref, m_ref, x_ref, xh, xl, th, tl, gram, gh, gl, sh, sl):
+def ortho_block_kernel(fresh, steps, halves_ref, m_ref, x_ref, xh, xl, th, tl, gram, gh, gl, sh, sl):
     size = m_ref.shape[0]
     tile = 256
     halves = halves_ref[0] == 1
@@ -563,18 +563,16 @@
             total = total + jnp.sum(piece * piece, axis=0, keepdims=True)
         return jnp.sum(total)
 
-    lower, upper = square_sum(slice(0, half)), square_sum(slice(half, size))
-    whole = lower + upper
-
-    def scale_of(own):
-        squares = jnp.full((1, half), jnp.where(halves, own, whole), jnp.float32)
-        return 1.0 / (jnp.sqrt(squares) + ORTHO_EPS)
-
-    for columns, own in ((slice(0, half), lower), (slice(half, size), upper)):
-        scale = scale_of(own)
-        for first in range(0, size, tile):
-            rows = slice(first, first + tile)
-            x_ref[rows, columns] = m_ref[rows, columns] * scale
+    if fresh:
+        lower, upper = square_sum(slice(0, half)), square_sum(slice(half, size))
+        for columns, own in ((slice(0, half), lower), (slice(half, size), upper)):
+            squares = jnp.full((1, half), jnp.where(halves, own, lower + upper), jnp.float32)
+            scale = 1.0 / (jnp.sqrt(squares) + ORTHO_EPS)
+            for first in range(0, size, tile):
+                rows = slice(first, first + tile)
+                x_ref[rows, columns] = m_ref[rows, columns] * scale
+    else:
+        x_ref[...] = m_ref[...]
 
     def mask(rows, columns, values):
         row = rows.start + lax.broadcasted_iota(jnp.int32, values.shape, 0)
@@ -606,14 +604,14 @@
             x_ref[rows, :] = POLY_ONE * x_ref[rows, :] + change
         return carry
 
-    lax.fori_loop(0, 5, iterate, 0)
-
-
-def ortho_block_call(block, halves):
+    lax.fori_loop(0, steps, iterate, 0)
+
+
+def ortho_block_call(fresh, steps, block, halves):
     size = block.shape[0]
     low = pltpu.VMEM((size, size), jnp.bfloat16)
     return pl.pallas_call(
-        ortho_block_kernel,
+        functools.partial(ortho_block_kernel, fresh, steps),
         in_specs=[
             pl.BlockSpec(memory_space=pltpu.SMEM),
             pl.BlockSpec(memory_space=pltpu.VMEM),
@@ -623,25 +621,26 @@
         scratch_shapes=[low] * 4 + [pltpu.VMEM((size, size), jnp.float32)] + [low] * 4,
         compiler_params=pltpu.CompilerParams(vmem_limit_bytes=56 * 1024 * 1024),
         cost_estimate=pl.CostEstimate(
-            flops=5 * 9 * 2 * size**3, bytes_accessed=8 * size * size, transcendentals=0
+            flops=steps * 9 * 2 * size**3, bytes_accessed=8 * size * size, transcendentals=0
         ),
         name="ortho_block",
     )(halves.reshape(1), block)
 
 
-def ortho_rows_kernel(m_ref, o_ref, xh, xl, th, tl, gram, pair_g, pair_p, pair_t, product, pair_q):
-    rows_all, size = m_ref.shape[1:]
-    own = o_ref.shape[1]
+def ortho_rows_kernel(m_ref, n_ref, o_ref, xh, xl, th, tl, gram, pair_g, pair_p, pair_t, product, pair_q):
+    side_rows, size = m_ref.shape
+    own = o_ref.shape[0]
     tile = 256
+    sides = [(side, first) for side in (m_ref, n_ref) for first in range(0, side_rows, tile)]
     squares = jnp.zeros((1, size), jnp.float32)
-    for first in range(0, rows_all, tile):
-        piece = m_ref[0, first : first + tile, :]
+    for side, first in sides:
+        piece = side[first : first + tile, :]
         squares = squares + jnp.sum(piece * piece, axis=0, keepdims=True)
     total = jnp.full((1, size), jnp.sum(squares), jnp.float32)
     scale = 1.0 / (jnp.sqrt(total) + ORTHO_EPS)
-    for first in range(0, rows_all, tile):
-        rows = slice(first, first + tile)
-        high, low = split_high(m_ref[0, rows, :] * scale)
+    for index, (side, first) in enumerate(sides):
+        rows = slice(index * tile, (index + 1) * tile)
+        high, low = split_high(side[first : first + tile, :] * scale)
         xh[rows, :] = high
         xl[rows, :] = low
         th[:, rows] = high.T
@@ -686,31 +685,28 @@
         return carry
 
     lax.fori_loop(0, 4, iterate, 0)
-    o_ref[0] = triple_dot((xh[:own, :], xl[:own, :]), (pair_q[0][...], pair_q[1][...]))
-
-
-def ortho_rows_call(group_rows, own_rows):
-    kinds, rows_all, size = group_rows.shape
+    o_ref[...] = triple_dot((xh[:own, :], xl[:own, :]), (pair_q[0][...], pair_q[1][...]))
+
+
+def ortho_rows_call(side_rows, other_rows, own_rows):
+    rows_all, size = 2 * side_rows.shape[0], side_rows.shape[1]
     low = jnp.bfloat16
     pair = pltpu.VMEM((2, size, size), low)
     square = pltpu.VMEM((size, size), jnp.float32)
     return pl.pallas_call(
         ortho_rows_kernel,
-        grid=(kinds,),
-        in_specs=[pl.BlockSpec((1, rows_all, size), lambda k: (k, 0, 0))],
-        out_specs=pl.BlockSpec((1, own_rows, size), lambda k: (k, 0, 0)),
-        out_shape=jax.ShapeDtypeStruct((kinds, own_rows, size), jnp.float32),
+        in_specs=[pl.BlockSpec(memory_space=pltpu.VMEM)] * 2,
+        out_specs=pl.BlockSpec(memory_space=pltpu.VMEM),
+        out_shape=jax.ShapeDtypeStruct((own_rows, size), jnp.float32),
         scratch_shapes=[pltpu.VMEM((rows_all, size), low)] * 2
         + [pltpu.VMEM((size, rows_all), low)] * 2
         + [square, pair, pair, pair, square, pair],
-        compiler_params=pltpu.CompilerParams(
-            dimension_semantics=("arbitrary",), vmem_limit_bytes=40 * 1024 * 1024
-        ),
+        compiler_params=pltpu.CompilerParams(vmem_limit_bytes=40 * 1024 * 1024),
         cost_estimate=pl.CostEstimate(
-            flops=kinds * 60 * 2 * size**3, bytes_accessed=16 * size * size, transcendentals=0
+            flops=60 * 2 * size**3, bytes_accessed=16 * size * size, transcendentals=0
         ),
         name="ortho_rows",
-    )(group_rows)
+    )(side_rows, other_rows)
 
 
 def take_half(values, axis, own):
@@ -831,9 +827,8 @@
             side ^ 1 if index == hop_of[bit] else side for index, side in enumerate(chunk)
         )
 
-    chunks = {(0, 0, 0): jnp.stack([own_half, swap_bit(own_half, count, bit_z)], axis=1)}
-    for chunk, bit in level_one:
-        chunks[chunk] = swap_bit(chunks[before_hop(chunk, bit)], count, bit)
+    own_half = after(own_half, full_packed)
+    from_z = swap_bit(own_half, count, bit_z)
     gain_one = full_gains[0].astype(jnp.float32)
     gain_two = full_gains[1].astype(jnp.float32)
     inputs = tokens.astype(jnp.float32)
@@ -867,8 +862,12 @@
         key_rows,
         value_rows,
         seq_len,
-        [chunks[0, 0, 0], old_tasks],
-    )
+        [old_tasks],
+    )
+    attended, own_half, from_z = lax.optimization_barrier((attended, own_half, from_z))
+    chunks = {(0, 0, 0): jnp.stack([own_half, from_z], axis=1)}
+    for chunk, bit in level_one:
+        chunks[chunk] = swap_bit(chunks[before_hop(chunk, bit)], count, bit)
     branch = plain_dot(attended, w_out, 1, 1)
     for chunk, bit in level_two:
         chunks[chunk] = swap_bit(after(chunks[before_hop(chunk, bit)], branch), count, bit)
@@ -1007,11 +1006,9 @@
         )
 
     first_heads = attend_back(0, [], [])
-    last_own, half_y[:2], _ = lax.optimization_barrier(
-        (grads[0, 0, 1], half_y[:2], first_heads[0])
-    )
-    grad_query, grad_key, grad_value = attend_back(1, first_heads, half_y[:2] + [moved[0, 1, 0]])
-    half_y[2], _ = lax.optimization_barrier((half_y[2], grad_query))
+    last_own, half_y[0], _ = lax.optimization_barrier((grads[0, 0, 1], half_y[0], first_heads[0]))
+    grad_query, grad_key, grad_value = attend_back(1, first_heads, [half_y[0], moved[0, 1, 0]])
+    half_y[1:], _ = lax.optimization_barrier((half_y[1:], grad_query))
     from_y = [
         swap_bit(total_of(last_own[kind], half_y[kind]), count, bit_y) for kind in range(3)
     ]
@@ -1019,7 +1016,6 @@
     block_out = (hidden_state + RESID_MULT * gather_sum([part[0] for part in late_parts])).astype(
         jnp.bfloat16
     )
-    grad_query, from_y[0] = lax.optimization_barrier((grad_query, from_y[0]))
     low_grad = [
         pin(plain_dot(normed_one, piece, 0, 0).astype(jnp.bfloat16))
         for piece in (grad_query, grad_key, grad_value)
@@ -1029,8 +1025,8 @@
         + plain_dot(grad_key, w_shared[:, :kv_width], 1, 1)
         + plain_dot(grad_value, w_shared[:, kv_width:], 1, 1)
     )
-    nearest, from_y[:2], grad_normed_one, low_grad[1:] = lax.optimization_barrier(
-        (grads[0, 0, 0], from_y[:2], grad_normed_one, low_grad[1:])
+    nearest, from_y[0], grad_normed_one, low_grad[1:] = lax.optimization_barrier(
+        (grads[0, 0, 0], from_y[0], grad_normed_one, low_grad[1:])
     )
     scale_one = lax.rsqrt(jnp.mean(inputs * inputs, axis=-1, keepdims=True) + NORM_EPS)
     unit_one = inputs * scale_one
@@ -1075,15 +1071,18 @@
     attn_block = jnp.concatenate(
         [gather_from_owners(side, count, place, [pair_bit], wide_x) for side in sides], axis=1
     )
-    from_y[2] = after(from_y[2], wide_sum)
+    from_y[1] = after(from_y[1], wide_sum)
+    from_y[2] = after(from_y[2], task_block)
     expert_sums = [
         total_of(nearest[kind], moved[1, 0, 0][kind], moved[0, 1, 0][kind], from_y[kind])
         for kind in range(3)
     ]
+    z_hops = [swap_bit(expert_sums[kind][1], count, bit_z) for kind in range(3)]
+    halves = (lax.axis_index("blk") == 1).astype(jnp.int32)
+    half_way = ortho_block_call(True, 3, attn_block, halves)
     moment_expert, group_rows = [], []
     for kind in range(3):
-        total = after(expert_sums[kind], wide_sum, shared_sum)
-        from_z = after(swap_bit(expert_sums[kind][1], count, bit_z), wide_sum, shared_sum)
+        total, from_z = after((expert_sums[kind], z_hops[kind]), half_way)
         total = total[0].astype(jnp.float32) + from_z.astype(jnp.float32)
         total = total.T if kind == 2 else total
         if early_bits:
@@ -1094,11 +1093,12 @@
             rows = jnp.concatenate([rows, swap_bit(rows, count, bit)])
         moment_expert.append(moment)
         group_rows.append((rows, swap_bit(rows, count, low_bits[-1])))
-    attn_block = after(attn_block, *moment_expert)
-    attn_iter = ortho_block_call(attn_block, (lax.axis_index("blk") == 1).astype(jnp.int32))
-    group_rows = after(tuple(group_rows), attn_iter)
-    group_rows = jnp.stack([jnp.concatenate(pieces) for pieces in group_rows])
-    ortho_expert = ortho_rows_call(group_rows, own_rows)
+    attn_iter = ortho_block_call(False, 2, after(half_way, *moment_expert), halves)
+    ortho_expert = [attn_iter]
+    for pieces in group_rows:
+        rows, other_rows = after(pieces, ortho_expert[-1])
+        ortho_expert.append(ortho_rows_call(rows, other_rows, own_rows))
+    ortho_expert = jnp.stack(ortho_expert[1:])
     returned = lax.dynamic_slice_in_dim(
         attn_iter, lax.axis_index("dp") * (n_blk * rows_each), n_blk * rows_each, 0
     )

time: 1030 us -> 1020 us (level)
    ppermute x45, waiting for transfers between devices: 225 us -> 196 us  [swap_bit(): return pin(lax.ppermute(pin(values), AXES, pairs))]
    all_gather x1, waiting for transfers between devices: 36.2 us -> 58.1 us  [shards(): lax.all_gather(jnp.concatenate([attn_low, small_low], axis=1), AXES, axis...]
    pallas_call x2 -> x5, Pallas kernels: 131 us -> 139 us  [the longest x2 84.8 us: ortho_block_call(): pl.pallas_call(functools.partial(ortho_block_kernel, fresh, steps), in_sp...]
    unnamed x184 -> x156, local copies, waits for them, and re-layouts: 34.4 us -> 39.3 us
  transfers between devices with their start and end apart: 50 -> 50, of which waited for: 21 -> 23; matrix products, arithmetic and copies ran while one was open for 20% -> 20% of each run, Pallas kernels for 43% -> 42%
where the time goes in v4:
time: 1020 us; the launch traced here: 1010 us
  Pallas kernels  446 us (44%)
  waiting for transfers between devices  259 us (25%)
  other arithmetic  124 us (12%)
  local copies, waits for them, and re-layouts  87.7 us (9%)
  starting transfers between devices  53.7 us (5%)
  matrix products  28.4 us (3%)
  between operations  16.2 us (2%)
    pallas_call x4, Pallas kernels, expert_call(): pl.pallas_call(functools.partial(expert_kernel, len(done), first), grid=(...  220 us
    ppermute x45, waiting for transfers between devices, swap_bit(): return pin(lax.ppermute(pin(values), AXES, pairs))  196 us
    pallas_call x2, Pallas kernels, ortho_block_call(): pl.pallas_call(functools.partial(ortho_block_kernel, fresh, steps), in_sp...  84.8 us
    all_gather x1, waiting for transfers between devices, shards(): lax.all_gather(jnp.concatenate([attn_low, small_low], axis=1), AXES, axis...  58.1 us
    pallas_call x3, Pallas kernels, ortho_rows_call(): pl.pallas_call(ortho_rows_kernel, in_specs=[pl.BlockSpec(memory_space=plt...  54.4 us
    pallas_call x2, Pallas kernels, attend_back_call(): pl.pallas_call(attend_back_kernel, grid=(seqs, groups), in_specs=[pl.Bloc...  45.8 us
    unnamed x156, local copies, waits for them, and re-layouts  39.3 us
    ppermute x45, starting transfers between devices, swap_bit(): return pin(lax.ppermute(pin(values), AXES, pairs))  33.5 us
  transfers between devices with their start and end apart: 50, of which 23 were waited for; matrix products, arithmetic and copies ran while one was open for 20% of the time, Pallas kernels for 42%

profile of v4, /device:TPU:0, one launch (start us, length us, event | category | flops | bytes accessed | tf_op | source)
XLA Modules:
  0.0 1014.9 jit_solution(2349048270636198826)
XLA Ops:
  31.2 58.1 %all-gather.2.cloned.1.call-done.wq_ref.wkv_ref = bf16[1024,3200]{1,0:T(8,128)(2,1)} async-done(((bf16[32,3200]{1,0:T(8,128)(2,1)}), bf16[1024,3200]{1,0:T(8,128)(2,1)}) %all-gather.2.cloned.1.call-update) | async-done | bytes 6553616 | tf_op jit(solution)/shard_map/all_gather | solution.py:811
  112.5 33.4 %attend.1 = (bf16[1024,1024]{1,0:T(8,128)(2,1)S(1)}, f32[4,8,1024]{2,1,0:T(8,128)S(1)}) custom-call(s32[1,1]{1,0:T(1,128)} %bitcast.219.len_ref, bf16[1024,1024]{1,0:T(8,128)(2,1)S(1)} %copy-done.9, bf16[1024,512]{1,0:T(8,128)(2,1)S(1)} %copy-done.12, bf16[1024,512]{1,0:T(8,128)(2,1)S(1)} %copy-done.15, f32[128,1024]{1,0:T(8,128)S(1)} %bitcast.223), custom_call_target="tpu_custom_call" | custom-call | flops 20000000000 | bytes 8000000 | tf_op jit(solution)/shard_map/attend/pallas_call | solution.py:234
  145.9 18.0 %collective-permute-done = bf16[3,512,512]{2,1,0:T(8,128)(2,1)} collective-permute-done((bf16[3,512,512]{2,1,0:T(8,128)(2,1)}, bf16[3,512,512]{2,1,0:T(8,128)(2,1)}, u32[]{:S(2)}, u32[]{:S(2)}) %collective-permute-start) | collective-permute-done | bytes 1572896 | tf_op jit(solution)/shard_map/ppermute | solution.py:75
  204.4 32.6 %collective-permute-done.6.refs_6_.refs_3_ = bf16[3,2,512,512]{3,2,1,0:T(8,128)(2,1)} collective-permute-done((bf16[3,2,512,512]{3,2,1,0:T(8,128)(2,1)}, bf16[3,2,512,512]{3,2,1,0:T(8,128)(2,1)}, u32[]{:S(2)}, u32[]{:S(2)}) %collective-permute-start.6) | collective-permute-done | bytes 3145760 | tf_op jit(solution)/shard_map/ppermute | solution.py:75
  240.2 55.0 %experts.4 = (bf16[2,1024,1024]{2,1,0:T(8,128)(2,1)}, bf16[2,1024,1024]{2,1,0:T(8,128)(2,1)}, f32[2048,128]{1,0:T(8,128)}, bf16[3,2,512,512]{3,2,1,0:T(8,128)(2,1)}, bf16[3,2,512,512]{3,2,1,0:T(8,128)(2,1)}) custom-call(bf16[2048,1024]{1,0:T(8,128)(2,1)} %pad_maximum_fusion.refs_0_, bf16[2048,1024]{1,0:T(8,128)(2,1)} %copy-done.49, ...), custom_call_target="tpu_custom_call" | custom-call | flops 57982058496 | bytes 50331648 | tf_op jit(solution)/shard_map/experts/pallas_call | solution.py:474
  296.2 12.3 %collective-permute-done.9.refs_6_.refs_4_ = bf16[3,2,512,512]{3,2,1,0:T(8,128)(2,1)} collective-permute-done((bf16[3,2,512,512]{3,2,1,0:T(8,128)(2,1)}, bf16[3,2,512,512]{3,2,1,0:T(8,128)(2,1)}, u32[]{:S(2)}, u32[]{:S(2)}) %collective-permute-start.9) | collective-permute-done | bytes 3145760 | tf_op jit(solution)/shard_map/ppermute | solution.py:75
  309.7 55.0 %experts.5 = (bf16[2,1024,1024]{2,1,0:T(8,128)(2,1)}, bf16[2,1024,1024]{2,1,0:T(8,128)(2,1)}, f32[2048,128]{1,0:T(8,128)}, bf16[3,2,512,512]{3,2,1,0:T(8,128)(2,1)}, bf16[3,2,512,512]{3,2,1,0:T(8,128)(2,1)}) custom-call(bf16[2048,1024]{1,0:T(8,128)(2,1)} %pad_maximum_fusion.refs_0_, bf16[2048,1024]{1,0:T(8,128)(2,1)} %copy-done.49, ...), custom_call_target="tpu_custom_call" | custom-call | flops 57982058496 | bytes 50331648 | tf_op jit(solution)/shard_map/experts/pallas_call | solution.py:474
  365.6 10.2 %collective-permute-done.11.refs_5_ = bf16[3,2,512,512]{3,2,1,0:T(8,128)(2,1)} collective-permute-done((bf16[3,2,512,512]{3,2,1,0:T(8,128)(2,1)}, bf16[3,2,512,512]{3,2,1,0:T(8,128)(2,1)}, u32[]{:S(2)}, u32[]{:S(2)}) %collective-permute-start.11) | collective-permute-done | bytes 3145760 | tf_op jit(solution)/shard_map/ppermute | solution.py:75
  375.9 54.8 %experts.6 = (bf16[2,1024,1024]{2,1,0:T(8,128)(2,1)}, bf16[2,1024,1024]{2,1,0:T(8,128)(2,1)}, f32[2048,128]{1,0:T(8,128)}, bf16[3,2,512,512]{3,2,1,0:T(8,128)(2,1)}, bf16[3,2,512,512]{3,2,1,0:T(8,128)(2,1)}) custom-call(bf16[2048,1024]{1,0:T(8,128)(2,1)} %pad_maximum_fusion.refs_0_, bf16[2048,1024]{1,0:T(8,128)(2,1)} %copy-done.49, ...), custom_call_target="tpu_custom_call" | custom-call | flops 57982058496 | bytes 50331648 | tf_op jit(solution)/shard_map/experts/pallas_call | solution.py:474
  432.7 8.1 collective-permute-done.13.refs_5_
  440.8 55.2 %experts.7 = (bf16[2,1024,1024]{2,1,0:T(8,128)(2,1)}, bf16[2,1024,1024]{2,1,0:T(8,128)(2,1)}, f32[2048,128]{1,0:T(8,128)}, bf16[3,2,512,512]{3,2,1,0:T(8,128)(2,1)}, bf16[3,2,512,512]{3,2,1,0:T(8,128)(2,1)}) custom-call(bf16[2048,1024]{1,0:T(8,128)(2,1)} %pad_maximum_fusion.refs_0_, bf16[2048,1024]{1,0:T(8,128)(2,1)} %copy-done.49, ...), custom_call_target="tpu_custom_call" | custom-call | flops 57982058496 | bytes 50331648 | tf_op jit(solution)/shard_map/experts/pallas_call | solution.py:474
  541.3 22.7 %attend_back.2 = (bf16[1024,1024]{1,0:T(8,128)(2,1)S(1)}, bf16[1024,512]{1,0:T(8,128)(2,1)S(1)}, bf16[1024,512]{1,0:T(8,128)(2,1)S(1)}) custom-call(s32[1,1]{1,0:T(1,128)} %bitcast.220.len_ref, bf16[1024,1024]{1,0:T(8,128)(2,1)S(1)} %copy-done.10, bf16[1024,512]{1,0:T(8,128)(2,1)S(1)} %copy-done.13, bf16[1024,512]{1,0:T(8,128)(2,1)S(1)} %copy-done.16, ...), custom_call_target="tpu_custom_call" | custom-call | flops 24000000000 | bytes 8000000 | tf_op jit(solution)/shard_map/attend_back/pallas_call | solution.py:333
  567.3 14.7 %collective-permute-done.21.refs_4_ = bf16[3,2,512,512]{3,2,1,0:T(8,128)(2,1)} collective-permute-done((bf16[3,2,512,512]{3,2,1,0:T(8,128)(2,1)}, bf16[3,2,512,512]{3,2,1,0:T(8,128)(2,1)}, u32[]{:S(2)}, u32[]{:S(2)}) %collective-permute-start.21) | collective-permute-done | bytes 3145760 | tf_op jit(solution)/shard_map/ppermute | solution.py:75
  582.0 23.1 %attend_back.3 = (bf16[1024,1024]{1,0:T(8,128)(2,1)S(1)}, bf16[1024,512]{1,0:T(8,128)(2,1)S(1)}, bf16[1024,512]{1,0:T(8,128)(2,1)S(1)}) custom-call(s32[1,1]{1,0:T(1,128)} %bitcast.221.len_ref, bf16[1024,1024]{1,0:T(8,128)(2,1)S(1)} %copy-done.10, bf16[1024,512]{1,0:T(8,128)(2,1)S(1)} %copy-done.13, ...), custom_call_target="tpu_custom_call", output_to_operand_aliasing={{0}: (8, {}), {1}: (9, {}), {2}: (10, {})} | custom-call | flops 24000000000 | bytes 8000000 | tf_op jit(solution)/shard_map/attend_back/pallas_call | solution.py:333
  625.0 16.0 %collective-permute-done.22 = bf16[2,512,512]{2,1,0:T(8,128)(2,1)} collective-permute-done((bf16[2,512,512]{2,1,0:T(8,128)(2,1)S(1)}, bf16[2,512,512]{2,1,0:T(8,128)(2,1)}, u32[]{:S(2)}, u32[]{:S(2)}) %collective-permute-start.22) | collective-permute-done | bytes 1048608 | tf_op jit(solution)/shard_map/ppermute | solution.py:75
  669.5 14.2 %collective-permute-done.24 = bf16[2,128,2048]{2,1,0:T(8,128)(2,1)} collective-permute-done((bf16[2,128,2048]{2,1,0:T(8,128)(2,1)}, bf16[2,128,2048]{2,1,0:T(8,128)(2,1)}, u32[]{:S(2)}, u32[]{:S(2)}) %collective-permute-start.24) | collective-permute-done | bytes 1048608 | tf_op jit(solution)/shard_map/ppermute | solution.py:75
  689.3 34.1 %collective-permute-done.25 = bf16[1,128,2048]{2,1,0:T(8,128)(2,1)S(1)} collective-permute-done((bf16[1,128,2048]{2,1,0:T(8,128)(2,1)S(1)}, bf16[1,128,2048]{2,1,0:T(8,128)(2,1)S(1)}, u32[]{:S(2)}, u32[]{:S(2)}) %collective-permute-start.25) | collective-permute-done | bytes 524320 | tf_op jit(solution)/shard_map/ppermute | solution.py:75
  729.3 9.1 add_bitcast_fusion
  807.7 49.9 %ortho_block.2.m_ref = f32[1024,1024]{1,0:T(8,128)} custom-call(s32[1]{0:T(128)} %bitcast.60.halves_ref, f32[1024,1024]{1,0:T(8,128)} %pad_maximum_fusion.2.m_ref), custom_call_target="tpu_custom_call" | custom-call | flops 57982058496 | bytes 8388608 | tf_op jit(solution)/shard_map/ortho_block/pallas_call | solution.py:613
  863.2 34.9 %ortho_block.3 = f32[1024,1024]{1,0:T(8,128)} custom-call(s32[1]{0:T(128)} %bitcast.60.halves_ref, f32[1024,1024]{1,0:T(8,128)} %ortho_block.2.m_ref), custom_call_target="tpu_custom_call" | custom-call | flops 38654705664 | bytes 8388608 | tf_op jit(solution)/shard_map/ortho_block/pallas_call | solution.py:613
  929.5 11.2 %collective-permute-done.42.n_ref = f32[512,512]{1,0:T(8,128)} collective-permute-done((f32[512,512]{1,0:T(8,128)S(1)}, f32[512,512]{1,0:T(8,128)}, u32[]{:S(2)}, u32[]{:S(2)}) %collective-permute-start.42) | collective-permute-done | bytes 1048608 | tf_op jit(solution)/shard_map/ppermute | solution.py:75
  940.7 18.1 %ortho_rows.3 = f32[512,512]{1,0:T(8,128)S(1)} custom-call(f32[512,512]{1,0:T(8,128)S(1)} %get-tuple-element.175.m_ref, f32[512,512]{1,0:T(8,128)} %collective-permute-done.42.n_ref), custom_call_target="tpu_custom_call" | custom-call | flops 16106127360 | bytes 4194304 | tf_op jit(solution)/shard_map/ortho_rows/pallas_call | solution.py:696
  963.1 18.3 %ortho_rows.4 = f32[512,512]{1,0:T(8,128)S(1)} custom-call(f32[512,512]{1,0:T(8,128)S(1)} %get-tuple-element.177.m_ref, f32[512,512]{1,0:T(8,128)} %collective-permute-done.43.n_ref), custom_call_target="tpu_custom_call" | custom-call | flops 16106127360 | bytes 4194304 | tf_op jit(solution)/shard_map/ortho_rows/pallas_call | solution.py:696
  984.3 18.0 %ortho_rows.5 = f32[512,512]{1,0:T(8,128)S(1)} custom-call(f32[512,512]{1,0:T(8,128)S(1)} %get-tuple-element.179.m_ref, f32[512,512]{1,0:T(8,128)} %collective-permute-done.44.n_ref), custom_call_target="tpu_custom_call" | custom-call | flops 16106127360 | bytes 4194304 | tf_op jit(solution)/shard_map/ortho_rows/pallas_call | solution.py:696
  (383 shorter events, 322.0 us)
Async XLA Ops:
  7.2 82.1 %all-gather.2.cloned.1.call-start = ((), (), s32[]{:S(2)}) async-start(), calls=%async_computation.4 | async-start | bytes 6758400 | tf_op jit(solution)/shard_map/all_gather | solution.py:811
  13.3 95.2 %all-to-all-start = ((f32[4,32,1024]{2,1,0:T(8,128)}), f32[4,32,1024]{2,1,0:T(8,128)S(1)}, u32[]{:S(2)}, u32[]{:S(2)}) async-start(f32[4,32,1024]{2,1,0:T(8,128)} %pad_maximum_fusion.8), calls=%async_computation | async-start | bytes 1048576 | tf_op jit(solution)/shard_map/all_to_all | solution.py:850
  92.4 71.5 %collective-permute-start = (bf16[3,512,512]{2,1,0:T(8,128)(2,1)}, bf16[3,512,512]{2,1,0:T(8,128)(2,1)}, u32[]{:S(2)}, u32[]{:S(2)}) collective-permute-start(bf16[3,512,512]{2,1,0:T(8,128)(2,1)} %convert_element_type.467), channel_id=1, source_target_pairs={{0,2},{1,3},{2,0},{3,1},{4,6},{5,7},{6,4},{7,5},{8,10},{9,11},{10,... | collective-permute-start | bytes 4718600 | tf_op jit(solution)/shard_map/ppermute | solution.py:75
  107.7 85.8 %collective-permute-start.2 = (bf16[1024,1024]{1,0:T(8,128)(2,1)}, bf16[1024,1024]{1,0:T(8,128)(2,1)}, u32[]{:S(2)}, u32[]{:S(2)}) collective-permute-start(bf16[1024,1024]{1,0:T(8,128)(2,1)} %maximum_select_fusion.3), channel_id=1, source_target_pairs={{0,4},{1,5},{2,6},{3,7},{4,0},{5,1},{6,2},{7,3},{8,12},{9,13},{10,... | collective-permute-start | bytes 6291464 | tf_op jit(solution)/shard_map/ppermute | solution.py:75
  167.3 69.8 %collective-permute-start.6 = (bf16[3,2,512,512]{3,2,1,0:T(8,128)(2,1)}, bf16[3,2,512,512]{3,2,1,0:T(8,128)(2,1)}, u32[]{:S(2)}, u32[]{:S(2)}) collective-permute-start(bf16[3,2,512,512]{3,2,1,0:T(8,128)(2,1)} %pad_maximum_fusion.3.refs_3_), channel_id=1, source_target_pairs={{0,16},{1,17},{2,18},{3,19},{4,20},{5,21},{6,22},{7,23},{8,24},{9,... | collective-permute-start | bytes 9437192 | tf_op jit(solution)/shard_map/ppermute | solution.py:75
  237.1 71.4 %collective-permute-start.9 = (bf16[3,2,512,512]{3,2,1,0:T(8,128)(2,1)}, bf16[3,2,512,512]{3,2,1,0:T(8,128)(2,1)}, u32[]{:S(2)}, u32[]{:S(2)}) collective-permute-start(bf16[3,2,512,512]{3,2,1,0:T(8,128)(2,1)} %collective-permute-done.6.refs_6_.refs_3_), channel_id=1, source_target_pairs={{0,1},{1,0},{2,3},{3,2},{4,5},{5,4},{6,7},{7,6},{8,9},{9,8},{10,11... | collective-permute-start | bytes 9437192 | tf_op jit(solution)/shard_map/ppermute | solution.py:75
  238.3 71.4 %collective-permute-start.8 = (bf16[3,2,512,512]{3,2,1,0:T(8,128)(2,1)}, bf16[3,2,512,512]{3,2,1,0:T(8,128)(2,1)}, u32[]{:S(2)}, u32[]{:S(2)}) collective-permute-start(bf16[3,2,512,512]{3,2,1,0:T(8,128)(2,1)} %collective-permute-done.5.refs_5_.refs_3_), channel_id=1, source_target_pairs={{0,16},{1,17},{2,18},{3,19},{4,20},{5,21},{6,22},{7,23},{8,24},{9,... | collective-permute-start | bytes 9437192 | tf_op jit(solution)/shard_map/ppermute | solution.py:75
  238.8 70.9 %collective-permute-start.7 = (bf16[3,2,512,512]{3,2,1,0:T(8,128)(2,1)}, bf16[3,2,512,512]{3,2,1,0:T(8,128)(2,1)}, u32[]{:S(2)}, u32[]{:S(2)}) collective-permute-start(bf16[3,2,512,512]{3,2,1,0:T(8,128)(2,1)} %collective-permute-done.4.refs_4_), channel_id=1, source_target_pairs={{0,8},{1,9},{2,10},{3,11},{4,12},{5,13},{6,14},{7,15},{8,0},{9,1},... | collective-permute-start | bytes 9437192 | tf_op jit(solution)/shard_map/ppermute | solution.py:75
  295.2 80.7 %collective-permute-start.12 = (bf16[2,1024,1024]{2,1,0:T(8,128)(2,1)}, bf16[2,1024,1024]{2,1,0:T(8,128)(2,1)}, u32[]{:S(2)}, u32[]{:S(2)}) collective-permute-start(bf16[2,1024,1024]{2,1,0:T(8,128)(2,1)} %get-tuple-element.117), channel_id=1, source_target_pairs={{0,4},{1,5},{2,6},{3,7},{4,0},{5,1},{6,2},{7,3},{8,12},{9,13},{10,... | collective-permute-start | bytes 12582920 | tf_op jit(solution)/shard_map/ppermute | solution.py:75
  295.2 80.7 %collective-permute-start.11 = (bf16[3,2,512,512]{3,2,1,0:T(8,128)(2,1)}, bf16[3,2,512,512]{3,2,1,0:T(8,128)(2,1)}, u32[]{:S(2)}, u32[]{:S(2)}) collective-permute-start(bf16[3,2,512,512]{3,2,1,0:T(8,128)(2,1)} %get-tuple-element.116), channel_id=1, source_target_pairs={{0,1},{1,0},{2,3},{3,2},{4,5},{5,4},{6,7},{7,6},{8,9},{9,8},{10,11... | collective-permute-start | bytes 9437192 | tf_op jit(solution)/shard_map/ppermute | solution.py:75
  364.7 76.1 %collective-permute-start.14 = (bf16[2,1024,1024]{2,1,0:T(8,128)(2,1)}, bf16[2,1024,1024]{2,1,0:T(8,128)(2,1)}, u32[]{:S(2)}, u32[]{:S(2)}) collective-permute-start(bf16[2,1024,1024]{2,1,0:T(8,128)(2,1)} %get-tuple-element.120), channel_id=1, source_target_pairs={{0,4},{1,5},{2,6},{3,7},{4,0},{5,1},{6,2},{7,3},{8,12},{9,13},{10,... | collective-permute-start | bytes 12582920 | tf_op jit(solution)/shard_map/ppermute | solution.py:75
  364.7 76.1 %collective-permute-start.13 = (bf16[3,2,512,512]{3,2,1,0:T(8,128)(2,1)}, bf16[3,2,512,512]{3,2,1,0:T(8,128)(2,1)}, u32[]{:S(2)}, u32[]{:S(2)}) collective-permute-start(bf16[3,2,512,512]{3,2,1,0:T(8,128)(2,1)} %get-tuple-element.119), channel_id=1, source_target_pairs={{0,1},{1,0},{2,3},{3,2},{4,5},{5,4},{6,7},{7,6},{8,9},{9,8},{10,11... | collective-permute-start | bytes 9437192 | tf_op jit(solution)/shard_map/ppermute | solution.py:75
  430.6 71.8 %collective-permute-start.17 = (bf16[2,1024,1024]{2,1,0:T(8,128)(2,1)}, bf16[2,1024,1024]{2,1,0:T(8,128)(2,1)}, u32[]{:S(2)}, u32[]{:S(2)}) collective-permute-start(bf16[2,1024,1024]{2,1,0:T(8,128)(2,1)} %get-tuple-element.127), channel_id=1, source_target_pairs={{0,4},{1,5},{2,6},{3,7},{4,0},{5,1},{6,2},{7,3},{8,12},{9,13},{10,... | collective-permute-start | bytes 12582920 | tf_op jit(solution)/shard_map/ppermute | solution.py:75
  430.6 70.8 %collective-permute-start.15 = (bf16[3,2,512,512]{3,2,1,0:T(8,128)(2,1)}, bf16[3,2,512,512]{3,2,1,0:T(8,128)(2,1)}, u32[]{:S(2)}, u32[]{:S(2)}) collective-permute-start(bf16[3,2,512,512]{3,2,1,0:T(8,128)(2,1)} %get-tuple-element.125), channel_id=1, source_target_pairs={{0,8},{1,9},{2,10},{3,11},{4,12},{5,13},{6,14},{7,15},{8,0},{9,1},... | collective-permute-start | bytes 9437192 | tf_op jit(solution)/shard_map/ppermute | solution.py:75
  432.0 70.5 %collective-permute-start.16 = (bf16[3,2,512,512]{3,2,1,0:T(8,128)(2,1)}, bf16[3,2,512,512]{3,2,1,0:T(8,128)(2,1)}, u32[]{:S(2)}, u32[]{:S(2)}) collective-permute-start(bf16[3,2,512,512]{3,2,1,0:T(8,128)(2,1)} %get-tuple-element.126), channel_id=1, source_target_pairs={{0,16},{1,17},{2,18},{3,19},{4,20},{5,21},{6,22},{7,23},{8,24},{9,... | collective-permute-start | bytes 9437192 | tf_op jit(solution)/shard_map/ppermute | solution.py:75
  511.6 70.4 %collective-permute-start.21 = (bf16[3,2,512,512]{3,2,1,0:T(8,128)(2,1)}, bf16[3,2,512,512]{3,2,1,0:T(8,128)(2,1)}, u32[]{:S(2)}, u32[]{:S(2)}) collective-permute-start(bf16[3,2,512,512]{3,2,1,0:T(8,128)(2,1)} %add_convert_fusion), channel_id=1, source_target_pairs={{0,8},{1,9},{2,10},{3,11},{4,12},{5,13},{6,14},{7,15},{8,0},{9,1},... | collective-permute-start | bytes 9437192 | tf_op jit(solution)/shard_map/ppermute | solution.py:75
  516.9 92.6 %collective-permute-start.36 = (bf16[2,512,512]{2,1,0:T(8,128)(2,1)}, bf16[2,512,512]{2,1,0:T(8,128)(2,1)}, u32[]{:S(2)}, u32[]{:S(2)}) collective-permute-start(bf16[2,512,512]{2,1,0:T(8,128)(2,1)} %get-tuple-element.298), channel_id=1, source_target_pairs={{0,1},{1,0},{2,3},{3,2},{4,5},{5,4},{6,7},{7,6},{8,9},{9,8},{10,11... | collective-permute-start | bytes 3145736 | tf_op jit(solution)/shard_map/ppermute | solution.py:75
  518.6 91.0 %collective-permute-start.37 = (bf16[2,512,512]{2,1,0:T(8,128)(2,1)S(1)}, bf16[2,512,512]{2,1,0:T(8,128)(2,1)}, u32[]{:S(2)}, u32[]{:S(2)}) collective-permute-start(bf16[2,512,512]{2,1,0:T(8,128)(2,1)S(1)} %get-tuple-element.297), channel_id=1, source_target_pairs={{0,1},{1,0},{2,3},{3,2},{4,5},{5,4},{6,7},{7,6},{8,9},{9,8},{10,11... | collective-permute-start | bytes 3145736 | tf_op jit(solution)/shard_map/ppermute | solution.py:75
  664.7 103.8 %collective-permute-start.38 = (bf16[2,512,512]{2,1,0:T(8,128)(2,1)}, bf16[2,512,512]{2,1,0:T(8,128)(2,1)}, u32[]{:S(2)}, u32[]{:S(2)}) collective-permute-start(bf16[2,512,512]{2,1,0:T(8,128)(2,1)} %get-tuple-element.307), channel_id=1, source_target_pairs={{0,16},{1,17},{2,18},{3,19},{4,20},{5,21},{6,22},{7,23},{8,24},{9,... | collective-permute-start | bytes 3145736 | tf_op jit(solution)/shard_map/ppermute | solution.py:75
  665.6 119.1 %collective-permute-start.40 = (bf16[2,512,512]{2,1,0:T(8,128)(2,1)}, bf16[2,512,512]{2,1,0:T(8,128)(2,1)}, u32[]{:S(2)}, u32[]{:S(2)}) collective-permute-start(bf16[2,512,512]{2,1,0:T(8,128)(2,1)} %get-tuple-element.308), channel_id=1, source_target_pairs={{0,16},{1,17},{2,18},{3,19},{4,20},{5,21},{6,22},{7,23},{8,24},{9,... | collective-permute-start | bytes 3145736 | tf_op jit(solution)/shard_map/ppermute | solution.py:75
  777.8 79.8 %collective-permute-start.39 = (bf16[512,512]{1,0:T(8,128)(2,1)}, bf16[512,512]{1,0:T(8,128)(2,1)}, u32[]{:S(2)}, u32[]{:S(2)}) collective-permute-start(bf16[512,512]{1,0:T(8,128)(2,1)} %slice_bitcast_fusion.1), channel_id=1, source_target_pairs={{0,2},{1,3},{2,0},{3,1},{4,6},{5,7},{6,4},{7,5},{8,10},{9,11},{10,... | collective-permute-start | bytes 1572872 | tf_op jit(solution)/shard_map/ppermute | solution.py:75
  784.6 75.0 %collective-permute-start.29 = (bf16[512,512]{1,0:T(8,128)(2,1)}, bf16[512,512]{1,0:T(8,128)(2,1)}, u32[]{:S(2)}, u32[]{:S(2)}) collective-permute-start(bf16[512,512]{1,0:T(8,128)(2,1)} %slice_bitcast_fusion.2), channel_id=1, source_target_pairs={{0,2},{1,3},{2,0},{3,1},{4,6},{5,7},{6,4},{7,5},{8,10},{9,11},{10,... | collective-permute-start | bytes 1572872 | tf_op jit(solution)/shard_map/ppermute | solution.py:75
  797.3 102.7 %all-to-all-start.2 = ((f32[4,32,1024]{2,1,0:T(8,128)}), f32[4,32,1024]{2,1,0:T(8,128)}, u32[]{:S(2)}, u32[]{:S(2)}) async-start(f32[4,32,1024]{2,1,0:T(8,128)} %multiply_add_fusion.2), calls=%async_computation.2 | async-start | bytes 1048576 | tf_op jit(solution)/shard_map/all_to_all | solution.py:850
  914.7 69.6 %collective-permute-start.44 = (f32[512,512]{1,0:T(8,128)S(1)}, f32[512,512]{1,0:T(8,128)}, u32[]{:S(2)}, u32[]{:S(2)}) collective-permute-start(f32[512,512]{1,0:T(8,128)S(1)} %get-tuple-element.179.m_ref), channel_id=1, source_target_pairs={{0,1},{1,0},{2,3},{3,2},{4,5},{5,4},{6,7},{7,6},{8,9},{9,8},{10,11... | collective-permute-start | bytes 3145736 | tf_op jit(solution)/shard_map/ppermute | solution.py:75
  (99 other events, 1451.0 us)
Sparse Core Ops, SparseCore 0:
  11.4 77.8 all-gather.1
